TPU v7x, 256 devices: a whole 4x4x8 slice. The times are simulated.
256 devices in a mesh: dp: 32 (over y, x, z_lo), seq: 8 (over z_hi, core).
Axes of the slice: x: 4, y: 4, z: 8 (z_hi: 4, z_lo: 2; z = z_hi * 2 + z_lo), core: 2. Of those that a mesh axis runs over, the one named last changes fastest.
Arguments:
- queries: bfloat16 [32, 1024, 1536], P('dp', 'seq'), may hold values from -6 to 6
- key_states: bfloat16 [32, 1024, 1536], P('dp', 'seq'), may hold values from -6 to 6
- value_states: bfloat16 [32, 1024, 1536], P('dp', 'seq'), may hold values from -6 to 6
- segment_ids: int32 [32, 1024], P('dp'), may hold values from 0 to 2, never falling along the last dimension, each value on 1 to 512 neighbouring positions
- inner_first: bfloat16 [24, 64, 256], replicated, may hold values from -0.75 to 0.75
- inner_second: bfloat16 [24, 64, 256], replicated, may hold values from -0.375 to 0.375
- inner_rate: float32 [24], replicated, may hold values from 0.02 to 0.3
- branch_gate: float32 [1536], replicated, may hold values from -1.5 to 1.5
- out_weight: bfloat16 [1536, 3072], P('dp'), may hold values from -0.15625 to 0.15625
Outputs:
- layer_out: bfloat16 [32, 1024, 3072], P('dp', 'seq')
Inputs may be any that keep to these rules, and one draw needn't show every extreme that they name: `segment_ids`: segment numbers never fall along a clip; each segment holds 1 to 512 tokens and one holds exactly 512.
All inputs are finite; a program needn't handle non-finite values.
Results may differ from a plain program's by a relative error of at most 0.006.
Values may be sent and summed in bfloat16 or wider, within the bound.
No kernel may reach another device: no remote copies, remote signals or barrier semaphores. Data moves between devices by JAX's collectives and lax.ppermute only.
A program may use at most 64 MiB of HBM per device.

v0:
```python
import math

import jax
import jax.numpy as jnp
from jax import lax
from jax.sharding import PartitionSpec as P

HD = 64
FFI = 256
CH = 64


def dense(form, left, right):
    return jnp.einsum(form, left, right, precision=lax.Precision.HIGHEST)


def inner_norm(matrix):
    center = matrix - jnp.mean(matrix, axis=-1, keepdims=True)
    spread = jnp.mean(center * center, axis=-1, keepdims=True)
    return center / jnp.sqrt(spread + 1e-06)


def rms_scale(matrix):
    return matrix / jnp.sqrt(jnp.mean(matrix * matrix, axis=-1, keepdims=True) + 1e-06)


def pack(weight_in, weight_out, bias_in, bias_out):
    width = weight_in.shape[1]
    hidden = weight_in.shape[2]
    padded = jnp.pad(bias_out, ((0, 0), (0, hidden - width)))
    return jnp.concatenate([weight_in, weight_out, bias_in[:, None, :], padded[:, None, :]], axis=1)


def unpack(state):
    width = (state.shape[1] - 2) // 2
    return (
        state[:, :width],
        state[:, width : 2 * width],
        state[:, 2 * width],
        state[:, 2 * width + 1, :width],
    )


def inner_span(carry, block, step_rate):
    weight_in, weight_out, bias_in, bias_out = carry
    query_part, key_part, value_part = block
    rate = step_rate[:, None, None]
    length = query_part.shape[1]
    hidden_pre = dense("hcd,hdf->hcf", key_part, weight_in) + bias_in[:, None, :]
    hidden_act, gelu_back = jax.vjp(jax.nn.gelu, hidden_pre)
    out_pre = dense("hcf,hdf->hcd", hidden_act, weight_out) + bias_out[:, None, :]
    normed, norm_back = jax.vjp(inner_norm, out_pre)
    error = normed - (value_part - key_part)
    grad_out = norm_back(error)[0]
    grad_hidden = gelu_back(dense("hcd,hdf->hcf", grad_out, weight_out))[0]
    causal = jnp.tril(jnp.ones((length, length), jnp.float32))
    first_kernel = (dense("hcd,hsd->hcs", query_part, key_part) + 1.0) * causal
    query_pre = (
        dense("hcd,hdf->hcf", query_part, weight_in)
        + bias_in[:, None, :]
        - rate * dense("hcs,hsf->hcf", first_kernel, grad_hidden)
    )
    query_act = jax.nn.gelu(query_pre)
    second_kernel = (dense("hcf,hsf->hcs", query_act, hidden_act) + 1.0) * causal
    query_out = (
        dense("hcf,hdf->hcd", query_act, weight_out)
        + bias_out[:, None, :]
        - rate * dense("hcs,hsd->hcd", second_kernel, grad_out)
    )
    result = query_part + inner_norm(query_out)
    new_in = weight_in - rate * dense("hsd,hsf->hdf", key_part, grad_hidden)
    new_bias_in = bias_in - step_rate[:, None] * jnp.sum(grad_hidden, axis=1)
    new_out = weight_out - rate * dense("hsd,hsf->hdf", grad_out, hidden_act)
    new_bias_out = bias_out - step_rate[:, None] * jnp.sum(grad_out, axis=1)
    return ((new_in, new_out, new_bias_in, new_bias_out), result)


def inner_run(query_part, key_part, value_part, state, step_rate):
    heads, length, width = query_part.shape
    blocks = length // CH

    def split(array):
        return array.reshape(heads, blocks, CH, width).transpose(1, 0, 2, 3)

    def advance(carry, block):
        return inner_span(carry, block, step_rate)

    final, outputs = lax.scan(
        advance, unpack(state), (split(query_part), split(key_part), split(value_part))
    )
    return (outputs.transpose(1, 0, 2, 3).reshape(heads, length, width), pack(*final))


def prepare(query_rows, key_rows, value_rows):
    count = query_rows.shape[0]
    heads = query_rows.shape[1] // HD

    def heads_first(rows):
        return rows.reshape(count, heads, HD).transpose(1, 0, 2).astype(jnp.float32)

    return (
        rms_scale(heads_first(query_rows)),
        rms_scale(heads_first(key_rows)),
        heads_first(value_rows),
    )


def attend_local(query_cols, key_cols, value_cols, segment_row):
    length = query_cols.shape[0]
    local = query_cols.shape[1] // HD
    block = math.gcd(length, 512)

    def heads_first(rows):
        return rows.reshape(length, local, HD).transpose(1, 0, 2)

    def one_head(arrays):
        query_head, key_head, value_head = arrays

        def one_block(index):
            begin = index * block
            query_block = lax.dynamic_slice_in_dim(query_head, begin, block, 0)
            query_seg = lax.dynamic_slice_in_dim(segment_row, begin, block, 0)
            allowed = query_seg[:, None] == segment_row[None, :]
            scores = jnp.einsum(
                "qd,kd->qk", query_block, key_head, preferred_element_type=jnp.float32
            ) * HD ** (-0.5)
            scores = jnp.where(allowed, scores, -1e30)
            top = jnp.max(scores, axis=-1, keepdims=True)
            expo = jnp.where(allowed, jnp.exp(scores - top), 0.0)
            total = jnp.sum(expo, axis=-1, keepdims=True)
            shares = expo.astype(jnp.bfloat16)
            return (
                jnp.einsum("qk,kd->qd", shares, value_head, preferred_element_type=jnp.float32)
                / total
            )

        return lax.map(one_block, jnp.arange(length // block, dtype=jnp.int32)).reshape(length, HD)

    return lax.map(
        one_head, (heads_first(query_cols), heads_first(key_cols), heads_first(value_cols))
    )


def combine(attended, inner_out, branch_gate):
    heads, count, width = attended.shape
    joined = attended.transpose(1, 0, 2).reshape(count, heads * width)
    inner_rows = inner_out.transpose(1, 0, 2).reshape(count, heads * width)
    return (joined + jnp.tanh(branch_gate)[None, :] * inner_rows).astype(jnp.bfloat16)


def on_device(
    queries,
    key_states,
    value_states,
    segment_ids,
    inner_first,
    inner_second,
    inner_rate,
    branch_gate,
    out_weight,
):
    position = lax.axis_index("seq")
    parts = lax.axis_size("seq")
    segment_row = segment_ids[0]
    heads = inner_first.shape[0]
    start_state = pack(
        inner_first.astype(jnp.float32),
        inner_second.astype(jnp.float32),
        jnp.zeros((heads, FFI), jnp.float32),
        jnp.zeros((heads, HD), jnp.float32),
    )
    step_rate = inner_rate / HD
    query_cols, key_cols, value_cols = (
        lax.all_to_all(queries[0], "seq", split_axis=1, concat_axis=0, tiled=True),
        lax.all_to_all(key_states[0], "seq", split_axis=1, concat_axis=0, tiled=True),
        lax.all_to_all(value_states[0], "seq", split_axis=1, concat_axis=0, tiled=True),
    )
    local = heads // parts
    first = position * local
    attended = attend_local(query_cols, key_cols, value_cols, segment_row)
    query_part, key_part, value_part = prepare(query_cols, key_cols, value_cols)
    state_part = lax.dynamic_slice_in_dim(start_state, first, local, 0)
    rate_part = lax.dynamic_slice_in_dim(step_rate, first, local, 0)
    inner_out, final_state = inner_run(query_part, key_part, value_part, state_part, rate_part)
    gate_part = lax.dynamic_slice_in_dim(branch_gate, first * HD, local * HD, 0)
    mixed_cols = combine(attended, inner_out, gate_part)
    mixed = lax.all_to_all(mixed_cols, "seq", split_axis=0, concat_axis=1, tiled=True)
    projected = jnp.dot(
        mixed,
        lax.all_gather(out_weight, "dp", axis=0, tiled=True),
        preferred_element_type=jnp.float32,
    )
    return projected.astype(jnp.bfloat16)[None]


def solution(mesh):
    in_specs = (
        P("dp", "seq", None),
        P("dp", "seq", None),
        P("dp", "seq", None),
        P("dp", None),
        P(),
        P(),
        P(),
        P(),
        P("dp", None),
    )
    out_specs = P("dp", "seq", None)
    return jax.shard_map(
        on_device, mesh=mesh, in_specs=in_specs, out_specs=out_specs, check_vma=False
    )
```

profile of v0, /device:TPU:1, one launch (start us, length us, event | category | flops | bytes accessed | tf_op | source)
XLA Modules:
  0.0 290.0 jit_solution(11848517502450059110)
XLA Ops:
  6.5 2.0 copy.56
  8.6 10.0 %all-to-all-start.1 = ((bf16[128,8,192]{0,2,1:T(8,128)(2,1)}), bf16[128,8,192]{0,2,1:T(8,128)(2,1)S(1)}, u32[]{:S(2)}, u32[]{:S(2)}) async-start(bf16[128,8,192]{0,2,1:T(8,128)(2,1)} %bitcast.14), calls=%async_computation.1 | async-start | bytes 786432 | tf_op jit(solution)/shard_map/all_to_all | solution.py:175
  23.1 7.8 %all-to-all-done.1 = bf16[128,8,192]{0,2,1:T(8,128)(2,1)S(1)} async-done(((bf16[128,8,192]{0,2,1:T(8,128)(2,1)}), bf16[128,8,192]{0,2,1:T(8,128)(2,1)S(1)}, u32[]{:S(2)}, u32[]{:S(2)}) %all-to-all-start.1) | async-done | bytes 393248 | tf_op jit(solution)/shard_map/all_to_all | solution.py:175
  31.0 6.2 %all-to-all-start = ((bf16[128,8,192]{0,2,1:T(8,128)(2,1)}), bf16[128,8,192]{0,2,1:T(8,128)(2,1)S(1)}, u32[]{:S(2)}, u32[]{:S(2)}) async-start(bf16[128,8,192]{0,2,1:T(8,128)(2,1)} %bitcast.11), calls=%async_computation | async-start | bytes 786432 | tf_op jit(solution)/shard_map/all_to_all | solution.py:174
  38.5 17.7 %all-to-all-done = bf16[128,8,192]{0,2,1:T(8,128)(2,1)S(1)} async-done(((bf16[128,8,192]{0,2,1:T(8,128)(2,1)}), bf16[128,8,192]{0,2,1:T(8,128)(2,1)S(1)}, u32[]{:S(2)}, u32[]{:S(2)}) %all-to-all-start) | async-done | bytes 393248 | tf_op jit(solution)/shard_map/all_to_all | solution.py:174
  56.2 3.8 %all-to-all-start.2 = ((bf16[128,8,192]{0,2,1:T(8,128)(2,1)}), bf16[128,8,192]{0,2,1:T(8,128)(2,1)S(1)}, u32[]{:S(2)}, u32[]{:S(2)}) async-start(bf16[128,8,192]{0,2,1:T(8,128)(2,1)} %bitcast.17), calls=%async_computation.2 | async-start | bytes 786432 | tf_op jit(solution)/shard_map/all_to_all | solution.py:176
  60.1 1.6 reshape.143
  62.3 1.6 reshape.145
  63.9 14.8 %all-to-all-done.2 = bf16[128,8,192]{0,2,1:T(8,128)(2,1)S(1)} async-done(((bf16[128,8,192]{0,2,1:T(8,128)(2,1)}), bf16[128,8,192]{0,2,1:T(8,128)(2,1)S(1)}, u32[]{:S(2)}, u32[]{:S(2)}) %all-to-all-start.2) | async-done | bytes 393248 | tf_op jit(solution)/shard_map/all_to_all | solution.py:176
  79.2 1.6 reshape.148
  80.8 149.0 %while.42 = (s32[]{:T(128)}, f32[3,64,256]{2,1,0:T(8,128)S(1)}, f32[3,64,256]{2,1,0:T(8,128)S(1)}, f32[3,256]{1,0:T(4,128)S(1)}, f32[3,64]{1,0:T(4,128)S(1)}, /*...) while((s32[]{:T(128)}, f32[3,64,256]{2,1,0:T(8,128)S(1)}, ...), condition=%wide.region_17.18_spmd, body=%wide.region_8.17_spmd.sunk | while | flops 362064704 | bytes 6488765 | solution.py:88
  83.0 1.5 constant_dynamic-slice_fusion.13
  92.3 1.5 constant_dynamic-slice_fusion.13
  101.7 1.5 constant_dynamic-slice_fusion.13
  111.0 1.5 constant_dynamic-slice_fusion.13
  120.3 1.5 constant_dynamic-slice_fusion.13
  129.6 1.5 constant_dynamic-slice_fusion.13
  138.9 1.5 constant_dynamic-slice_fusion.13
  148.2 1.5 constant_dynamic-slice_fusion.13
  157.5 1.5 constant_dynamic-slice_fusion.13
  166.8 1.5 constant_dynamic-slice_fusion.13
  176.2 1.5 constant_dynamic-slice_fusion.13
  185.5 1.5 constant_dynamic-slice_fusion.13
  194.8 1.5 constant_dynamic-slice_fusion.13
  229.8 2.1 copy.71
  234.6 24.1 %while.41 = (s32[]{:T(128)}, f32[3,1024,64]{2,1,0:T(8,128)}, bf16[3,1024,64]{1,2,0:T(8,128)(2,1)S(1)}, bf16[3,1024,64]{1,2,0:T(8,128)(2,1)S(1)}, bf16[3,1024,64]...) while((s32[]{:T(128)}, f32[3,1024,64]{2,1,0:T(8,128)}, ...), condition=%wide.region_5.6_spmd, body=%wide.region_0.5_spmd.sunk | while | flops 142638080 | bytes 9995192 | solution.py:139
  235.2 6.3 %while.43 = (s32[]{:T(128)}, f32[2,512,64]{1,2,0:T(8,128)S(1)}, s32[2]{0:T(128)S(1)}, s32[1024]{0:T(1024)S(1)}, s32[1,1024]{1,0:T(1,128)S(1)}, /*index=5*/bf16[1...) while((s32[]{:T(128)}, f32[2,512,64]{1,2,0:T(8,128)S(1)}, ...), condition=%wide.region_4.4_spmd, body=%wide.region_1.3_spmd.sunk | while | flops 142638080 | bytes 7110843 | solution.py:137
  243.2 6.3 %while.43 = (s32[]{:T(128)}, f32[2,512,64]{1,2,0:T(8,128)S(1)}, s32[2]{0:T(128)S(1)}, s32[1024]{0:T(1024)S(1)}, s32[1,1024]{1,0:T(1,128)S(1)}, /*index=5*/bf16[1...) while((s32[]{:T(128)}, f32[2,512,64]{1,2,0:T(8,128)S(1)}, ...), condition=%wide.region_4.4_spmd, body=%wide.region_1.3_spmd.sunk | while | flops 142638080 | bytes 7110843 | solution.py:137
  251.2 6.3 %while.43 = (s32[]{:T(128)}, f32[2,512,64]{1,2,0:T(8,128)S(1)}, s32[2]{0:T(128)S(1)}, s32[1024]{0:T(1024)S(1)}, s32[1,1024]{1,0:T(1,128)S(1)}, /*index=5*/bf16[1...) while((s32[]{:T(128)}, f32[2,512,64]{1,2,0:T(8,128)S(1)}, ...), condition=%wide.region_4.4_spmd, body=%wide.region_1.3_spmd.sunk | while | flops 142638080 | bytes 7110843 | solution.py:137
  258.6 1.9 copy.63
  261.0 16.2 %all_to_all.64 = bf16[8,128,192]{1,2,0:T(8,128)(2,1)S(1)} all-to-all(bf16[8,128,192]{1,2,0:T(8,128)(2,1)S(1)} %copy.72), channel_id=1, replica_groups=mesh['dp'=32,'seq'=8] {'seq'}, dimensions={0} | all-to-all | bytes 786432 | tf_op jit(solution)/shard_map/all_to_all | solution.py:187
  277.2 6.0 %fusion.43 = bf16[1,128,3072]{2,1,0:T(8,128)(2,1)} fusion(bf16[128,1536]{0,1:T(8,128)(2,1)S(1)} %bitcast.206, bf16[1536,3072]{1,0:T(8,128)(2,1)} %all-gather.2.cloned.1.call-done), kind=kOutput, calls=%fused_computation.83 | convolution fusion | flops 1208352768 | bytes 10616832 | tf_op jit(solution)/shard_map/dot_general | solution.py:188
  (591 shorter events, 157.8 us)
Async XLA Ops:
  6.5 12.8 %copy-start.2 = (bf16[24,64,256]{2,1,0:T(8,128)(2,1)S(1)}, bf16[24,64,256]{2,1,0:T(8,128)(2,1)}, u32[]{:S(2)}) copy-start(bf16[24,64,256]{2,1,0:T(8,128)(2,1)} %param.19) | copy-start | bytes 2359300
  6.5 12.8 %copy-start.1 = (bf16[24,64,256]{2,1,0:T(8,128)(2,1)S(1)}, bf16[24,64,256]{2,1,0:T(8,128)(2,1)}, u32[]{:S(2)}) copy-start(bf16[24,64,256]{2,1,0:T(8,128)(2,1)} %param.20) | copy-start | bytes 2359300
  8.6 22.4 %all-to-all-start.1 = ((bf16[128,8,192]{0,2,1:T(8,128)(2,1)}), bf16[128,8,192]{0,2,1:T(8,128)(2,1)S(1)}, u32[]{:S(2)}, u32[]{:S(2)}) async-start(bf16[128,8,192]{0,2,1:T(8,128)(2,1)} %bitcast.14), calls=%async_computation.1 | async-start | bytes 786432 | tf_op jit(solution)/shard_map/all_to_all | solution.py:175
  18.5 258.6 %all-gather.2.cloned.1.call-start = ((), (), s32[]{:S(2)}) async-start(), calls=%async_computation.4 | async-start | bytes 9732096 | tf_op jit(solution)/shard_map/all_gather | solution.py:190
  20.3 0.7 copy-start.5
  20.3 1.0 copy-start.3
  20.6 1.6 copy-start.4
  31.0 25.2 %all-to-all-start = ((bf16[128,8,192]{0,2,1:T(8,128)(2,1)}), bf16[128,8,192]{0,2,1:T(8,128)(2,1)S(1)}, u32[]{:S(2)}, u32[]{:S(2)}) async-start(bf16[128,8,192]{0,2,1:T(8,128)(2,1)} %bitcast.11), calls=%async_computation | async-start | bytes 786432 | tf_op jit(solution)/shard_map/all_to_all | solution.py:174
  56.2 22.5 %all-to-all-start.2 = ((bf16[128,8,192]{0,2,1:T(8,128)(2,1)}), bf16[128,8,192]{0,2,1:T(8,128)(2,1)S(1)}, u32[]{:S(2)}, u32[]{:S(2)}) async-start(bf16[128,8,192]{0,2,1:T(8,128)(2,1)} %bitcast.17), calls=%async_computation.2 | async-start | bytes 786432 | tf_op jit(solution)/shard_map/all_to_all | solution.py:176
  231.9 2.6 copy-start
Sparse Core Ops, SparseCore 0:
  21.1 232.0 all-gather.1
where the time goes:
time: 293 us; the launch traced here: 290 us
  matrix products  82 us (28%)
  local copies, waits for them, and re-layouts  75.2 us (26%)
  waiting for transfers between devices  41 us (14%)
  other arithmetic  36.5 us (12%)
  starting transfers between devices  19.9 us (7%)
  blocking collectives  16.2 us (6%)
  between operations  13.7 us (5%)
  loops' own time  5.48 us (2%)
    dot_general x176, matrix products, dense(): return jnp.einsum(form, left, right, precision=lax.Precision.HIGHEST)  68.4 us
    dynamic_slice x80, local copies, waits for them, and re-layouts, inner_run(): lax.scan(advance, unpack(state), (split(query_part), split(key_part), spl...  48.5 us
    all_to_all x1, waiting for transfers between devices, on_device(): lax.all_to_all(queries[0], 'seq', split_axis=1, concat_axis=0, tiled=True)  17.7 us
    all_to_all x1, blocking collectives, on_device(): lax.all_to_all(mixed_cols, 'seq', split_axis=0, concat_axis=1, tiled=True)  16.2 us
    all_to_all x1, waiting for transfers between devices, on_device(): lax.all_to_all(value_states[0], 'seq', split_axis=1, concat_axis=0, tiled...  14.8 us
    dynamic_update_slice x16, other arithmetic, inner_run(): lax.scan(advance, unpack(state), (split(query_part), split(key_part), spl...  12.2 us
    all_to_all x1, starting transfers between devices, on_device(): lax.all_to_all(key_states[0], 'seq', split_axis=1, concat_axis=0, tiled=T...  9.97 us
    all_to_all x1, waiting for transfers between devices, on_device(): lax.all_to_all(key_states[0], 'seq', split_axis=1, concat_axis=0, tiled=T...  7.83 us
  transfers between devices with their start and end apart: 4, of which 3 were waited for; matrix products, arithmetic and copies ran while one was open for 64% of the time, Pallas kernels for 0%

commit v1 on v0

v1 whole, which is shorter than its diff:
```python
import functools
import math

import jax
import jax.numpy as jnp
from jax import lax
from jax.experimental import pallas as pl
from jax.experimental.pallas import tpu as pltpu
from jax.sharding import PartitionSpec as P

HD = 64
FFI = 256
CH = 64
LOCAL = 3
PARTS = 8
TOK = 128
LEN = 1024
HH = 1536
WIDTH = LOCAL * HD
SAME = 32.0
EPS = 1e-6
GA = math.sqrt(2.0 / math.pi)
GB = GA * 0.044715
VMEM_MOST = 56 * 1024 * 1024

f32 = jnp.float32
bf16 = jnp.bfloat16


def dot(left, right):
    return jnp.dot(left, right, preferred_element_type=f32)


def dot_nt(left, right):
    return lax.dot_general(left, right, (((1,), (1,)), ((), ())), preferred_element_type=f32)


def dot_tn(left, right):
    return lax.dot_general(left, right, (((0,), (0,)), ((), ())), preferred_element_type=f32)


def lane_mean(value):
    return jnp.mean(value, axis=-1, keepdims=True)


def pack_kernel(me_ref, q_ref, k_ref, v_ref, *rest):
    outs, held, sems = rest[:PARTS], rest[PARTS], rest[PARTS + 1]
    for part in range(PARTS):
        cols = slice(part * WIDTH, (part + 1) * WIDTH)
        for group, ref in enumerate((q_ref, k_ref, v_ref)):
            for half in range(2):
                at = (2 * group + half) * WIDTH
                held[part, :, at : at + WIDTH] = ref[half * CH : (half + 1) * CH, cols]
    me = me_ref[0]
    copies = []
    for step in range(PARTS):
        copies.append(pltpu.make_async_copy(held.at[lax.rem(me + step, PARTS)], outs[step], sems.at[step]))
    for copy in copies:
        copy.start()
    for copy in copies:
        copy.wait()


def pack(me, queries, keys, values):
    vmem = pl.BlockSpec(memory_space=pltpu.VMEM)
    return pl.pallas_call(
        pack_kernel,
        out_shape=[jax.ShapeDtypeStruct((CH, 6 * WIDTH), bf16)] * PARTS,
        in_specs=[pl.BlockSpec(memory_space=pltpu.SMEM), vmem, vmem, vmem],
        out_specs=[pl.BlockSpec(memory_space=pl.ANY)] * PARTS,
        scratch_shapes=[pltpu.VMEM((PARTS, CH, 6 * WIDTH), bf16), pltpu.SemaphoreType.DMA((PARTS,))],
        compiler_params=pltpu.CompilerParams(vmem_limit_bytes=VMEM_MOST),
        name="pack_rows",
    )(me, queries, keys, values)


def gelu_parts(z, slope):
    square = z * z
    half = 0.5 * jnp.tanh(z * (GB * square + GA)) + 0.5
    act = z * half
    if not slope:
        return act, None
    return act, half + (act - act * half) * (6.0 * GB * square + 2.0 * GA)


def heads_kernel(
    me_ref, rate_ref, *rest,
):
    xs = rest[:PARTS]
    seg_ref, first_ref, second_ref, gate_ref = rest[PARTS : PARTS + 4]
    outs = rest[PARTS + 4 : 2 * PARTS + 4]
    (
        x, w1, w2, mixed, q_aug, k_aug, v_aug, att,
        w1s, w2s, b1s, b2s, z1s, q1s, a_prev, g2_prev, b2_prev, xq_prev,
        sems, wsems,
    ) = rest[2 * PARTS + 4 :]
    me = me_ref[0]
    copies = [
        pltpu.make_async_copy(xs[step], x.at[lax.rem(me + PARTS - step, PARTS)], sems.at[step])
        for step in range(PARTS)
    ]
    weights = [
        pltpu.make_async_copy(first_ref.at[pl.ds(me * LOCAL, LOCAL)], w1, wsems.at[0]),
        pltpu.make_async_copy(second_ref.at[pl.ds(me * LOCAL, LOCAL)], w2, wsems.at[1]),
    ]
    for copy in copies + weights:
        copy.start()
    for copy in copies + weights:
        copy.wait()

    def cut(group, head, source, half):
        at = (2 * group + half) * WIDTH + head * HD
        return x[source, :, at : at + HD]

    def prepare(source, carry):
        for half in range(2):
            rows = pl.ds(pl.multiple_of(source * TOK + half * CH, CH), CH)
            seg = seg_ref[rows, :]
            ones = jnp.ones((CH, HD), bf16)
            for head in range(LOCAL):
                q_aug[head, rows, :] = jnp.concatenate([cut(0, head, source, half) * 0.125, seg], axis=1).astype(bf16)
                k_aug[head, rows, :] = jnp.concatenate([cut(1, head, source, half), seg], axis=1)
                v_aug[head, rows, :] = jnp.concatenate([cut(2, head, source, half), ones], axis=1)
        return carry

    lax.fori_loop(0, PARTS, prepare, 0)

    def attend(source, carry):
        rows = pl.ds(pl.multiple_of(source * TOK, TOK), TOK)
        for head in range(LOCAL):
            scores = dot_nt(q_aug[head, rows, :], k_aug[head])
            top = jnp.max(scores, axis=-1, keepdims=True)
            shares = jnp.exp(scores - top).astype(bf16)
            got = dot(shares, v_aug[head])
            att[head, rows, :] = got[:, :HD] / got[:, HD:]
        return carry

    lax.fori_loop(0, PARTS, attend, 0)

    causal = lax.broadcasted_iota(jnp.int32, (CH, CH), 0) >= lax.broadcasted_iota(jnp.int32, (CH, CH), 1)

    def rms(value):
        return lax.rsqrt(lane_mean(value * value) + EPS)

    def stacked(head, q_source, q_half, k_source, k_half):
        q = cut(0, head, q_source, q_half)
        k = cut(1, head, k_source, k_half)
        rows = jnp.concatenate([q, k], axis=0)
        wide = rows.astype(f32)
        scale = rms(wide)
        return rows, wide * scale, scale

    def project(head, rows, scale):
        state = w1s[head]
        high = state.astype(bf16)
        low = (state - high.astype(f32)).astype(bf16)
        both = dot(jnp.concatenate([rows, rows], axis=1), jnp.concatenate([high, low], axis=0))
        return both * scale + b1s[head]

    for head in range(LOCAL):
        w1s[head] = w1[head].astype(f32)
        start = w2[head].astype(f32)
        w2s[head] = start - jnp.mean(start, axis=0, keepdims=True)
        b1s[head] = jnp.zeros((1, FFI), f32)
        b2s[head] = jnp.zeros((1, HD), f32)
        b2_prev[head] = jnp.zeros((1, HD), f32)
        k = cut(1, head, 0, 0)
        z1s[head] = project(head, k, rms(k.astype(f32)))
        q1s[head] = jnp.zeros((CH, FFI), f32)
        a_prev[head] = jnp.zeros((CH + HD, FFI), bf16)
        g2_prev[head] = jnp.zeros((CH, HD), bf16)
        xq_prev[head] = jnp.zeros((CH, HD), f32)

    def query_side(block):
        rows = pl.ds(pl.multiple_of(block * CH, CH), CH)
        for head in range(LOCAL):
            act, _ = gelu_parts(q1s[head], False)
            high = act.astype(bf16)
            low = (act - high.astype(f32)).astype(bf16)
            both = dot_nt(high, a_prev[head])
            second = jnp.where(causal, both[:, :CH] + 1.0, 0.0).astype(bf16)
            out = both[:, CH:] + dot_nt(low, a_prev[head, CH:, :]) + b2_prev[head] - dot(second, g2_prev[head])
            inner = xq_prev[head] + out * lax.rsqrt(lane_mean(out * out) + EPS)
            gate = jnp.tanh(gate_ref[me * LOCAL + head])
            yield (att[head, rows, :] + gate * inner).astype(bf16)

    def key_side(source, half, next_source, next_half):
        for head in range(LOCAL):
            eta = rate_ref[me * LOCAL + head] * (1.0 / HD)
            k = cut(1, head, source, half).astype(f32)
            keys = k * rms(k)
            target = cut(2, head, source, half).astype(f32) - keys
            target = target - lane_mean(target)
            keys_low = keys.astype(bf16)
            rows, normed, scale = stacked(head, source, half, next_source, next_half)
            ahead = project(head, rows, scale)
            cross = dot_nt(normed.astype(bf16), keys_low) + 1.0
            cross = jnp.concatenate([jnp.where(causal, cross[:CH], 0.0), cross[CH:]], axis=0).astype(bf16)

            act, slope = gelu_parts(z1s[head], True)
            act_low = act.astype(bf16)
            second = w2s[head]
            second_low = second.astype(bf16)
            c = dot_nt(act_low, second_low) + b2s[head]
            r = lax.rsqrt(lane_mean(c * c) + EPS)
            mix = lane_mean(c * target)
            grad = (eta * r) * (c * (r * (EPS * r * r + mix * r)) - target)
            grad_low = grad.astype(bf16)
            deep = dot(grad_low, second_low) * slope
            deep_low = deep.astype(bf16)
            both = ahead - dot(cross, deep_low)

            q1s[head] = both[:CH]
            z1s[head] = both[CH:]
            a_prev[head, :CH, :] = act_low
            a_prev[head, CH:, :] = second_low
            g2_prev[head] = grad_low
            b2_prev[head] = b2s[head]
            xq_prev[head] = normed[:CH]
            w1s[head] = w1s[head] - dot_tn(keys_low, deep_low)
            b1s[head] = b1s[head] - jnp.sum(deep, axis=0, keepdims=True)
            w2s[head] = second - dot_tn(grad_low, act_low)
            b2s[head] = b2s[head] - jnp.sum(grad, axis=0, keepdims=True)

    def blocks(source, carry):
        for head, rows in enumerate(query_side(jnp.maximum(2 * source - 1, 0))):
            mixed[source, :, WIDTH + head * HD : WIDTH + (head + 1) * HD] = rows
        key_side(source, 0, source, 1)
        for head, rows in enumerate(query_side(2 * source)):
            mixed[source + 1, :, head * HD : (head + 1) * HD] = rows
        key_side(source, 1, jnp.minimum(source + 1, PARTS - 1), 0)
        return carry

    lax.fori_loop(0, PARTS, blocks, 0)
    for head, rows in enumerate(query_side(2 * PARTS - 1)):
        mixed[PARTS, :, WIDTH + head * HD : WIDTH + (head + 1) * HD] = rows

    copies = [
        pltpu.make_async_copy(mixed.at[1 + lax.rem(me + step, PARTS)], outs[step], sems.at[step])
        for step in range(PARTS)
    ]
    for copy in copies:
        copy.start()
    for copy in copies:
        copy.wait()


def run_heads(me, rate, pieces, seg, first, second, gate):
    vmem = pl.BlockSpec(memory_space=pltpu.VMEM)
    smem = pl.BlockSpec(memory_space=pltpu.SMEM)
    hbm = pl.BlockSpec(memory_space=pl.ANY)
    return pl.pallas_call(
        heads_kernel,
        out_shape=[jax.ShapeDtypeStruct((CH, 2 * WIDTH), bf16)] * PARTS,
        in_specs=[smem, smem] + [hbm] * PARTS + [vmem, hbm, hbm, vmem],
        out_specs=[hbm] * PARTS,
        scratch_shapes=[
            pltpu.VMEM((PARTS, CH, 6 * WIDTH), bf16),
            pltpu.VMEM((LOCAL, HD, FFI), bf16),
            pltpu.VMEM((LOCAL, HD, FFI), bf16),
            pltpu.VMEM((PARTS + 1, CH, 2 * WIDTH), bf16),
            pltpu.VMEM((LOCAL, LEN, 2 * HD), bf16),
            pltpu.VMEM((LOCAL, LEN, 2 * HD), bf16),
            pltpu.VMEM((LOCAL, LEN, 2 * HD), bf16),
            pltpu.VMEM((LOCAL, LEN, HD), f32),
            pltpu.VMEM((LOCAL, HD, FFI), f32),
            pltpu.VMEM((LOCAL, HD, FFI), f32),
            pltpu.VMEM((LOCAL, 1, FFI), f32),
            pltpu.VMEM((LOCAL, 1, HD), f32),
            pltpu.VMEM((LOCAL, CH, FFI), f32),
            pltpu.VMEM((LOCAL, CH, FFI), f32),
            pltpu.VMEM((LOCAL, CH + HD, FFI), bf16),
            pltpu.VMEM((LOCAL, CH, HD), bf16),
            pltpu.VMEM((LOCAL, 1, HD), f32),
            pltpu.VMEM((LOCAL, CH, HD), f32),
            pltpu.SemaphoreType.DMA((PARTS,)),
            pltpu.SemaphoreType.DMA((2,)),
        ],
        compiler_params=pltpu.CompilerParams(vmem_limit_bytes=VMEM_MOST),
        name="run_heads",
    )(me, rate, *pieces, seg, first, second, gate)


def project_kernel(place_ref, *rest):
    mixed = rest[:PARTS]
    own, sib = rest[PARTS : PARTS + 4], rest[PARTS + 4 : PARTS + 8]
    out, held, weight, sems, wsems = rest[PARTS + 8 :]
    me, dp = place_ref[0], place_ref[1]
    core = lax.rem(me, 2)
    copies = [
        pltpu.make_async_copy(mixed[step], held.at[lax.rem(me + PARTS - step, PARTS)], sems.at[step])
        for step in range(PARTS)
    ]
    y, x, z = dp // 8, lax.rem(dp // 2, 4), lax.rem(dp, 2)
    for side, blocks in enumerate((own, sib)):
        axis = core if side == 0 else 1 - core
        for i, far in enumerate(STEPS):
            for j, near in enumerate(STEPS):
                dx = jnp.where(axis == 0, near, far)
                dy = jnp.where(axis == 0, far, near)
                line = lax.rem(y + 4 - dy, 4) * 8 + lax.rem(x + 4 - dx, 4) * 2
                for flip in range(2):
                    row = pl.multiple_of((line + (z + flip) - 2 * z * flip) * ROWS, ROWS)
                    slot = (2 * j + flip) * ROWS
                    copies.append(
                        pltpu.make_async_copy(
                            blocks[i].at[pl.ds(slot, ROWS)],
                            weight.at[axis, pl.ds(row, ROWS)],
                            wsems.at[side, 8 * i + 2 * j + flip],
                        )
                    )
    for copy in copies:
        copy.start()
    for copy in copies:
        copy.wait()
    rows = [jnp.concatenate([held[part, :, half * WIDTH : (half + 1) * WIDTH] for part in range(PARTS)], axis=1) for half in range(2)]
    rows = jnp.concatenate(rows, axis=0)
    wide = weight.shape[2]
    for side in range(2):
        for at in range(0, wide, 256):
            out[:, side * wide + at : side * wide + at + 256] = dot(rows, weight[side, :, at : at + 256]).astype(bf16)


def run_project(place, mixed, own, sib):
    hbm = pl.BlockSpec(memory_space=pl.ANY)
    wide = own[0].shape[1]
    return pl.pallas_call(
        project_kernel,
        out_shape=jax.ShapeDtypeStruct((TOK, 2 * wide), bf16),
        in_specs=[pl.BlockSpec(memory_space=pltpu.SMEM)] + [hbm] * (PARTS + 8),
        out_specs=pl.BlockSpec(memory_space=pltpu.VMEM),
        scratch_shapes=[
            pltpu.VMEM((PARTS, CH, 2 * WIDTH), bf16),
            pltpu.VMEM((2, HH, wide), bf16),
            pltpu.SemaphoreType.DMA((PARTS,)),
            pltpu.SemaphoreType.DMA((2, 32)),
        ],
        compiler_params=pltpu.CompilerParams(vmem_limit_bytes=VMEM_MOST),
        name="project_rows",
    )(place, *mixed, *own, *sib)


ROWS = HH // 32
STEPS = (0, 1, 3, 2)


def where_is(index):
    dp, seq = divmod(index, PARTS)
    return dp // 8, (dp // 2) % 4, dp % 2, seq // 2, seq % 2


def index_of(y, x, z, group, core):
    return ((y % 4) * 8 + (x % 4) * 2 + z % 2) * PARTS + (group % 4) * 2 + core % 2


def move(array, place):
    pairs = [(i, index_of(*place(*where_is(i)))) for i in range(32 * PARTS)]
    return lax.ppermute(array, ("dp", "seq"), pairs)


def turn(array, step):
    return lax.ppermute(array, "seq", [(i, (i + step) % PARTS) for i in range(PARTS)])


def near_axis(step):
    return lambda y, x, z, group, core: (y + step * core, x + step * (1 - core), z, group, core)


def far_axis(step):
    return lambda y, x, z, group, core: (y + step * (1 - core), x + step * core, z, group, core)


def flip_z(y, x, z, group, core):
    return y, x, 1 - z, group, core


def flip_core(y, x, z, group, core):
    return y, x, z, group, 1 - core


def on_device(
    queries, key_states, value_states, segment_ids, inner_first, inner_second, inner_rate, branch_gate, out_weight
):
    seq, dp = lax.axis_index("seq"), lax.axis_index("dp")
    place = jnp.stack([seq, dp]).astype(jnp.int32)
    wide = out_weight.shape[1] // 2
    slab = lax.dynamic_slice_in_dim(out_weight, (seq % 2) * wide, wide, 1)
    slab = jnp.concatenate([slab, move(slab, flip_z)], axis=0)

    pieces = pack(place, queries[0], key_states[0], value_states[0])
    pieces = [pieces[0]] + [turn(pieces[step], step) for step in range(1, PARTS)]

    slab = jnp.concatenate([slab] + [move(slab, near_axis(step)) for step in STEPS[1:]], axis=0)
    own = [slab] + [move(slab, far_axis(step)) for step in STEPS[1:]]

    seg = jnp.where(segment_ids[0][:, None] == jnp.arange(HD)[None, :], SAME, 0.0).astype(bf16)
    gate = branch_gate.reshape(-1, 1, HD)
    mixed = run_heads(place, inner_rate, pieces, seg, inner_first, inner_second, gate)
    mixed = [mixed[0]] + [turn(mixed[step], step) for step in range(1, PARTS)]
    sib = [move(block, flip_core) for block in own]
    return run_project(place, mixed, own, sib)[None]


def solution(mesh):
    in_specs = (
        P("dp", "seq", None),
        P("dp", "seq", None),
        P("dp", "seq", None),
        P("dp", None),
        P(),
        P(),
        P(),
        P(),
        P("dp", None),
    )
    return jax.shard_map(
        on_device, mesh=mesh, in_specs=in_specs, out_specs=P("dp", "seq", None), check_vma=False
    )
```

time: 293 us -> 195 us (0.67)
  matrix products: 82 us -> 0 us
  local copies, waits for them, and re-layouts: 75.2 us -> 2.91 us
  Pallas kernels: 0 us -> 53.5 us
  starting transfers between devices: 19.9 us -> 68.3 us
  other arithmetic: 36.5 us -> 1.57 us
  waiting for transfers between devices: 41 us -> 67.9 us
  blocking collectives: 16.2 us -> 0 us
  between operations: 13.7 us -> 0.36 us
  loops' own time: 5.48 us -> 0 us
    dot_general x189 -> x0, matrix products: 82 us -> none  [the longest x176 68.4 us: dense(): return jnp.einsum(form, left, right, precision=lax.Precision.HIGHEST)]
    ppermute x0 -> x25, starting transfers between devices: none -> 68.3 us  [the longest x14 48.6 us: turn(): lax.ppermute(array, 'seq', [(i, (i + step) % PARTS) for i in range(PARTS)])]
    ppermute x0 -> x25, waiting for transfers between devices: none -> 67.9 us  [the longest x14 50.4 us: turn(): lax.ppermute(array, 'seq', [(i, (i + step) % PARTS) for i in range(PARTS)])]
    dynamic_slice x108 -> x0, local copies, waits for them, and re-layouts: 54.1 us -> none  [the longest x80 48.5 us: inner_run(): lax.scan(advance, unpack(state), (split(query_part), split(key_part), spl...]
    pallas_call x0 -> x3, Pallas kernels: none -> 53.5 us  [the longest x1 43.3 us: run_heads(): pl.pallas_call(heads_kernel, out_shape=[jax.ShapeDtypeStruct((CH, 2 * WID...]
    all_to_all x3 -> x0, waiting for transfers between devices: 40.3 us -> none  [the longest x1 17.7 us: on_device(): lax.all_to_all(queries[0], 'seq', split_axis=1, concat_axis=0, tiled=True)]
    all_to_all x3 -> x0, starting transfers between devices: 19.9 us -> none  [the longest x1 9.97 us: on_device(): lax.all_to_all(key_states[0], 'seq', split_axis=1, concat_axis=0, tiled=T...]
    reduce_sum x88 -> x0, other arithmetic: 19.1 us -> none  [the longest x32 5.67 us: inner_norm(): spread = jnp.mean(center * center, axis=-1, keepdims=True)]
  transfers between devices with their start and end apart: 4 -> 25, of which waited for: 3 -> 18; matrix products, arithmetic and copies ran while one was open for 64% -> 1% of each run, Pallas kernels for 0% -> 24%
where the time goes in v1:
time: 195 us
  starting transfers between devices  68.3 us (35%)
  waiting for transfers between devices  67.9 us (35%)
  Pallas kernels  53.5 us (27%)
  local copies, waits for them, and re-layouts  2.91 us (1%)
    ppermute x14, waiting for transfers between devices, turn(): lax.ppermute(array, 'seq', [(i, (i + step) % PARTS) for i in range(PARTS)])  50.4 us
    ppermute x14, starting transfers between devices, turn(): lax.ppermute(array, 'seq', [(i, (i + step) % PARTS) for i in range(PARTS)])  48.6 us
    pallas_call x1, Pallas kernels, run_heads(): pl.pallas_call(heads_kernel, out_shape=[jax.ShapeDtypeStruct((CH, 2 * WID...  43.3 us
    ppermute x11, starting transfers between devices, move(): return lax.ppermute(array, ('dp', 'seq'), pairs)  19.7 us
    ppermute x11, waiting for transfers between devices, move(): return lax.ppermute(array, ('dp', 'seq'), pairs)  17.6 us
    pallas_call x1, Pallas kernels, run_project(): pl.pallas_call(project_kernel, out_shape=jax.ShapeDtypeStruct((TOK, 2 * w...  7.58 us
  transfers between devices with their start and end apart: 25, of which 18 were waited for; matrix products, arithmetic and copies ran while one was open for 1% of the time, Pallas kernels for 24%

profile of v1, /device:TPU:1, one launch (start us, length us, event | category | flops | bytes accessed | tf_op | source)
XLA Modules:
  0.0 194.6 jit_solution(1095114461174184136)
XLA Ops:
  0.9 2.6 %collective-permute-start.14 = (bf16[48,1536]{1,0:T(8,128)(2,1)S(1)}, bf16[48,1536]{1,0:T(8,128)(2,1)S(1)}, u32[]{:S(2)}, u32[]{:S(2)}) collective-permute-start(bf16[48,1536]{1,0:T(8,128)(2,1)S(1)} %get-tuple-element.38), channel_id=1, source_target_pairs={{0,8},{1,9},{2,10},{3,11},{4,12},{5,13},{6,14},{7,15},{8,0},{9,1},... | collective-permute-start | bytes 442376 | tf_op jit(solution)/shard_map/ppermute | solution.py:358
  3.5 2.5 %collective-permute-done.14 = bf16[48,1536]{1,0:T(8,128)(2,1)S(1)} collective-permute-done((bf16[48,1536]{1,0:T(8,128)(2,1)S(1)}, bf16[48,1536]{1,0:T(8,128)(2,1)S(1)}, u32[]{:S(2)}, u32[]{:S(2)}) %collective-permute-start.14) | collective-permute-done | bytes 147488 | tf_op jit(solution)/shard_map/ppermute | solution.py:358
  6.0 2.3 %collective-permute-start.15 = (bf16[96,1536]{1,0:T(8,128)(2,1)S(1)}, bf16[96,1536]{1,0:T(8,128)(2,1)S(1)}, u32[]{:S(2)}, u32[]{:S(2)}) collective-permute-start(bf16[96,1536]{1,0:T(8,128)(2,1)S(1)} %pad_maximum_fusion), channel_id=1, source_target_pairs={{0,16},{1,65},{2,18},{3,67},{4,20},{5,69},{6,22},{7,71},{8,24},{9,... | collective-permute-start | bytes 884744 | tf_op jit(solution)/shard_map/ppermute | solution.py:358
  8.3 2.6 %collective-permute-start.17 = (bf16[96,1536]{1,0:T(8,128)(2,1)S(1)}, bf16[96,1536]{1,0:T(8,128)(2,1)S(1)}, u32[]{:S(2)}, u32[]{:S(2)}) collective-permute-start(bf16[96,1536]{1,0:T(8,128)(2,1)S(1)} %pad_maximum_fusion), channel_id=1, source_target_pairs={{0,32},{1,129},{2,34},{3,131},{4,36},{5,133},{6,38},{7,135},{8,40}... | collective-permute-start | bytes 884744 | tf_op jit(solution)/shard_map/ppermute | solution.py:358
  14.2 3.8 %collective-permute-done.16 = bf16[96,1536]{1,0:T(8,128)(2,1)S(1)} collective-permute-done((bf16[96,1536]{1,0:T(8,128)(2,1)S(1)}, bf16[96,1536]{1,0:T(8,128)(2,1)S(1)}, u32[]{:S(2)}, u32[]{:S(2)}) %collective-permute-start.16) | collective-permute-done | bytes 294944 | tf_op jit(solution)/shard_map/ppermute | solution.py:358
  18.6 2.5 %collective-permute-start.20 = (bf16[384,1536]{1,0:T(8,128)(2,1)S(1)}, bf16[384,1536]{1,0:T(8,128)(2,1)S(1)}, u32[]{:S(2)}, u32[]{:S(2)}) collective-permute-start(bf16[384,1536]{1,0:T(8,128)(2,1)S(1)} %constant_dynamic-update-slice_fusion.rest_8_), channel_id=1, source_target_pairs={{0,128},{1,33},{2,130},{3,35},{4,132},{5,37},{6,134},{7,39},{8,136... | collective-permute-start | bytes 3538952 | tf_op jit(solution)/shard_map/ppermute | solution.py:358
  23.2 2.6 %pack_rows.1 = (bf16[64,1152]{1,0:T(8,128)(2,1)}, bf16[64,1152]{1,0:T(8,128)(2,1)}, bf16[64,1152]{1,0:T(8,128)(2,1)}, bf16[64,1152]{1,0:T(8,128)(2,1)}, bf16[64,...) custom-call(s32[2]{0:T(128)} %pad_add_fusion.me_ref.place_ref, ...), custom_call_target="tpu_custom_call" | custom-call | tf_op jit(solution)/shard_map/pack_rows/pallas_call | solution.py:66
  25.8 6.2 %collective-permute-start = (bf16[64,1152]{1,0:T(8,128)(2,1)}, bf16[64,1152]{1,0:T(8,128)(2,1)S(1)}, u32[]{:S(2)}, u32[]{:S(2)}) collective-permute-start(bf16[64,1152]{1,0:T(8,128)(2,1)} %get-tuple-element.22), channel_id=1, source_target_pairs={{0,1},{1,2},{2,3},{3,4},{4,5},{5,6},{6,7},{7,0},{8,9},{9,10},{10,1... | collective-permute-start | bytes 442376 | tf_op jit(solution)/shard_map/ppermute | solution.py:362
  32.0 4.0 %collective-permute-start.1 = (bf16[64,1152]{1,0:T(8,128)(2,1)}, bf16[64,1152]{1,0:T(8,128)(2,1)}, u32[]{:S(2)}, u32[]{:S(2)}) collective-permute-start(bf16[64,1152]{1,0:T(8,128)(2,1)} %get-tuple-element.23), channel_id=1, source_target_pairs={{0,2},{1,3},{2,4},{3,5},{4,6},{5,7},{6,0},{7,1},{8,10},{9,11},{10,... | collective-permute-start | bytes 442376 | tf_op jit(solution)/shard_map/ppermute | solution.py:362
  36.3 3.2 %collective-permute-start.24 = (bf16[384,1536]{1,0:T(8,128)(2,1)S(1)}, bf16[384,1536]{1,0:T(8,128)(2,1)}, u32[]{:S(2)}, u32[]{:S(2)}) collective-permute-start(bf16[384,1536]{1,0:T(8,128)(2,1)S(1)} %collective-permute-done.20.rest_11_), channel_id=1, source_target_pairs={{0,1},{1,0},{2,3},{3,2},{4,5},{5,4},{6,7},{7,6},{8,9},{9,8},{10,11... | collective-permute-start | bytes 3538952 | tf_op jit(solution)/shard_map/ppermute | solution.py:358
  39.5 8.6 %collective-permute-done.19.rest_10_ = bf16[384,1536]{1,0:T(8,128)(2,1)S(1)} collective-permute-done((bf16[384,1536]{1,0:T(8,128)(2,1)S(1)}, bf16[384,1536]{1,0:T(8,128)(2,1)S(1)}, u32[]{:S(2)}, u32[]{:S(2)}) %collective-permute-start.19) | collective-permute-done | bytes 1179680 | tf_op jit(solution)/shard_map/ppermute | solution.py:358
  48.1 3.2 %collective-permute-start.23 = (bf16[384,1536]{1,0:T(8,128)(2,1)S(1)}, bf16[384,1536]{1,0:T(8,128)(2,1)}, u32[]{:S(2)}, u32[]{:S(2)}) collective-permute-start(bf16[384,1536]{1,0:T(8,128)(2,1)S(1)} %collective-permute-done.19.rest_10_), channel_id=1, source_target_pairs={{0,1},{1,0},{2,3},{3,2},{4,5},{5,4},{6,7},{7,6},{8,9},{9,8},{10,11... | collective-permute-start | bytes 3538952 | tf_op jit(solution)/shard_map/ppermute | solution.py:358
  52.1 6.3 %collective-permute-start.2 = (bf16[64,1152]{1,0:T(8,128)(2,1)}, bf16[64,1152]{1,0:T(8,128)(2,1)}, u32[]{:S(2)}, u32[]{:S(2)}) collective-permute-start(bf16[64,1152]{1,0:T(8,128)(2,1)} %get-tuple-element.24), channel_id=1, source_target_pairs={{0,3},{1,4},{2,5},{3,6},{4,7},{5,0},{6,1},{7,2},{8,11},{9,12},{10,... | collective-permute-start | bytes 442376 | tf_op jit(solution)/shard_map/ppermute | solution.py:362
  58.5 6.9 %collective-permute-done.2.rest_3_ = bf16[64,1152]{1,0:T(8,128)(2,1)} collective-permute-done((bf16[64,1152]{1,0:T(8,128)(2,1)}, bf16[64,1152]{1,0:T(8,128)(2,1)}, u32[]{:S(2)}, u32[]{:S(2)}) %collective-permute-start.2) | collective-permute-done | bytes 147488 | tf_op jit(solution)/shard_map/ppermute | solution.py:362
  65.4 4.1 %collective-permute-start.3 = (bf16[64,1152]{1,0:T(8,128)(2,1)}, bf16[64,1152]{1,0:T(8,128)(2,1)}, u32[]{:S(2)}, u32[]{:S(2)}) collective-permute-start(bf16[64,1152]{1,0:T(8,128)(2,1)} %get-tuple-element.25), channel_id=1, source_target_pairs={{0,4},{1,5},{2,6},{3,7},{4,0},{5,1},{6,2},{7,3},{8,12},{9,13},{10,... | collective-permute-start | bytes 442376 | tf_op jit(solution)/shard_map/ppermute | solution.py:362
  69.5 5.2 %collective-permute-done.3.rest_4_ = bf16[64,1152]{1,0:T(8,128)(2,1)} collective-permute-done((bf16[64,1152]{1,0:T(8,128)(2,1)}, bf16[64,1152]{1,0:T(8,128)(2,1)}, u32[]{:S(2)}, u32[]{:S(2)}) %collective-permute-start.3) | collective-permute-done | bytes 147488 | tf_op jit(solution)/shard_map/ppermute | solution.py:362
  74.7 6.8 %collective-permute-start.4 = (bf16[64,1152]{1,0:T(8,128)(2,1)}, bf16[64,1152]{1,0:T(8,128)(2,1)}, u32[]{:S(2)}, u32[]{:S(2)}) collective-permute-start(bf16[64,1152]{1,0:T(8,128)(2,1)} %get-tuple-element.26), channel_id=1, source_target_pairs={{0,5},{1,6},{2,7},{3,0},{4,1},{5,2},{6,3},{7,4},{8,13},{9,14},{10,... | collective-permute-start | bytes 442376 | tf_op jit(solution)/shard_map/ppermute | solution.py:362
  81.5 2.4 %collective-permute-done.4.rest_5_ = bf16[64,1152]{1,0:T(8,128)(2,1)} collective-permute-done((bf16[64,1152]{1,0:T(8,128)(2,1)}, bf16[64,1152]{1,0:T(8,128)(2,1)}, u32[]{:S(2)}, u32[]{:S(2)}) %collective-permute-start.4) | collective-permute-done | bytes 147488 | tf_op jit(solution)/shard_map/ppermute | solution.py:362
  83.9 2.2 %collective-permute-start.5 = (bf16[64,1152]{1,0:T(8,128)(2,1)}, bf16[64,1152]{1,0:T(8,128)(2,1)}, u32[]{:S(2)}, u32[]{:S(2)}) collective-permute-start(bf16[64,1152]{1,0:T(8,128)(2,1)} %get-tuple-element.27), channel_id=1, source_target_pairs={{0,6},{1,7},{2,0},{3,1},{4,2},{5,3},{6,4},{7,5},{8,14},{9,15},{10,... | collective-permute-start | bytes 442376 | tf_op jit(solution)/shard_map/ppermute | solution.py:362
  86.7 6.1 %collective-permute-done.5.rest_6_ = bf16[64,1152]{1,0:T(8,128)(2,1)} collective-permute-done((bf16[64,1152]{1,0:T(8,128)(2,1)}, bf16[64,1152]{1,0:T(8,128)(2,1)}, u32[]{:S(2)}, u32[]{:S(2)}) %collective-permute-start.5) | collective-permute-done | bytes 147488 | tf_op jit(solution)/shard_map/ppermute | solution.py:362
  94.9 4.3 %collective-permute-done.6.rest_7_ = bf16[64,1152]{1,0:T(8,128)(2,1)S(1)} collective-permute-done((bf16[64,1152]{1,0:T(8,128)(2,1)}, bf16[64,1152]{1,0:T(8,128)(2,1)S(1)}, u32[]{:S(2)}, u32[]{:S(2)}) %collective-permute-start.6) | collective-permute-done | bytes 147488 | tf_op jit(solution)/shard_map/ppermute | solution.py:362
  99.8 43.3 %run_heads.1 = (bf16[64,384]{1,0:T(8,128)(2,1)}, bf16[64,384]{1,0:T(8,128)(2,1)}, bf16[64,384]{1,0:T(8,128)(2,1)}, bf16[64,384]{1,0:T(8,128)(2,1)}, bf16[64,384]...) custom-call(s32[2]{0:T(128)} %pad_add_fusion.me_ref.place_ref, ...), custom_call_target="tpu_custom_call" | custom-call | tf_op jit(solution)/shard_map/run_heads/pallas_call | solution.py:252
  144.8 3.1 %collective-permute-start.8 = (bf16[64,384]{1,0:T(8,128)(2,1)}, bf16[64,384]{1,0:T(8,128)(2,1)S(1)}, u32[]{:S(2)}, u32[]{:S(2)}) collective-permute-start(bf16[64,384]{1,0:T(8,128)(2,1)} %get-tuple-element.31), channel_id=1, source_target_pairs={{0,2},{1,3},{2,4},{3,5},{4,6},{5,7},{6,0},{7,1},{8,10},{9,11},{10,... | collective-permute-start | bytes 147464 | tf_op jit(solution)/shard_map/ppermute | solution.py:362
  147.9 2.8 %collective-permute-done.8.rest_2_ = bf16[64,384]{1,0:T(8,128)(2,1)S(1)} collective-permute-done((bf16[64,384]{1,0:T(8,128)(2,1)}, bf16[64,384]{1,0:T(8,128)(2,1)S(1)}, u32[]{:S(2)}, u32[]{:S(2)}) %collective-permute-start.8) | collective-permute-done | bytes 49184 | tf_op jit(solution)/shard_map/ppermute | solution.py:362
  150.7 8.3 %collective-permute-start.9 = (bf16[64,384]{1,0:T(8,128)(2,1)}, bf16[64,384]{1,0:T(8,128)(2,1)S(1)}, u32[]{:S(2)}, u32[]{:S(2)}) collective-permute-start(bf16[64,384]{1,0:T(8,128)(2,1)} %get-tuple-element.32), channel_id=1, source_target_pairs={{0,3},{1,4},{2,5},{3,6},{4,7},{5,0},{6,1},{7,2},{8,11},{9,12},{10,... | collective-permute-start | bytes 147464 | tf_op jit(solution)/shard_map/ppermute | solution.py:362
  160.5 2.2 %collective-permute-start.10 = (bf16[64,384]{1,0:T(8,128)(2,1)}, bf16[64,384]{1,0:T(8,128)(2,1)S(1)}, u32[]{:S(2)}, u32[]{:S(2)}) collective-permute-start(bf16[64,384]{1,0:T(8,128)(2,1)} %get-tuple-element.33), channel_id=1, source_target_pairs={{0,4},{1,5},{2,6},{3,7},{4,0},{5,1},{6,2},{7,3},{8,12},{9,13},{10,... | collective-permute-start | bytes 147464 | tf_op jit(solution)/shard_map/ppermute | solution.py:362
  162.7 4.9 %collective-permute-done.10.rest_4_ = bf16[64,384]{1,0:T(8,128)(2,1)S(1)} collective-permute-done((bf16[64,384]{1,0:T(8,128)(2,1)}, bf16[64,384]{1,0:T(8,128)(2,1)S(1)}, u32[]{:S(2)}, u32[]{:S(2)}) %collective-permute-start.10) | collective-permute-done | bytes 49184 | tf_op jit(solution)/shard_map/ppermute | solution.py:362
  167.5 3.7 %collective-permute-start.11 = (bf16[64,384]{1,0:T(8,128)(2,1)}, bf16[64,384]{1,0:T(8,128)(2,1)S(1)}, u32[]{:S(2)}, u32[]{:S(2)}) collective-permute-start(bf16[64,384]{1,0:T(8,128)(2,1)} %get-tuple-element.34), channel_id=1, source_target_pairs={{0,5},{1,6},{2,7},{3,0},{4,1},{5,2},{6,3},{7,4},{8,13},{9,14},{10,... | collective-permute-start | bytes 147464 | tf_op jit(solution)/shard_map/ppermute | solution.py:362
  171.2 5.6 %collective-permute-done.11.rest_5_ = bf16[64,384]{1,0:T(8,128)(2,1)S(1)} collective-permute-done((bf16[64,384]{1,0:T(8,128)(2,1)}, bf16[64,384]{1,0:T(8,128)(2,1)S(1)}, u32[]{:S(2)}, u32[]{:S(2)}) %collective-permute-start.11) | collective-permute-done | bytes 49184 | tf_op jit(solution)/shard_map/ppermute | solution.py:362
  176.8 4.8 %collective-permute-done.12.rest_6_ = bf16[64,384]{1,0:T(8,128)(2,1)S(1)} collective-permute-done((bf16[64,384]{1,0:T(8,128)(2,1)}, bf16[64,384]{1,0:T(8,128)(2,1)S(1)}, u32[]{:S(2)}, u32[]{:S(2)}) %collective-permute-start.12) | collective-permute-done | bytes 49184 | tf_op jit(solution)/shard_map/ppermute | solution.py:362
  182.1 4.1 %collective-permute-done.13.rest_7_ = bf16[64,384]{1,0:T(8,128)(2,1)S(1)} collective-permute-done((bf16[64,384]{1,0:T(8,128)(2,1)}, bf16[64,384]{1,0:T(8,128)(2,1)S(1)}, u32[]{:S(2)}, u32[]{:S(2)}) %collective-permute-start.13) | collective-permute-done | bytes 49184 | tf_op jit(solution)/shard_map/ppermute | solution.py:362
  186.8 7.6 %project_rows.1 = bf16[128,3072]{1,0:T(8,128)(2,1)} custom-call(s32[2]{0:T(128)} %pad_add_fusion.me_ref.place_ref, bf16[64,384]{1,0:T(8,128)(2,1)} %get-tuple-element.29.rest_0_, bf16[64,384]{1,0:T(8,128)(2,1)} %copy-done.5, bf16[64,384]{1,0:T(8,128)(2,1)} %copy-done.6, bf16[64,384]{1,0:T(8,128)(2,1)} %copy-done.7, bf16[64,384]{1,0:T(8,128)(2,1)} %copy-done.8, ...), custom_call_target="tpu_custom_call" | custom-call | tf_op jit(solution)/shard_map/project_rows/pallas_call | solution.py:327
  (58 shorter events, 15.4 us)
Async XLA Ops:
  0.9 5.1 %collective-permute-start.14 = (bf16[48,1536]{1,0:T(8,128)(2,1)S(1)}, bf16[48,1536]{1,0:T(8,128)(2,1)S(1)}, u32[]{:S(2)}, u32[]{:S(2)}) collective-permute-start(bf16[48,1536]{1,0:T(8,128)(2,1)S(1)} %get-tuple-element.38), channel_id=1, source_target_pairs={{0,8},{1,9},{2,10},{3,11},{4,12},{5,13},{6,14},{7,15},{8,0},{9,1},... | collective-permute-start | bytes 442376 | tf_op jit(solution)/shard_map/ppermute | solution.py:358
  6.0 8.1 %collective-permute-start.15 = (bf16[96,1536]{1,0:T(8,128)(2,1)S(1)}, bf16[96,1536]{1,0:T(8,128)(2,1)S(1)}, u32[]{:S(2)}, u32[]{:S(2)}) collective-permute-start(bf16[96,1536]{1,0:T(8,128)(2,1)S(1)} %pad_maximum_fusion), channel_id=1, source_target_pairs={{0,16},{1,65},{2,18},{3,67},{4,20},{5,69},{6,22},{7,71},{8,24},{9,... | collective-permute-start | bytes 884744 | tf_op jit(solution)/shard_map/ppermute | solution.py:358
  8.3 10.2 %collective-permute-start.17 = (bf16[96,1536]{1,0:T(8,128)(2,1)S(1)}, bf16[96,1536]{1,0:T(8,128)(2,1)S(1)}, u32[]{:S(2)}, u32[]{:S(2)}) collective-permute-start(bf16[96,1536]{1,0:T(8,128)(2,1)S(1)} %pad_maximum_fusion), channel_id=1, source_target_pairs={{0,32},{1,129},{2,34},{3,131},{4,36},{5,133},{6,38},{7,135},{8,40}... | collective-permute-start | bytes 884744 | tf_op jit(solution)/shard_map/ppermute | solution.py:358
  11.0 7.1 %collective-permute-start.16 = (bf16[96,1536]{1,0:T(8,128)(2,1)S(1)}, bf16[96,1536]{1,0:T(8,128)(2,1)S(1)}, u32[]{:S(2)}, u32[]{:S(2)}) collective-permute-start(bf16[96,1536]{1,0:T(8,128)(2,1)S(1)} %pad_maximum_fusion), channel_id=1, source_target_pairs={{0,48},{1,193},{2,50},{3,195},{4,52},{5,197},{6,54},{7,199},{8,56}... | collective-permute-start | bytes 884744 | tf_op jit(solution)/shard_map/ppermute | solution.py:358
  14.2 71.9 %copy-start.12 = (f32[1536]{0:T(1024)S(1)}, f32[1536]{0:T(1024)}, u32[]{:S(2)}) copy-start(f32[1536]{0:T(1024)} %param.16) | copy-start | bytes 18436
  14.2 79.7 %copy-start.13 = (s32[1,1024]{1,0:T(1,128)S(1)}, s32[1,1024]{1,0:T(1,128)}, u32[]{:S(2)}) copy-start(s32[1,1024]{1,0:T(1,128)} %param.12) | copy-start | bytes 12292
  18.5 124.7 %copy-start = (bf16[384,1536]{1,0:T(8,128)(2,1)}, bf16[384,1536]{1,0:T(8,128)(2,1)S(1)}, u32[]{:S(2)}) copy-start(bf16[384,1536]{1,0:T(8,128)(2,1)S(1)} %constant_dynamic-update-slice_fusion.rest_8_) | copy-start | bytes 3538948
  18.6 17.8 %collective-permute-start.20 = (bf16[384,1536]{1,0:T(8,128)(2,1)S(1)}, bf16[384,1536]{1,0:T(8,128)(2,1)S(1)}, u32[]{:S(2)}, u32[]{:S(2)}) collective-permute-start(bf16[384,1536]{1,0:T(8,128)(2,1)S(1)} %constant_dynamic-update-slice_fusion.rest_8_), channel_id=1, source_target_pairs={{0,128},{1,33},{2,130},{3,35},{4,132},{5,37},{6,134},{7,39},{8,136... | collective-permute-start | bytes 3538952 | tf_op jit(solution)/shard_map/ppermute | solution.py:358
  21.1 27.0 %collective-permute-start.19 = (bf16[384,1536]{1,0:T(8,128)(2,1)S(1)}, bf16[384,1536]{1,0:T(8,128)(2,1)S(1)}, u32[]{:S(2)}, u32[]{:S(2)}) collective-permute-start(bf16[384,1536]{1,0:T(8,128)(2,1)S(1)} %constant_dynamic-update-slice_fusion.rest_8_), channel_id=1, source_target_pairs={{0,192},{1,49},{2,194},{3,51},{4,196},{5,53},{6,198},{7,55},{8,200... | collective-permute-start | bytes 3538952 | tf_op jit(solution)/shard_map/ppermute | solution.py:358
  22.0 29.4 %collective-permute-start.18 = (bf16[384,1536]{1,0:T(8,128)(2,1)S(1)}, bf16[384,1536]{1,0:T(8,128)(2,1)}, u32[]{:S(2)}, u32[]{:S(2)}) collective-permute-start(bf16[384,1536]{1,0:T(8,128)(2,1)S(1)} %constant_dynamic-update-slice_fusion.rest_8_), channel_id=1, source_target_pairs={{0,64},{1,17},{2,66},{3,19},{4,68},{5,21},{6,70},{7,23},{8,72},{9,... | collective-permute-start | bytes 3538952 | tf_op jit(solution)/shard_map/ppermute | solution.py:358
  25.8 10.5 %collective-permute-start = (bf16[64,1152]{1,0:T(8,128)(2,1)}, bf16[64,1152]{1,0:T(8,128)(2,1)S(1)}, u32[]{:S(2)}, u32[]{:S(2)}) collective-permute-start(bf16[64,1152]{1,0:T(8,128)(2,1)} %get-tuple-element.22), channel_id=1, source_target_pairs={{0,1},{1,2},{2,3},{3,4},{4,5},{5,6},{6,7},{7,0},{8,9},{9,10},{10,1... | collective-permute-start | bytes 442376 | tf_op jit(solution)/shard_map/ppermute | solution.py:362
  32.0 20.1 %collective-permute-start.1 = (bf16[64,1152]{1,0:T(8,128)(2,1)}, bf16[64,1152]{1,0:T(8,128)(2,1)}, u32[]{:S(2)}, u32[]{:S(2)}) collective-permute-start(bf16[64,1152]{1,0:T(8,128)(2,1)} %get-tuple-element.23), channel_id=1, source_target_pairs={{0,2},{1,3},{2,4},{3,5},{4,6},{5,7},{6,0},{7,1},{8,10},{9,11},{10,... | collective-permute-start | bytes 442376 | tf_op jit(solution)/shard_map/ppermute | solution.py:362
  36.3 149.9 %collective-permute-start.21 = (bf16[384,1536]{1,0:T(8,128)(2,1)S(1)}, bf16[384,1536]{1,0:T(8,128)(2,1)}, u32[]{:S(2)}, u32[]{:S(2)}) collective-permute-start(bf16[384,1536]{1,0:T(8,128)(2,1)S(1)} %constant_dynamic-update-slice_fusion.rest_8_), channel_id=1, source_target_pairs={{0,1},{1,0},{2,3},{3,2},{4,5},{5,4},{6,7},{7,6},{8,9},{9,8},{10,11... | collective-permute-start | bytes 3538952 | tf_op jit(solution)/shard_map/ppermute | solution.py:358
  36.3 106.9 %copy-start.1 = (bf16[384,1536]{1,0:T(8,128)(2,1)}, bf16[384,1536]{1,0:T(8,128)(2,1)S(1)}, u32[]{:S(2)}) copy-start(bf16[384,1536]{1,0:T(8,128)(2,1)S(1)} %collective-permute-done.20.rest_11_) | copy-start | bytes 3538948
  36.3 149.9 %collective-permute-start.24 = (bf16[384,1536]{1,0:T(8,128)(2,1)S(1)}, bf16[384,1536]{1,0:T(8,128)(2,1)}, u32[]{:S(2)}, u32[]{:S(2)}) collective-permute-start(bf16[384,1536]{1,0:T(8,128)(2,1)S(1)} %collective-permute-done.20.rest_11_), channel_id=1, source_target_pairs={{0,1},{1,0},{2,3},{3,2},{4,5},{5,4},{6,7},{7,6},{8,9},{9,8},{10,11... | collective-permute-start | bytes 3538952 | tf_op jit(solution)/shard_map/ppermute | solution.py:358
  48.1 95.1 %copy-start.2 = (bf16[384,1536]{1,0:T(8,128)(2,1)}, bf16[384,1536]{1,0:T(8,128)(2,1)S(1)}, u32[]{:S(2)}) copy-start(bf16[384,1536]{1,0:T(8,128)(2,1)S(1)} %collective-permute-done.19.rest_10_) | copy-start | bytes 3538948
  48.1 138.1 %collective-permute-start.23 = (bf16[384,1536]{1,0:T(8,128)(2,1)S(1)}, bf16[384,1536]{1,0:T(8,128)(2,1)}, u32[]{:S(2)}, u32[]{:S(2)}) collective-permute-start(bf16[384,1536]{1,0:T(8,128)(2,1)S(1)} %collective-permute-done.19.rest_10_), channel_id=1, source_target_pairs={{0,1},{1,0},{2,3},{3,2},{4,5},{5,4},{6,7},{7,6},{8,9},{9,8},{10,11... | collective-permute-start | bytes 3538952 | tf_op jit(solution)/shard_map/ppermute | solution.py:358
  51.3 134.9 %collective-permute-start.22 = (bf16[384,1536]{1,0:T(8,128)(2,1)}, bf16[384,1536]{1,0:T(8,128)(2,1)}, u32[]{:S(2)}, u32[]{:S(2)}) collective-permute-start(bf16[384,1536]{1,0:T(8,128)(2,1)} %collective-permute-done.18.rest_9_), channel_id=1, source_target_pairs={{0,1},{1,0},{2,3},{3,2},{4,5},{5,4},{6,7},{7,6},{8,9},{9,8},{10,11... | collective-permute-start | bytes 3538952 | tf_op jit(solution)/shard_map/ppermute | solution.py:358
  52.1 13.2 %collective-permute-start.2 = (bf16[64,1152]{1,0:T(8,128)(2,1)}, bf16[64,1152]{1,0:T(8,128)(2,1)}, u32[]{:S(2)}, u32[]{:S(2)}) collective-permute-start(bf16[64,1152]{1,0:T(8,128)(2,1)} %get-tuple-element.24), channel_id=1, source_target_pairs={{0,3},{1,4},{2,5},{3,6},{4,7},{5,0},{6,1},{7,2},{8,11},{9,12},{10,... | collective-permute-start | bytes 442376 | tf_op jit(solution)/shard_map/ppermute | solution.py:362
  65.4 9.3 %collective-permute-start.3 = (bf16[64,1152]{1,0:T(8,128)(2,1)}, bf16[64,1152]{1,0:T(8,128)(2,1)}, u32[]{:S(2)}, u32[]{:S(2)}) collective-permute-start(bf16[64,1152]{1,0:T(8,128)(2,1)} %get-tuple-element.25), channel_id=1, source_target_pairs={{0,4},{1,5},{2,6},{3,7},{4,0},{5,1},{6,2},{7,3},{8,12},{9,13},{10,... | collective-permute-start | bytes 442376 | tf_op jit(solution)/shard_map/ppermute | solution.py:362
  74.7 9.2 %collective-permute-start.4 = (bf16[64,1152]{1,0:T(8,128)(2,1)}, bf16[64,1152]{1,0:T(8,128)(2,1)}, u32[]{:S(2)}, u32[]{:S(2)}) collective-permute-start(bf16[64,1152]{1,0:T(8,128)(2,1)} %get-tuple-element.26), channel_id=1, source_target_pairs={{0,5},{1,6},{2,7},{3,0},{4,1},{5,2},{6,3},{7,4},{8,13},{9,14},{10,... | collective-permute-start | bytes 442376 | tf_op jit(solution)/shard_map/ppermute | solution.py:362
  83.9 8.9 %collective-permute-start.5 = (bf16[64,1152]{1,0:T(8,128)(2,1)}, bf16[64,1152]{1,0:T(8,128)(2,1)}, u32[]{:S(2)}, u32[]{:S(2)}) collective-permute-start(bf16[64,1152]{1,0:T(8,128)(2,1)} %get-tuple-element.27), channel_id=1, source_target_pairs={{0,6},{1,7},{2,0},{3,1},{4,2},{5,3},{6,4},{7,5},{8,14},{9,15},{10,... | collective-permute-start | bytes 442376 | tf_op jit(solution)/shard_map/ppermute | solution.py:362
  92.8 6.3 %collective-permute-start.6 = (bf16[64,1152]{1,0:T(8,128)(2,1)}, bf16[64,1152]{1,0:T(8,128)(2,1)S(1)}, u32[]{:S(2)}, u32[]{:S(2)}) collective-permute-start(bf16[64,1152]{1,0:T(8,128)(2,1)} %get-tuple-element.28), channel_id=1, source_target_pairs={{0,7},{1,0},{2,1},{3,2},{4,3},{5,4},{6,5},{7,6},{8,15},{9,8},{10,9... | collective-permute-start | bytes 442376 | tf_op jit(solution)/shard_map/ppermute | solution.py:362
  143.2 1.6 collective-permute-start.7
  144.8 41.4 %copy-start.5 = (bf16[64,384]{1,0:T(8,128)(2,1)}, bf16[64,384]{1,0:T(8,128)(2,1)S(1)}, u32[]{:S(2)}) copy-start(bf16[64,384]{1,0:T(8,128)(2,1)S(1)} %collective-permute-done.7.rest_1_) | copy-start | bytes 147460
  144.8 5.9 %collective-permute-start.8 = (bf16[64,384]{1,0:T(8,128)(2,1)}, bf16[64,384]{1,0:T(8,128)(2,1)S(1)}, u32[]{:S(2)}, u32[]{:S(2)}) collective-permute-start(bf16[64,384]{1,0:T(8,128)(2,1)} %get-tuple-element.31), channel_id=1, source_target_pairs={{0,2},{1,3},{2,4},{3,5},{4,6},{5,7},{6,0},{7,1},{8,10},{9,11},{10,... | collective-permute-start | bytes 147464 | tf_op jit(solution)/shard_map/ppermute | solution.py:362
  150.7 35.6 %copy-start.6 = (bf16[64,384]{1,0:T(8,128)(2,1)}, bf16[64,384]{1,0:T(8,128)(2,1)S(1)}, u32[]{:S(2)}) copy-start(bf16[64,384]{1,0:T(8,128)(2,1)S(1)} %collective-permute-done.8.rest_2_) | copy-start | bytes 147460
  150.7 9.8 %collective-permute-start.9 = (bf16[64,384]{1,0:T(8,128)(2,1)}, bf16[64,384]{1,0:T(8,128)(2,1)S(1)}, u32[]{:S(2)}, u32[]{:S(2)}) collective-permute-start(bf16[64,384]{1,0:T(8,128)(2,1)} %get-tuple-element.32), channel_id=1, source_target_pairs={{0,3},{1,4},{2,5},{3,6},{4,7},{5,0},{6,1},{7,2},{8,11},{9,12},{10,... | collective-permute-start | bytes 147464 | tf_op jit(solution)/shard_map/ppermute | solution.py:362
  160.5 7.1 %collective-permute-start.10 = (bf16[64,384]{1,0:T(8,128)(2,1)}, bf16[64,384]{1,0:T(8,128)(2,1)S(1)}, u32[]{:S(2)}, u32[]{:S(2)}) collective-permute-start(bf16[64,384]{1,0:T(8,128)(2,1)} %get-tuple-element.33), channel_id=1, source_target_pairs={{0,4},{1,5},{2,6},{3,7},{4,0},{5,1},{6,2},{7,3},{8,12},{9,13},{10,... | collective-permute-start | bytes 147464 | tf_op jit(solution)/shard_map/ppermute | solution.py:362
  167.5 9.3 %collective-permute-start.11 = (bf16[64,384]{1,0:T(8,128)(2,1)}, bf16[64,384]{1,0:T(8,128)(2,1)S(1)}, u32[]{:S(2)}, u32[]{:S(2)}) collective-permute-start(bf16[64,384]{1,0:T(8,128)(2,1)} %get-tuple-element.34), channel_id=1, source_target_pairs={{0,5},{1,6},{2,7},{3,0},{4,1},{5,2},{6,3},{7,4},{8,13},{9,14},{10,... | collective-permute-start | bytes 147464 | tf_op jit(solution)/shard_map/ppermute | solution.py:362
  176.8 4.8 %collective-permute-start.12 = (bf16[64,384]{1,0:T(8,128)(2,1)}, bf16[64,384]{1,0:T(8,128)(2,1)S(1)}, u32[]{:S(2)}, u32[]{:S(2)}) collective-permute-start(bf16[64,384]{1,0:T(8,128)(2,1)} %get-tuple-element.35), channel_id=1, source_target_pairs={{0,6},{1,7},{2,0},{3,1},{4,2},{5,3},{6,4},{7,5},{8,14},{9,15},{10,... | collective-permute-start | bytes 147464 | tf_op jit(solution)/shard_map/ppermute | solution.py:362
  181.6 4.6 %collective-permute-start.13 = (bf16[64,384]{1,0:T(8,128)(2,1)}, bf16[64,384]{1,0:T(8,128)(2,1)S(1)}, u32[]{:S(2)}, u32[]{:S(2)}) collective-permute-start(bf16[64,384]{1,0:T(8,128)(2,1)} %get-tuple-element.36), channel_id=1, source_target_pairs={{0,7},{1,0},{2,1},{3,2},{4,3},{5,4},{6,5},{7,6},{8,15},{9,8},{10,9... | collective-permute-start | bytes 147464 | tf_op jit(solution)/shard_map/ppermute | solution.py:362
  (7 other events, 75.0 us)

commit v2 on v1

v2 whole, which is shorter than its diff:
```python
import functools
import math

import jax
import jax.numpy as jnp
from jax import lax
from jax.experimental import pallas as pl
from jax.experimental.pallas import tpu as pltpu
from jax.sharding import PartitionSpec as P

HD = 64
FFI = 256
CH = 64
LOCAL = 3
PARTS = 8
TOK = 128
LEN = 1024
HH = 1536
WIDTH = LOCAL * HD
SAME = 32.0
EPS = 1e-6
GA = math.sqrt(2.0 / math.pi)
GB = GA * 0.044715
VMEM_MOST = 56 * 1024 * 1024

f32 = jnp.float32
bf16 = jnp.bfloat16


def dot(left, right):
    return jnp.dot(left, right, preferred_element_type=f32)


def dot_nt(left, right):
    return lax.dot_general(left, right, (((1,), (1,)), ((), ())), preferred_element_type=f32)


def dot_tn(left, right):
    return lax.dot_general(left, right, (((0,), (0,)), ((), ())), preferred_element_type=f32)


def lane_mean(value):
    return jnp.mean(value, axis=-1, keepdims=True)


MOVES = ((2, 0), (1, 0), (3, 0), (2, 1), (1, 1), (3, 1), (0, 1))


def target_of(me, step):
    chips, swap = MOVES[step - 1] if step else (0, 0)
    core = lax.rem(me, 2)
    return lax.rem(me // 2 + chips, 4) * 2 + (1 - core if swap else core)


def source_of(me, step):
    chips, swap = MOVES[step - 1] if step else (0, 0)
    core = lax.rem(me, 2)
    return lax.rem(me // 2 + 4 - chips, 4) * 2 + (1 - core if swap else core)


def pack_kernel(q_ref, k_ref, v_ref, out):
    for part in range(PARTS):
        cols = slice(part * WIDTH, (part + 1) * WIDTH)
        for group, ref in enumerate((q_ref, k_ref, v_ref)):
            for half in range(2):
                at = (2 * group + half) * WIDTH
                out[part, :, at : at + WIDTH] = ref[half * CH : (half + 1) * CH, cols]


def pack(queries, keys, values):
    return pl.pallas_call(
        pack_kernel,
        out_shape=jax.ShapeDtypeStruct((PARTS, CH, 6 * WIDTH), bf16),
        compiler_params=pltpu.CompilerParams(vmem_limit_bytes=VMEM_MOST),
        name="pack_rows",
    )(queries, keys, values)


def gelu_parts(z, slope):
    square = z * z
    half = 0.5 * jnp.tanh(z * (GB * square + GA)) + 0.5
    act = z * half
    if not slope:
        return act, None
    return act, half + (act - act * half) * (6.0 * GB * square + 2.0 * GA)


def cutter(x):
    def cut(group, head, source, half):
        at = (2 * group + half) * WIDTH + head * HD
        return x[source, :, at : at + HD]

    return cut


def inner_kernel(
    me_ref, rate_ref, x_ref, first_ref, second_ref, inner,
    x, w1, w2, w1s, w2s, b1s, b2s, z1s, q1s, a_prev, g2_prev, b2_prev, xq_prev, sems, wsems,
):
    me = me_ref[0]
    copies = [pltpu.make_async_copy(x_ref, x, sems.at[0])]
    weights = [
        pltpu.make_async_copy(first_ref.at[pl.ds(me * LOCAL, LOCAL)], w1, wsems.at[0]),
        pltpu.make_async_copy(second_ref.at[pl.ds(me * LOCAL, LOCAL)], w2, wsems.at[1]),
    ]
    for copy in copies + weights:
        copy.start()
    for copy in copies + weights:
        copy.wait()
    cut = cutter(x)

    causal = lax.broadcasted_iota(jnp.int32, (CH, CH), 0) >= lax.broadcasted_iota(jnp.int32, (CH, CH), 1)

    def rms(value):
        return lax.rsqrt(lane_mean(value * value) + EPS)

    def stacked(head, q_source, q_half, k_source, k_half):
        q = cut(0, head, q_source, q_half)
        k = cut(1, head, k_source, k_half)
        rows = jnp.concatenate([q, k], axis=0)
        wide = rows.astype(f32)
        scale = rms(wide)
        return rows, wide * scale, scale

    def project(state, bias, rows, scale):
        high = state.astype(bf16)
        low = (state - high.astype(f32)).astype(bf16)
        both = dot(jnp.concatenate([rows, rows], axis=1), jnp.concatenate([high, low], axis=0))
        return both * scale + bias

    for head in range(LOCAL):
        w1s[head] = w1[head].astype(f32)
        start = w2[head].astype(f32)
        w2s[head] = start - jnp.mean(start, axis=0, keepdims=True)
        b1s[head] = jnp.zeros((1, FFI), f32)
        b2s[head] = jnp.zeros((1, HD), f32)
        b2_prev[head] = jnp.zeros((1, HD), f32)
        k = cut(1, head, 0, 0)
        z1s[head] = project(w1s[head], b1s[head], k, rms(k.astype(f32)))
        q1s[head] = jnp.zeros((CH, FFI), f32)
        a_prev[head] = jnp.zeros((CH + HD, FFI), bf16)
        g2_prev[head] = jnp.zeros((CH, HD), bf16)
        xq_prev[head] = jnp.zeros((CH, HD), f32)

    heads = range(LOCAL)
    etas = [rate_ref[me * LOCAL + head] * (1.0 / HD) for head in heads]

    def query_first():
        held = [(q1s[h], a_prev[h], g2_prev[h], b2_prev[h], xq_prev[h]) for h in heads]
        acts = [gelu_parts(held[h][0], False)[0] for h in heads]
        highs = [act.astype(bf16) for act in acts]
        lows = [(act - high.astype(f32)).astype(bf16) for act, high in zip(acts, highs)]
        boths = [dot_nt(highs[h], held[h][1]) for h in heads]
        rests = [dot_nt(lows[h], held[h][1][CH:]) for h in heads]
        return held, boths, rests

    def query_last(state):
        held, boths, rests = state
        seconds = [jnp.where(causal, both[:, :CH] + 1.0, 0.0).astype(bf16) for both in boths]
        outs = [boths[h][:, CH:] + rests[h] + held[h][3] - dot(seconds[h], held[h][2]) for h in heads]
        scales = [lax.rsqrt(lane_mean(out * out) + EPS) for out in outs]
        return [held[h][4] + outs[h] * scales[h] for h in heads]

    def one_block(source, half, next_source, next_half):
        z1 = [z1s[h] for h in heads]
        w2 = [w2s[h] for h in heads]
        b2 = [b2s[h] for h in heads]
        w1 = [w1s[h] for h in heads]
        b1 = [b1s[h] for h in heads]
        query = query_first()

        keys, targets, ahead, cross, normed_q = [], [], [], [], []
        for h in heads:
            k = cut(1, h, source, half).astype(f32)
            key = k * rms(k)
            target = cut(2, h, source, half).astype(f32) - key
            targets.append(target - lane_mean(target))
            keys.append(key.astype(bf16))
            rows, normed, scale = stacked(h, source, half, next_source, next_half)
            ahead.append(project(w1[h], b1[h], rows, scale))
            pair = dot_nt(normed.astype(bf16), keys[h]) + 1.0
            cross.append(jnp.concatenate([jnp.where(causal, pair[:CH], 0.0), pair[CH:]], axis=0).astype(bf16))
            normed_q.append(normed[:CH])

        parts = [gelu_parts(z, True) for z in z1]
        acts = [act.astype(bf16) for act, _ in parts]
        w2_low = [w.astype(bf16) for w in w2]
        cs = [dot_nt(acts[h], w2_low[h]) + b2[h] for h in heads]
        squares = [lane_mean(c * c) for c in cs]
        mixes = [lane_mean(c * target) for c, target in zip(cs, targets)]
        grads = []
        for h in heads:
            r = lax.rsqrt(squares[h] + EPS)
            grads.append((etas[h] * r) * (cs[h] * (r * (EPS * r * r + mixes[h] * r)) - targets[h]))
        grad_low = [grad.astype(bf16) for grad in grads]
        deeps = [dot(grad_low[h], w2_low[h]) * parts[h][1] for h in heads]
        deep_low = [deep.astype(bf16) for deep in deeps]
        boths = [ahead[h] - dot(cross[h], deep_low[h]) for h in heads]
        new_w2 = [w2[h] - dot_tn(grad_low[h], acts[h]) for h in heads]
        new_b2 = [b2[h] - jnp.sum(grads[h], axis=0, keepdims=True) for h in heads]
        new_w1 = [w1[h] - dot_tn(keys[h], deep_low[h]) for h in heads]
        new_b1 = [b1[h] - jnp.sum(deeps[h], axis=0, keepdims=True) for h in heads]
        done = query_last(query)

        for h in heads:
            z1s[h] = boths[h][CH:]
            q1s[h] = boths[h][:CH]
            a_prev[h, :CH, :] = acts[h]
            a_prev[h, CH:, :] = w2_low[h]
            g2_prev[h] = grad_low[h]
            b2_prev[h] = b2[h]
            xq_prev[h] = normed_q[h]
            w1s[h] = new_w1[h]
            b1s[h] = new_b1[h]
            w2s[h] = new_w2[h]
            b2s[h] = new_b2[h]
        return done

    def blocks(source, carry):
        done = one_block(source, 0, source, 1)
        for h in heads:
            inner[jnp.maximum(source - 1, 0), :, WIDTH + h * HD : WIDTH + (h + 1) * HD] = done[h]
        done = one_block(source, 1, jnp.minimum(source + 1, PARTS - 1), 0)
        for h in heads:
            inner[source, :, h * HD : (h + 1) * HD] = done[h]
        return carry

    lax.fori_loop(0, PARTS, blocks, 0)
    done = query_last(query_first())
    for h in heads:
        inner[PARTS - 1, :, WIDTH + h * HD : WIDTH + (h + 1) * HD] = done[h]


VMEM = pl.BlockSpec(memory_space=pltpu.VMEM)
SMEM = pl.BlockSpec(memory_space=pltpu.SMEM)
HBM = pl.BlockSpec(memory_space=pl.ANY)


def run_inner(me, rate, pieces, first, second):
    return pl.pallas_call(
        inner_kernel,
        out_shape=jax.ShapeDtypeStruct((PARTS, CH, 2 * WIDTH), f32),
        in_specs=[SMEM, SMEM, HBM, HBM, HBM],
        out_specs=VMEM,
        scratch_shapes=[
            pltpu.VMEM((PARTS, CH, 6 * WIDTH), bf16),
            pltpu.VMEM((LOCAL, HD, FFI), bf16),
            pltpu.VMEM((LOCAL, HD, FFI), bf16),
            pltpu.VMEM((LOCAL, HD, FFI), f32),
            pltpu.VMEM((LOCAL, HD, FFI), f32),
            pltpu.VMEM((LOCAL, 1, FFI), f32),
            pltpu.VMEM((LOCAL, 1, HD), f32),
            pltpu.VMEM((LOCAL, CH, FFI), f32),
            pltpu.VMEM((LOCAL, CH, FFI), f32),
            pltpu.VMEM((LOCAL, CH + HD, FFI), bf16),
            pltpu.VMEM((LOCAL, CH, HD), bf16),
            pltpu.VMEM((LOCAL, 1, HD), f32),
            pltpu.VMEM((LOCAL, CH, HD), f32),
            pltpu.SemaphoreType.DMA((1,)),
            pltpu.SemaphoreType.DMA((2,)),
        ],
        compiler_params=pltpu.CompilerParams(vmem_limit_bytes=VMEM_MOST),
        cost_estimate=pl.CostEstimate(flops=4_000_000_000, bytes_accessed=100_000_000, transcendentals=0),
        name="run_inner",
    )(me, rate, pieces, first, second)


def attend_kernel(steps, me_ref, *rest):
    count = len(steps)
    x_ref, seg_ref, gate_ref, inner_ref = rest[:4]
    outs = rest[4 : 4 + count]
    x, inner, k_aug, v_aug, mixed, sems, isems = rest[4 + count :]
    me = me_ref[0]
    targets = [target_of(me, step) for step in steps]
    copies = [pltpu.make_async_copy(x_ref, x, sems.at[0])] + [
        pltpu.make_async_copy(inner_ref.at[target], inner.at[i], isems.at[i]) for i, target in enumerate(targets)
    ]
    for copy in copies:
        copy.start()
    for copy in copies:
        copy.wait()
    cut = cutter(x)
    ones = jnp.ones((CH, HD), bf16)

    def prepare(source, carry):
        for half in range(2):
            rows = pl.ds(pl.multiple_of(source * TOK + half * CH, CH), CH)
            for head in range(LOCAL):
                k_aug[head, rows, :] = jnp.concatenate([cut(1, head, source, half), seg_ref[rows, :]], axis=1)
                v_aug[head, rows, :] = jnp.concatenate([cut(2, head, source, half), ones], axis=1)
        return carry

    lax.fori_loop(0, PARTS, prepare, 0)
    gates = [jnp.tanh(gate_ref[me * LOCAL + head]) for head in range(LOCAL)]
    for i, target in enumerate(targets):
        seg = seg_ref[pl.ds(pl.multiple_of(target * TOK, TOK), TOK), :]
        for head in range(LOCAL):
            q = jnp.concatenate([cut(0, head, target, half) for half in range(2)], axis=0)
            q = jnp.concatenate([(q * 0.125).astype(bf16), seg], axis=1)
            scores = dot_nt(q, k_aug[head])
            top = jnp.max(scores, axis=-1, keepdims=True)
            got = dot(jnp.exp(scores - top).astype(bf16), v_aug[head])
            got = got[:, :HD] / got[:, HD:]
            for half in range(2):
                at = slice(half * WIDTH + head * HD, half * WIDTH + (head + 1) * HD)
                part = got[half * CH : (half + 1) * CH] + gates[head] * inner[i, :, at]
                mixed[i, :, at] = part.astype(bf16)
    copies = [pltpu.make_async_copy(mixed.at[i], outs[i], isems.at[i]) for i in range(count)]
    for copy in copies:
        copy.start()
    for copy in copies:
        copy.wait()


def run_attend(steps, me, pieces, seg, gate, inner):
    count = len(steps)
    return pl.pallas_call(
        functools.partial(attend_kernel, steps),
        out_shape=[jax.ShapeDtypeStruct((CH, 2 * WIDTH), bf16)] * count,
        in_specs=[SMEM, HBM, VMEM, VMEM, HBM],
        out_specs=[HBM] * count,
        scratch_shapes=[
            pltpu.VMEM((PARTS, CH, 6 * WIDTH), bf16),
            pltpu.VMEM((count, CH, 2 * WIDTH), f32),
            pltpu.VMEM((LOCAL, LEN, 2 * HD), bf16),
            pltpu.VMEM((LOCAL, LEN, 2 * HD), bf16),
            pltpu.VMEM((count, CH, 2 * WIDTH), bf16),
            pltpu.SemaphoreType.DMA((1,)),
            pltpu.SemaphoreType.DMA((count,)),
        ],
        compiler_params=pltpu.CompilerParams(vmem_limit_bytes=VMEM_MOST),
        cost_estimate=pl.CostEstimate(flops=100_000_000 * count, bytes_accessed=2_500_000 * count, transcendentals=0),
        name="run_attend",
    )(me, pieces, seg, gate, inner)


def project_kernel(place_ref, *rest):
    mixed = rest[:PARTS]
    own, sib = rest[PARTS : PARTS + 4], rest[PARTS + 4 : PARTS + 8]
    out, held, weight, sems, wsems = rest[PARTS + 8 :]
    me, dp = place_ref[0], place_ref[1]
    core = lax.rem(me, 2)
    y, x = dp // 8, lax.rem(dp // 2, 4)
    wide = weight.shape[2]
    loads = []
    for side, blocks in enumerate((own, sib)):
        axis = core if side == 0 else 1 - core
        for i, far in enumerate(STEPS):
            for j, near in enumerate(STEPS):
                dx = jnp.where(axis == 0, near, far)
                dy = jnp.where(axis == 0, far, near)
                line = lax.rem(y + 4 - dy, 4) * 4 + lax.rem(x + 4 - dx, 4)
                loads.append(
                    pltpu.make_async_copy(
                        blocks[i].at[pl.ds(j * 2 * ROWS, 2 * ROWS)],
                        weight.at[side, pl.ds(pl.multiple_of(line * 2 * ROWS, 2 * ROWS), 2 * ROWS)],
                        wsems.at[side, 4 * i + j],
                    )
                )
    copies = [
        pltpu.make_async_copy(mixed[step], held.at[source_of(me, step)], sems.at[step]) for step in range(PARTS)
    ]
    for copy in copies + loads:
        copy.start()
    for copy in copies:
        copy.wait()
    rows = [
        jnp.concatenate([held[part, :, half * WIDTH : (half + 1) * WIDTH] for part in range(PARTS)], axis=1)
        for half in range(2)
    ]
    rows = jnp.concatenate(rows, axis=0)
    for side in range(2):
        for copy in loads[16 * side : 16 * side + 16]:
            copy.wait()
        axis = core if side == 0 else 1 - core
        for at in range(0, wide, 256):
            to = pl.multiple_of(axis * wide + at, 256)
            out[:, pl.ds(to, 256)] = dot(rows, weight[side, :, at : at + 256]).astype(bf16)


def run_project(place, mixed, own, sib):
    hbm = pl.BlockSpec(memory_space=pl.ANY)
    wide = own[0].shape[1]
    return pl.pallas_call(
        project_kernel,
        out_shape=jax.ShapeDtypeStruct((TOK, 2 * wide), bf16),
        in_specs=[pl.BlockSpec(memory_space=pltpu.SMEM)] + [hbm] * (PARTS + 8),
        out_specs=pl.BlockSpec(memory_space=pltpu.VMEM),
        scratch_shapes=[
            pltpu.VMEM((PARTS, CH, 2 * WIDTH), bf16),
            pltpu.VMEM((2, HH, wide), bf16),
            pltpu.SemaphoreType.DMA((PARTS,)),
            pltpu.SemaphoreType.DMA((2, 16)),
        ],
        compiler_params=pltpu.CompilerParams(vmem_limit_bytes=VMEM_MOST),
        name="project_rows",
    )(place, *mixed, *own, *sib)


ROWS = HH // 32
STEPS = (0, 1, 3, 2)


def where_is(index):
    dp, seq = divmod(index, PARTS)
    return dp // 8, (dp // 2) % 4, dp % 2, seq // 2, seq % 2


def index_of(y, x, z, group, core):
    return ((y % 4) * 8 + (x % 4) * 2 + z % 2) * PARTS + (group % 4) * 2 + core % 2


def move(array, place):
    pairs = [(i, index_of(*place(*where_is(i)))) for i in range(32 * PARTS)]
    return lax.ppermute(array, ("dp", "seq"), pairs)


def turn(array, step):
    return lax.ppermute(array, "seq", [(i, (i + step) % PARTS) for i in range(PARTS)])


def near_axis(step):
    return lambda y, x, z, group, core: (y + step * core, x + step * (1 - core), z, group, core)


def far_axis(step):
    return lambda y, x, z, group, core: (y + step * (1 - core), x + step * core, z, group, core)


def flip_z(y, x, z, group, core):
    return y, x, 1 - z, group, core


def flip_core(y, x, z, group, core):
    return y, x, z, group, 1 - core


GROUPS = ((1, 2, 3, 4, 5, 6, 7), (0,))


def after(value, *first):
    return lax.optimization_barrier((value, *first))[0]


def other_chip(step, swap):
    return lambda y, x, z, group, core: (y, x, z, group + step, (core + swap) % 2)


def on_device(
    queries, key_states, value_states, segment_ids, inner_first, inner_second, inner_rate, branch_gate, out_weight
):
    seq, dp = lax.axis_index("seq"), lax.axis_index("dp")
    place = jnp.stack([seq, dp]).astype(jnp.int32)
    wide = out_weight.shape[1] // 2
    slab = lax.dynamic_slice_in_dim(out_weight, (seq % 2) * wide, wide, 1)
    other = move(slab, flip_z)
    upper = dp % 2 == 1
    slab = jnp.concatenate([jnp.where(upper, other, slab), jnp.where(upper, slab, other)], axis=0)

    pieces = pack(queries[0], key_states[0], value_states[0])
    pieces = lax.all_to_all(pieces, "seq", split_axis=0, concat_axis=0, tiled=True)
    near = [move(slab, near_axis(step)) for step in STEPS[1:]]
    slab = jnp.concatenate([slab] + near, axis=0)
    own = [slab] + [move(slab, far_axis(step)) for step in STEPS[1:]]
    sib = [move(slab, flip_core)]

    seg = jnp.where(segment_ids[0][:, None] == jnp.arange(HD)[None, :], SAME, 0.0).astype(bf16)
    gate = branch_gate.reshape(-1, 1, HD)
    pieces, slab, seg, gate = lax.optimization_barrier((pieces, slab, seg, gate))
    inner = run_inner(place, inner_rate, pieces, inner_first, inner_second)
    inner, *own = lax.optimization_barrier((inner, *own))
    sib += [move(block, flip_core) for block in own[1:]]
    mixed = [None] * PARTS
    for turn, steps in enumerate(GROUPS):
        group = run_attend(steps, place, pieces, seg, gate, inner)
        if turn == 0:
            group, sib, inner = lax.optimization_barrier((group, sib, inner))
        for step, piece in zip(steps, group):
            mixed[step] = move(piece, other_chip(*MOVES[step - 1])) if step else piece
    return run_project(place, mixed, own, sib)[None]


def solution(mesh):
    in_specs = (
        P("dp", "seq", None),
        P("dp", "seq", None),
        P("dp", "seq", None),
        P("dp", None),
        P(),
        P(),
        P(),
        P(),
        P("dp", None),
    )
    return jax.shard_map(
        on_device, mesh=mesh, in_specs=in_specs, out_specs=P("dp", "seq", None), check_vma=False
    )
```

time: 195 us -> 117 us (0.60)
  waiting for transfers between devices: 67.9 us -> 14.1 us
  starting transfers between devices: 68.3 us -> 41 us
  Pallas kernels: 53.5 us -> 55.8 us
    ppermute x14 -> x0, waiting for transfers between devices: 50.4 us -> none  [turn(): lax.ppermute(array, 'seq', [(i, (i + step) % PARTS) for i in range(PARTS)])]
    ppermute x14 -> x0, starting transfers between devices: 48.6 us -> none  [turn(): lax.ppermute(array, 'seq', [(i, (i + step) % PARTS) for i in range(PARTS)])]
    ppermute x11 -> x18, starting transfers between devices: 19.7 us -> 32.3 us  [move(): return lax.ppermute(array, ('dp', 'seq'), pairs)]
    ppermute x11 -> x18, waiting for transfers between devices: 17.6 us -> 7.09 us  [move(): return lax.ppermute(array, ('dp', 'seq'), pairs)]
    all_to_all x0 -> x1, starting transfers between devices: none -> 8.65 us  [on_device(): lax.all_to_all(pieces, 'seq', split_axis=0, concat_axis=0, tiled=True)]
    all_to_all x0 -> x1, waiting for transfers between devices: none -> 7.06 us  [on_device(): lax.all_to_all(pieces, 'seq', split_axis=0, concat_axis=0, tiled=True)]
    pallas_call x2 -> x4, Pallas kernels: 45.9 us -> 48.6 us  [the longest x1 27.9 us: run_inner(): pl.pallas_call(inner_kernel, out_shape=jax.ShapeDtypeStruct((PARTS, CH, 2...]
  transfers between devices with their start and end apart: 25 -> 19, of which waited for: 18 -> 4; matrix products, arithmetic and copies ran while one was open for 1% -> 2% of each run, Pallas kernels for 24% -> 42%
where the time goes in v2:
time: 117 us
  Pallas kernels  55.8 us (48%)
  starting transfers between devices  41 us (35%)
  waiting for transfers between devices  14.1 us (12%)
  local copies, waits for them, and re-layouts  3.89 us (3%)
  other arithmetic  1.68 us (1%)
    ppermute x18, starting transfers between devices, move(): return lax.ppermute(array, ('dp', 'seq'), pairs)  32.3 us
    pallas_call x1, Pallas kernels, run_inner(): pl.pallas_call(inner_kernel, out_shape=jax.ShapeDtypeStruct((PARTS, CH, 2...  27.9 us
    pallas_call x2, Pallas kernels, run_attend(): pl.pallas_call(functools.partial(attend_kernel, steps), out_shape=[jax.Sh...  18.1 us
    all_to_all x1, starting transfers between devices, on_device(): lax.all_to_all(pieces, 'seq', split_axis=0, concat_axis=0, tiled=True)  8.65 us
    pallas_call x1, Pallas kernels, run_project(): pl.pallas_call(project_kernel, out_shape=jax.ShapeDtypeStruct((TOK, 2 * w...  7.2 us
    ppermute x18, waiting for transfers between devices, move(): return lax.ppermute(array, ('dp', 'seq'), pairs)  7.09 us
    all_to_all x1, waiting for transfers between devices, on_device(): lax.all_to_all(pieces, 'seq', split_axis=0, concat_axis=0, tiled=True)  7.06 us
    pallas_call x1, Pallas kernels, pack(): pl.pallas_call(pack_kernel, out_shape=jax.ShapeDtypeStruct((PARTS, CH, 6...  2.56 us
  transfers between devices with their start and end apart: 19, of which 4 were waited for; matrix products, arithmetic and copies ran while one was open for 2% of the time, Pallas kernels for 42%

profile of v2, /device:TPU:1, one launch (start us, length us, event | category | flops | bytes accessed | tf_op | source)
XLA Modules:
  0.0 117.0 jit_solution(3175013363688534467)
XLA Ops:
  0.0 0.9 constant_dynamic-slice_fusion
  0.9 2.6 %collective-permute-start = (bf16[48,1536]{1,0:T(8,128)(2,1)S(1)}, bf16[48,1536]{1,0:T(8,128)(2,1)S(1)}, u32[]{:S(2)}, u32[]{:S(2)}) collective-permute-start(bf16[48,1536]{1,0:T(8,128)(2,1)S(1)} %constant_dynamic-slice_fusion), channel_id=1, source_target_pairs={{0,8},{1,9},{2,10},{3,11},{4,12},{5,13},{6,14},{7,15},{8,0},{9,1},... | collective-permute-start | bytes 442376 | tf_op jit(solution)/shard_map/ppermute | solution.py:415
  3.5 2.6 %pack_rows.1 = bf16[8,64,1152]{2,1,0:T(8,128)(2,1)} custom-call(bf16[128,1536]{1,0:T(8,128)(2,1)} %bitcast.7, bf16[128,1536]{1,0:T(8,128)(2,1)} %bitcast.8, bf16[128,1536]{1,0:T(8,128)(2,1)} %bitcast.9), custom_call_target="tpu_custom_call" | custom-call | tf_op jit(solution)/shard_map/pack_rows/pallas_call | solution.py:71
  6.0 8.6 %all-to-all-start = ((bf16[8,64,1152]{2,1,0:T(8,128)(2,1)}), bf16[8,64,1152]{2,1,0:T(8,128)(2,1)S(1)}, u32[]{:S(2)}, u32[]{:S(2)}) async-start(bf16[8,64,1152]{2,1,0:T(8,128)(2,1)} %pack_rows.1), calls=%async_computation | async-start | bytes 2359296 | tf_op jit(solution)/shard_map/all_to_all | solution.py:461
  14.9 1.4 %collective-permute-start.1 = (bf16[96,1536]{1,0:T(8,128)(2,1)S(1)}, bf16[96,1536]{1,0:T(8,128)(2,1)S(1)}, u32[]{:S(2)}, u32[]{:S(2)}) collective-permute-start(bf16[96,1536]{1,0:T(8,128)(2,1)S(1)} %pad_maximum_fusion), channel_id=1, source_target_pairs={{0,16},{1,65},{2,18},{3,67},{4,20},{5,69},{6,22},{7,71},{8,24},{9,... | collective-permute-start | bytes 884744 | tf_op jit(solution)/shard_map/ppermute | solution.py:415
  16.2 1.5 %collective-permute-start.2 = (bf16[96,1536]{1,0:T(8,128)(2,1)S(1)}, bf16[96,1536]{1,0:T(8,128)(2,1)S(1)}, u32[]{:S(2)}, u32[]{:S(2)}) collective-permute-start(bf16[96,1536]{1,0:T(8,128)(2,1)S(1)} %pad_maximum_fusion), channel_id=1, source_target_pairs={{0,48},{1,193},{2,50},{3,195},{4,52},{5,197},{6,54},{7,199},{8,56}... | collective-permute-start | bytes 884744 | tf_op jit(solution)/shard_map/ppermute | solution.py:415
  17.8 1.6 %collective-permute-start.3 = (bf16[96,1536]{1,0:T(8,128)(2,1)S(1)}, bf16[96,1536]{1,0:T(8,128)(2,1)S(1)}, u32[]{:S(2)}, u32[]{:S(2)}) collective-permute-start(bf16[96,1536]{1,0:T(8,128)(2,1)S(1)} %pad_maximum_fusion), channel_id=1, source_target_pairs={{0,32},{1,129},{2,34},{3,131},{4,36},{5,133},{6,38},{7,135},{8,40}... | collective-permute-start | bytes 884744 | tf_op jit(solution)/shard_map/ppermute | solution.py:415
  19.3 2.8 %collective-permute-done.1 = bf16[96,1536]{1,0:T(8,128)(2,1)S(1)} collective-permute-done((bf16[96,1536]{1,0:T(8,128)(2,1)S(1)}, bf16[96,1536]{1,0:T(8,128)(2,1)S(1)}, u32[]{:S(2)}, u32[]{:S(2)}) %collective-permute-start.1) | collective-permute-done | bytes 294944 | tf_op jit(solution)/shard_map/ppermute | solution.py:415
  22.1 2.5 %collective-permute-done.2 = bf16[96,1536]{1,0:T(8,128)(2,1)S(1)} collective-permute-done((bf16[96,1536]{1,0:T(8,128)(2,1)S(1)}, bf16[96,1536]{1,0:T(8,128)(2,1)S(1)}, u32[]{:S(2)}, u32[]{:S(2)}) %collective-permute-start.2) | collective-permute-done | bytes 294944 | tf_op jit(solution)/shard_map/ppermute | solution.py:415
  24.6 1.8 %collective-permute-done.3 = bf16[96,1536]{1,0:T(8,128)(2,1)S(1)} collective-permute-done((bf16[96,1536]{1,0:T(8,128)(2,1)S(1)}, bf16[96,1536]{1,0:T(8,128)(2,1)S(1)}, u32[]{:S(2)}, u32[]{:S(2)}) %collective-permute-start.3) | collective-permute-done | bytes 294944 | tf_op jit(solution)/shard_map/ppermute | solution.py:415
  26.4 2.8 %collective-permute-start.6 = (bf16[384,1536]{1,0:T(8,128)(2,1)S(1)}, bf16[384,1536]{1,0:T(8,128)(2,1)S(1)}, u32[]{:S(2)}, u32[]{:S(2)}) collective-permute-start(bf16[384,1536]{1,0:T(8,128)(2,1)S(1)} %constant_dynamic-update-slice_fusion.rest_8_), channel_id=1, source_target_pairs={{0,128},{1,33},{2,130},{3,35},{4,132},{5,37},{6,134},{7,39},{8,136... | collective-permute-start | bytes 3538952 | tf_op jit(solution)/shard_map/ppermute | solution.py:415
  29.3 0.9 collective-permute-start.5
  30.1 0.6 collective-permute-start.4
  30.7 0.7 reshape.4.rest_2_
  31.4 0.6 pad_add_fusion.me_ref.place_ref
  32.1 0.9 select_convert_fusion.rest_1_
  33.0 1.6 %collective-permute-start.7 = (bf16[384,1536]{1,0:T(8,128)(2,1)S(1)}, bf16[384,1536]{1,0:T(8,128)(2,1)}, u32[]{:S(2)}, u32[]{:S(2)}) collective-permute-start(bf16[384,1536]{1,0:T(8,128)(2,1)S(1)} %constant_dynamic-update-slice_fusion.rest_8_), channel_id=1, source_target_pairs={{0,1},{1,0},{2,3},{3,2},{4,5},{5,4},{6,7},{7,6},{8,9},{9,8},{10,11... | collective-permute-start | bytes 3538952 | tf_op jit(solution)/shard_map/ppermute | solution.py:415
  34.6 7.1 %all-to-all-done.x_ref.rest_0_ = bf16[8,64,1152]{2,1,0:T(8,128)(2,1)S(1)} async-done(((bf16[8,64,1152]{2,1,0:T(8,128)(2,1)}), bf16[8,64,1152]{2,1,0:T(8,128)(2,1)S(1)}, u32[]{:S(2)}, u32[]{:S(2)}) %all-to-all-start) | async-done | bytes 1179680 | tf_op jit(solution)/shard_map/all_to_all | solution.py:461
  41.7 1.0 copy-done
  42.7 27.9 %run_inner.1.rest_3_ = f32[8,64,384]{2,1,0:T(8,128)} custom-call(s32[2]{0:T(128)} %pad_add_fusion.me_ref.place_ref, f32[24]{0:T(128)} %rate_ref.1, bf16[8,64,1152]{2,1,0:T(8,128)(2,1)} %copy-done, bf16[24,64,256]{2,1,0:T(8,128)(2,1)} %first_ref.1, bf16[24,64,256]{2,1,0:T(8,128)(2,1)} %second_ref.1), custom_call_target="tpu_custom_call" | custom-call | flops 4000000000 | bytes 100000000 | tf_op jit(solution)/shard_map/run_inner/pallas_call | solution.py:240
  70.6 5.2 %collective-permute-start.8 = (bf16[384,1536]{1,0:T(8,128)(2,1)}, bf16[384,1536]{1,0:T(8,128)(2,1)S(1)}, u32[]{:S(2)}, u32[]{:S(2)}) collective-permute-start(bf16[384,1536]{1,0:T(8,128)(2,1)} %collective-permute-done.4.rest_9_), channel_id=1, source_target_pairs={{0,1},{1,0},{2,3},{3,2},{4,5},{5,4},{6,7},{7,6},{8,9},{9,8},{10,11... | collective-permute-start | bytes 3538952 | tf_op jit(solution)/shard_map/ppermute | solution.py:415
  75.9 0.4 collective-permute-start.10
  76.3 12.9 %run_attend.2 = (bf16[64,384]{1,0:T(8,128)(2,1)}, bf16[64,384]{1,0:T(8,128)(2,1)}, bf16[64,384]{1,0:T(8,128)(2,1)}, bf16[64,384]{1,0:T(8,128)(2,1)}, bf16[64,384...) custom-call(s32[2]{0:T(128)} %pad_add_fusion.me_ref.place_ref, bf16[8,64,1152]{2,1,0:T(8,128)(2,1)} %copy-done, ...), custom_call_target="tpu_custom_call" | custom-call | flops 700000000 | bytes 17500000 | tf_op jit(solution)/shard_map/run_attend/pallas_call | solution.py:317
  89.4 0.4 collective-permute-start.11
  89.7 1.8 %collective-permute-start.12 = (bf16[64,384]{1,0:T(8,128)(2,1)}, bf16[64,384]{1,0:T(8,128)(2,1)S(1)}, u32[]{:S(2)}, u32[]{:S(2)}) collective-permute-start(bf16[64,384]{1,0:T(8,128)(2,1)} %get-tuple-element.48), channel_id=1, source_target_pairs={{0,2},{1,3},{2,4},{3,5},{4,6},{5,7},{6,0},{7,1},{8,10},{9,11},{10,... | collective-permute-start | bytes 147464 | tf_op jit(solution)/shard_map/ppermute | solution.py:415
  91.5 1.8 %collective-permute-start.13 = (bf16[64,384]{1,0:T(8,128)(2,1)}, bf16[64,384]{1,0:T(8,128)(2,1)S(1)}, u32[]{:S(2)}, u32[]{:S(2)}) collective-permute-start(bf16[64,384]{1,0:T(8,128)(2,1)} %get-tuple-element.49), channel_id=1, source_target_pairs={{0,6},{1,7},{2,0},{3,1},{4,2},{5,3},{6,4},{7,5},{8,14},{9,15},{10,... | collective-permute-start | bytes 147464 | tf_op jit(solution)/shard_map/ppermute | solution.py:415
  93.3 5.9 %collective-permute-start.14 = (bf16[64,384]{1,0:T(8,128)(2,1)}, bf16[64,384]{1,0:T(8,128)(2,1)S(1)}, u32[]{:S(2)}, u32[]{:S(2)}) collective-permute-start(bf16[64,384]{1,0:T(8,128)(2,1)} %get-tuple-element.50), channel_id=1, source_target_pairs={{0,5},{1,4},{2,7},{3,6},{4,1},{5,0},{6,3},{7,2},{8,13},{9,12},{10,... | collective-permute-start | bytes 147464 | tf_op jit(solution)/shard_map/ppermute | solution.py:415
  99.2 3.9 %collective-permute-start.16 = (bf16[64,384]{1,0:T(8,128)(2,1)}, bf16[64,384]{1,0:T(8,128)(2,1)S(1)}, u32[]{:S(2)}, u32[]{:S(2)}) collective-permute-start(bf16[64,384]{1,0:T(8,128)(2,1)} %get-tuple-element.52), channel_id=1, source_target_pairs={{0,7},{1,6},{2,1},{3,0},{4,3},{5,2},{6,5},{7,4},{8,15},{9,14},{10,... | collective-permute-start | bytes 147464 | tf_op jit(solution)/shard_map/ppermute | solution.py:415
  103.1 5.2 %run_attend.3.rest_0_ = bf16[64,384]{1,0:T(8,128)(2,1)} custom-call(s32[2]{0:T(128)} %pad_add_fusion.me_ref.place_ref, bf16[8,64,1152]{2,1,0:T(8,128)(2,1)} %copy-done, bf16[1024,64]{1,0:T(8,128)(2,1)} %select_convert_fusion.rest_1_, f32[24,1,64]{2,1,0:T(1,128)} %reshape.4.rest_2_, f32[8,64,384]{2,1,0:T(8,128)} %run_inner.1.rest_3_), custom_call_target="tpu_custom_call" | custom-call | flops 100000000 | bytes 2500000 | tf_op jit(solution)/shard_map/run_attend/pallas_call | solution.py:317
  108.4 0.5 copy-done.9
  109.0 0.6 copy-done.13
  109.6 7.2 %project_rows.1 = bf16[128,3072]{1,0:T(8,128)(2,1)} custom-call(s32[2]{0:T(128)} %pad_add_fusion.me_ref.place_ref, bf16[64,384]{1,0:T(8,128)(2,1)} %run_attend.3.rest_0_, bf16[64,384]{1,0:T(8,128)(2,1)} %copy-done.7, bf16[64,384]{1,0:T(8,128)(2,1)} %copy-done.8, bf16[64,384]{1,0:T(8,128)(2,1)} %copy-done.9, bf16[64,384]{1,0:T(8,128)(2,1)} %copy-done.10, ...), custom_call_target="tpu_custom_call" | custom-call | tf_op jit(solution)/shard_map/project_rows/pallas_call | solution.py:384
  (53 shorter events, 0.4 us)
Async XLA Ops:
  0.9 13.8 %collective-permute-start = (bf16[48,1536]{1,0:T(8,128)(2,1)S(1)}, bf16[48,1536]{1,0:T(8,128)(2,1)S(1)}, u32[]{:S(2)}, u32[]{:S(2)}) collective-permute-start(bf16[48,1536]{1,0:T(8,128)(2,1)S(1)} %constant_dynamic-slice_fusion), channel_id=1, source_target_pairs={{0,8},{1,9},{2,10},{3,11},{4,12},{5,13},{6,14},{7,15},{8,0},{9,1},... | collective-permute-start | bytes 442376 | tf_op jit(solution)/shard_map/ppermute | solution.py:415
  6.0 8.7 %copy-start.6 = (bf16[48,3072]{1,0:T(8,128)(2,1)S(1)}, bf16[48,3072]{1,0:T(8,128)(2,1)}, u32[]{:S(2)}) copy-start(bf16[48,3072]{1,0:T(8,128)(2,1)} %param.17) | copy-start | bytes 884740
  6.0 35.6 %all-to-all-start = ((bf16[8,64,1152]{2,1,0:T(8,128)(2,1)}), bf16[8,64,1152]{2,1,0:T(8,128)(2,1)S(1)}, u32[]{:S(2)}, u32[]{:S(2)}) async-start(bf16[8,64,1152]{2,1,0:T(8,128)(2,1)} %pack_rows.1), calls=%async_computation | async-start | bytes 2359296 | tf_op jit(solution)/shard_map/all_to_all | solution.py:461
  14.8 15.9 %copy-start.14 = (f32[1536]{0:T(1024)S(1)}, f32[1536]{0:T(1024)}, u32[]{:S(2)}) copy-start(f32[1536]{0:T(1024)} %param.16) | copy-start | bytes 18436
  14.8 17.3 %copy-start.15 = (s32[1,1024]{1,0:T(1,128)S(1)}, s32[1,1024]{1,0:T(1,128)}, u32[]{:S(2)}) copy-start(s32[1,1024]{1,0:T(1,128)} %param.12) | copy-start | bytes 12292
  14.9 7.2 %collective-permute-start.1 = (bf16[96,1536]{1,0:T(8,128)(2,1)S(1)}, bf16[96,1536]{1,0:T(8,128)(2,1)S(1)}, u32[]{:S(2)}, u32[]{:S(2)}) collective-permute-start(bf16[96,1536]{1,0:T(8,128)(2,1)S(1)} %pad_maximum_fusion), channel_id=1, source_target_pairs={{0,16},{1,65},{2,18},{3,67},{4,20},{5,69},{6,22},{7,71},{8,24},{9,... | collective-permute-start | bytes 884744 | tf_op jit(solution)/shard_map/ppermute | solution.py:415
  16.2 8.4 %collective-permute-start.2 = (bf16[96,1536]{1,0:T(8,128)(2,1)S(1)}, bf16[96,1536]{1,0:T(8,128)(2,1)S(1)}, u32[]{:S(2)}, u32[]{:S(2)}) collective-permute-start(bf16[96,1536]{1,0:T(8,128)(2,1)S(1)} %pad_maximum_fusion), channel_id=1, source_target_pairs={{0,48},{1,193},{2,50},{3,195},{4,52},{5,197},{6,54},{7,199},{8,56}... | collective-permute-start | bytes 884744 | tf_op jit(solution)/shard_map/ppermute | solution.py:415
  17.8 8.7 %collective-permute-start.3 = (bf16[96,1536]{1,0:T(8,128)(2,1)S(1)}, bf16[96,1536]{1,0:T(8,128)(2,1)S(1)}, u32[]{:S(2)}, u32[]{:S(2)}) collective-permute-start(bf16[96,1536]{1,0:T(8,128)(2,1)S(1)} %pad_maximum_fusion), channel_id=1, source_target_pairs={{0,32},{1,129},{2,34},{3,131},{4,36},{5,133},{6,38},{7,135},{8,40}... | collective-permute-start | bytes 884744 | tf_op jit(solution)/shard_map/ppermute | solution.py:415
  26.4 44.1 %copy-start.1 = (bf16[384,1536]{1,0:T(8,128)(2,1)}, bf16[384,1536]{1,0:T(8,128)(2,1)S(1)}, u32[]{:S(2)}) copy-start(bf16[384,1536]{1,0:T(8,128)(2,1)S(1)} %constant_dynamic-update-slice_fusion.rest_8_) | copy-start | bytes 3538948
  26.4 44.1 %collective-permute-start.6 = (bf16[384,1536]{1,0:T(8,128)(2,1)S(1)}, bf16[384,1536]{1,0:T(8,128)(2,1)S(1)}, u32[]{:S(2)}, u32[]{:S(2)}) collective-permute-start(bf16[384,1536]{1,0:T(8,128)(2,1)S(1)} %constant_dynamic-update-slice_fusion.rest_8_), channel_id=1, source_target_pairs={{0,128},{1,33},{2,130},{3,35},{4,132},{5,37},{6,134},{7,39},{8,136... | collective-permute-start | bytes 3538952 | tf_op jit(solution)/shard_map/ppermute | solution.py:415
  29.3 41.3 %collective-permute-start.5 = (bf16[384,1536]{1,0:T(8,128)(2,1)S(1)}, bf16[384,1536]{1,0:T(8,128)(2,1)}, u32[]{:S(2)}, u32[]{:S(2)}) collective-permute-start(bf16[384,1536]{1,0:T(8,128)(2,1)S(1)} %constant_dynamic-update-slice_fusion.rest_8_), channel_id=1, source_target_pairs={{0,192},{1,49},{2,194},{3,51},{4,196},{5,53},{6,198},{7,55},{8,200... | collective-permute-start | bytes 3538952 | tf_op jit(solution)/shard_map/ppermute | solution.py:415
  30.1 40.5 %collective-permute-start.4 = (bf16[384,1536]{1,0:T(8,128)(2,1)S(1)}, bf16[384,1536]{1,0:T(8,128)(2,1)}, u32[]{:S(2)}, u32[]{:S(2)}) collective-permute-start(bf16[384,1536]{1,0:T(8,128)(2,1)S(1)} %constant_dynamic-update-slice_fusion.rest_8_), channel_id=1, source_target_pairs={{0,64},{1,17},{2,66},{3,19},{4,68},{5,21},{6,70},{7,23},{8,72},{9,... | collective-permute-start | bytes 3538952 | tf_op jit(solution)/shard_map/ppermute | solution.py:415
  33.0 56.3 %collective-permute-start.7 = (bf16[384,1536]{1,0:T(8,128)(2,1)S(1)}, bf16[384,1536]{1,0:T(8,128)(2,1)}, u32[]{:S(2)}, u32[]{:S(2)}) collective-permute-start(bf16[384,1536]{1,0:T(8,128)(2,1)S(1)} %constant_dynamic-update-slice_fusion.rest_8_), channel_id=1, source_target_pairs={{0,1},{1,0},{2,3},{3,2},{4,5},{5,4},{6,7},{7,6},{8,9},{9,8},{10,11... | collective-permute-start | bytes 3538952 | tf_op jit(solution)/shard_map/ppermute | solution.py:415
  41.7 1.0 copy-start
  70.6 18.7 %copy-start.2 = (bf16[384,1536]{1,0:T(8,128)(2,1)}, bf16[384,1536]{1,0:T(8,128)(2,1)S(1)}, u32[]{:S(2)}) copy-start(bf16[384,1536]{1,0:T(8,128)(2,1)S(1)} %collective-permute-done.6.rest_11_) | copy-start | bytes 3538948
  70.6 18.7 %collective-permute-start.8 = (bf16[384,1536]{1,0:T(8,128)(2,1)}, bf16[384,1536]{1,0:T(8,128)(2,1)S(1)}, u32[]{:S(2)}, u32[]{:S(2)}) collective-permute-start(bf16[384,1536]{1,0:T(8,128)(2,1)} %collective-permute-done.4.rest_9_), channel_id=1, source_target_pairs={{0,1},{1,0},{2,3},{3,2},{4,5},{5,4},{6,7},{7,6},{8,9},{9,8},{10,11... | collective-permute-start | bytes 3538952 | tf_op jit(solution)/shard_map/ppermute | solution.py:415
  75.8 13.5 %collective-permute-start.9 = (bf16[384,1536]{1,0:T(8,128)(2,1)}, bf16[384,1536]{1,0:T(8,128)(2,1)S(1)}, u32[]{:S(2)}, u32[]{:S(2)}) collective-permute-start(bf16[384,1536]{1,0:T(8,128)(2,1)} %collective-permute-done.5.rest_10_), channel_id=1, source_target_pairs={{0,1},{1,0},{2,3},{3,2},{4,5},{5,4},{6,7},{7,6},{8,9},{9,8},{10,11... | collective-permute-start | bytes 3538952 | tf_op jit(solution)/shard_map/ppermute | solution.py:415
  75.9 13.4 %collective-permute-start.10 = (bf16[384,1536]{1,0:T(8,128)(2,1)S(1)}, bf16[384,1536]{1,0:T(8,128)(2,1)S(1)}, u32[]{:S(2)}, u32[]{:S(2)}) collective-permute-start(bf16[384,1536]{1,0:T(8,128)(2,1)S(1)} %collective-permute-done.6.rest_11_), channel_id=1, source_target_pairs={{0,1},{1,0},{2,3},{3,2},{4,5},{5,4},{6,7},{7,6},{8,9},{9,8},{10,11... | collective-permute-start | bytes 3538952 | tf_op jit(solution)/shard_map/ppermute | solution.py:415
  89.3 19.1 %copy-start.3 = (bf16[384,1536]{1,0:T(8,128)(2,1)}, bf16[384,1536]{1,0:T(8,128)(2,1)S(1)}, u32[]{:S(2)}) copy-start(bf16[384,1536]{1,0:T(8,128)(2,1)S(1)} %collective-permute-done.8.rest_13_) | copy-start | bytes 3538948
  89.3 19.1 %copy-start.4 = (bf16[384,1536]{1,0:T(8,128)(2,1)}, bf16[384,1536]{1,0:T(8,128)(2,1)S(1)}, u32[]{:S(2)}) copy-start(bf16[384,1536]{1,0:T(8,128)(2,1)S(1)} %collective-permute-done.9.rest_14_) | copy-start | bytes 3538948
  89.3 19.0 %copy-start.5 = (bf16[384,1536]{1,0:T(8,128)(2,1)}, bf16[384,1536]{1,0:T(8,128)(2,1)S(1)}, u32[]{:S(2)}) copy-start(bf16[384,1536]{1,0:T(8,128)(2,1)S(1)} %collective-permute-done.10.rest_15_) | copy-start | bytes 3538948
  89.4 9.8 %collective-permute-start.11 = (bf16[64,384]{1,0:T(8,128)(2,1)}, bf16[64,384]{1,0:T(8,128)(2,1)S(1)}, u32[]{:S(2)}, u32[]{:S(2)}) collective-permute-start(bf16[64,384]{1,0:T(8,128)(2,1)} %get-tuple-element.47), channel_id=1, source_target_pairs={{0,4},{1,5},{2,6},{3,7},{4,0},{5,1},{6,2},{7,3},{8,12},{9,13},{10,... | collective-permute-start | bytes 147464 | tf_op jit(solution)/shard_map/ppermute | solution.py:415
  89.7 13.3 %collective-permute-start.12 = (bf16[64,384]{1,0:T(8,128)(2,1)}, bf16[64,384]{1,0:T(8,128)(2,1)S(1)}, u32[]{:S(2)}, u32[]{:S(2)}) collective-permute-start(bf16[64,384]{1,0:T(8,128)(2,1)} %get-tuple-element.48), channel_id=1, source_target_pairs={{0,2},{1,3},{2,4},{3,5},{4,6},{5,7},{6,0},{7,1},{8,10},{9,11},{10,... | collective-permute-start | bytes 147464 | tf_op jit(solution)/shard_map/ppermute | solution.py:415
  91.5 16.8 %collective-permute-start.13 = (bf16[64,384]{1,0:T(8,128)(2,1)}, bf16[64,384]{1,0:T(8,128)(2,1)S(1)}, u32[]{:S(2)}, u32[]{:S(2)}) collective-permute-start(bf16[64,384]{1,0:T(8,128)(2,1)} %get-tuple-element.49), channel_id=1, source_target_pairs={{0,6},{1,7},{2,0},{3,1},{4,2},{5,3},{6,4},{7,5},{8,14},{9,15},{10,... | collective-permute-start | bytes 147464 | tf_op jit(solution)/shard_map/ppermute | solution.py:415
  93.3 15.0 %collective-permute-start.14 = (bf16[64,384]{1,0:T(8,128)(2,1)}, bf16[64,384]{1,0:T(8,128)(2,1)S(1)}, u32[]{:S(2)}, u32[]{:S(2)}) collective-permute-start(bf16[64,384]{1,0:T(8,128)(2,1)} %get-tuple-element.50), channel_id=1, source_target_pairs={{0,5},{1,4},{2,7},{3,6},{4,1},{5,0},{6,3},{7,2},{8,13},{9,12},{10,... | collective-permute-start | bytes 147464 | tf_op jit(solution)/shard_map/ppermute | solution.py:415
  99.2 9.1 %collective-permute-start.15 = (bf16[64,384]{1,0:T(8,128)(2,1)}, bf16[64,384]{1,0:T(8,128)(2,1)S(1)}, u32[]{:S(2)}, u32[]{:S(2)}) collective-permute-start(bf16[64,384]{1,0:T(8,128)(2,1)} %get-tuple-element.51), channel_id=1, source_target_pairs={{0,3},{1,2},{2,5},{3,4},{4,7},{5,6},{6,1},{7,0},{8,11},{9,10},{10,... | collective-permute-start | bytes 147464 | tf_op jit(solution)/shard_map/ppermute | solution.py:415
  99.2 9.2 %copy-start.7 = (bf16[64,384]{1,0:T(8,128)(2,1)}, bf16[64,384]{1,0:T(8,128)(2,1)S(1)}, u32[]{:S(2)}) copy-start(bf16[64,384]{1,0:T(8,128)(2,1)S(1)} %collective-permute-done.11.rest_1_) | copy-start | bytes 147460
  99.2 9.1 %collective-permute-start.16 = (bf16[64,384]{1,0:T(8,128)(2,1)}, bf16[64,384]{1,0:T(8,128)(2,1)S(1)}, u32[]{:S(2)}, u32[]{:S(2)}) collective-permute-start(bf16[64,384]{1,0:T(8,128)(2,1)} %get-tuple-element.52), channel_id=1, source_target_pairs={{0,7},{1,6},{2,1},{3,0},{4,3},{5,2},{6,5},{7,4},{8,15},{9,14},{10,... | collective-permute-start | bytes 147464 | tf_op jit(solution)/shard_map/ppermute | solution.py:415
  103.1 5.3 %copy-start.8 = (bf16[64,384]{1,0:T(8,128)(2,1)}, bf16[64,384]{1,0:T(8,128)(2,1)S(1)}, u32[]{:S(2)}) copy-start(bf16[64,384]{1,0:T(8,128)(2,1)S(1)} %collective-permute-done.12.rest_2_) | copy-start | bytes 147460
  103.1 5.3 %collective-permute-start.17 = (bf16[64,384]{1,0:T(8,128)(2,1)}, bf16[64,384]{1,0:T(8,128)(2,1)S(1)}, u32[]{:S(2)}, u32[]{:S(2)}) collective-permute-start(bf16[64,384]{1,0:T(8,128)(2,1)} %get-tuple-element.53), channel_id=1, source_target_pairs={{0,1},{1,0},{2,3},{3,2},{4,5},{5,4},{6,7},{7,6},{8,9},{9,8},{10,11... | collective-permute-start | bytes 147464 | tf_op jit(solution)/shard_map/ppermute | solution.py:415
  108.3 0.6 copy-start.10
  109.0 0.6 copy-start.13
  (3 other events, 1.8 us)

commit v3 on v0

v3 whole, which is shorter than its diff:
```python
import functools
import math

import jax
import jax.numpy as jnp
from jax import lax
from jax.experimental import pallas as pl
from jax.experimental.pallas import tpu as pltpu
from jax.sharding import PartitionSpec as P

HD = 64
FFI = 256
CH = 64
BATCH = 4
LOCAL = 3
PARTS = 8
TOK = 128
LEN = 1024
HH = 1536
WIDTH = LOCAL * HD
SAME = 32.0
EPS = 1e-6
GA = math.sqrt(2.0 / math.pi)
GB = GA * 0.044715
MIB = 1024 * 1024

f32 = jnp.float32
bf16 = jnp.bfloat16


def dot(left, right):
    return jnp.dot(left, right, preferred_element_type=f32)


def dot_nt(left, right):
    return lax.dot_general(left, right, (((1,), (1,)), ((), ())), preferred_element_type=f32)


def dot_tn(left, right):
    return lax.dot_general(left, right, (((0,), (0,)), ((), ())), preferred_element_type=f32)


def lane_mean(value):
    return jnp.mean(value, axis=-1, keepdims=True)


def pack_kernel(q_ref, k_ref, v_ref, weight_ref, out, slab):
    wide = slab.shape[1]
    core = lax.rem(lax.axis_index("seq"), 2)
    slab[...] = weight_ref[:, pl.ds(pl.multiple_of(core * wide, wide), wide)]
    for part in range(PARTS):
        cols = slice(part * WIDTH, (part + 1) * WIDTH)
        for group, ref in enumerate((q_ref, k_ref, v_ref)):
            for half in range(2):
                at = (2 * group + half) * WIDTH
                out[part, :, at : at + WIDTH] = ref[half * CH : (half + 1) * CH, cols]


def pack(queries, keys, values, weight):
    return pl.pallas_call(
        pack_kernel,
        out_shape=[
            jax.ShapeDtypeStruct((PARTS, CH, 6 * WIDTH), bf16),
            jax.ShapeDtypeStruct((weight.shape[0], weight.shape[1] // 2), bf16),
        ],
        compiler_params=pltpu.CompilerParams(vmem_limit_bytes=62 * MIB),
        name="pack_rows",
    )(queries, keys, values, weight)


def gelu_parts(z, slope):
    square = z * z
    half = 0.5 * jnp.tanh(z * (GB * square + GA)) + 0.5
    act = z * half
    if not slope:
        return act, None
    return act, half + (act - act * half) * (6.0 * GB * square + 2.0 * GA)


def stack_heads(joint):
    head = lax.broadcasted_iota(jnp.int32, joint.shape, 1) // HD
    zero = jnp.zeros_like(joint)
    return jnp.concatenate([jnp.where(head == h, joint, zero) for h in range(LOCAL)], axis=0)


def join_heads(full):
    rows = full.shape[0] // LOCAL
    blocks = [full[h * rows : (h + 1) * rows] for h in range(LOCAL)]
    head = lax.broadcasted_iota(jnp.int32, blocks[0].shape, 1) // HD
    joint = blocks[0]
    for h in range(1, LOCAL):
        joint = jnp.where(head == h, blocks[h], joint)
    return joint


def halves(value):
    high = value.astype(bf16)
    return high, (value - high.astype(f32)).astype(bf16)


def head_means(value, spread):
    rows = value.shape[0]
    both = dot(jnp.concatenate(halves(value), axis=0), spread)
    return both[:rows] + both[rows:]


def heads_kernel(
    rate_ref, x, seg_ref, weights, gate_ref, mixed,
    q_low, k_low, q_wide, k_wide, xq, target, attended, w1s, w2s, b1s, b2s, z1s, q1s, a_prev,
    w2_prev, g2_prev, b2_prev,
):
    me = lax.axis_index("seq")
    heads = range(LOCAL)
    column = lax.broadcasted_iota(jnp.int32, (WIDTH, WIDTH), 1) // HD
    row = lax.broadcasted_iota(jnp.int32, (WIDTH, WIDTH), 0) // HD
    spread = jnp.where(row == column, 1.0 / HD, 0.0).astype(bf16)
    token = lax.broadcasted_iota(jnp.int32, (CH, WIDTH), 0)
    causal = token >= lax.rem(lax.broadcasted_iota(jnp.int32, (CH, WIDTH), 1), HD)
    lane_head = lax.broadcasted_iota(jnp.int32, (1, WIDTH), 1) // HD
    etas = jnp.zeros((1, WIDTH), f32)
    for h in heads:
        etas = jnp.where(lane_head == h, rate_ref[me * LOCAL + h] * (1.0 / HD), etas)

    half_rows = PARTS * CH
    number = lax.broadcasted_iota(jnp.int32, (HD, LEN), 0)
    unit = jnp.where(
        lax.broadcasted_iota(jnp.int32, (HD, HD), 0) == lax.broadcasted_iota(jnp.int32, (HD, HD), 1), 1.0, 0.0
    )
    seg = dot_tn(jnp.where(seg_ref[...] == number, SAME, 0.0).astype(bf16), unit.astype(bf16)).astype(bf16)
    seg = seg.reshape(PARTS, 2, CH, HD)
    segs = [seg[:, half].reshape(half_rows, HD) for half in range(2)]

    def columns(group, h, half):
        at = (2 * group + half) * WIDTH + h * HD
        return x[:, :, at : at + HD].reshape(half_rows, HD)

    ones = jnp.ones((half_rows, HD), bf16)
    for h in heads:
        keys = [jnp.concatenate([columns(1, h, half), segs[half]], axis=1) for half in range(2)]
        values = [jnp.concatenate([columns(2, h, half), ones], axis=1) for half in range(2)]
        keys, values = jnp.concatenate(keys, axis=0), jnp.concatenate(values, axis=0)
        for half in range(2):
            q = jnp.concatenate([(columns(0, h, half) * 0.125).astype(bf16), segs[half]], axis=1)
            scores = dot_nt(q, keys)
            top = jnp.max(scores, axis=-1, keepdims=True)
            got = dot(jnp.exp(scores - top).astype(bf16), values)
            got = got[:, :HD] / got[:, HD:]
            attended[:, half, :, h * HD : (h + 1) * HD] = got.reshape(PARTS, CH, HD)

    for begin in range(0, PARTS, BATCH):
        some = slice(begin, begin + BATCH)
        for half in range(2):
            q, k, v = (
                x[some, :, (2 * g + half) * WIDTH : (2 * g + half + 1) * WIDTH].reshape(BATCH * CH, WIDTH)
                for g in range(3)
            )
            both = jnp.concatenate([q, k], axis=0).astype(f32)
            both = both * lax.rsqrt(head_means(both * both, spread) + EPS)
            high, low = halves(both)
            goal = v.astype(f32) - both[BATCH * CH :]
            goal = goal - head_means(goal, spread)
            per_block = (BATCH, CH, WIDTH)
            xq[some, half] = both[: BATCH * CH].reshape(per_block)
            target[some, half] = goal.reshape(per_block)
            q_low[some, half] = high[: BATCH * CH].reshape(per_block)
            k_low[some, half] = high[BATCH * CH :].reshape(per_block)
            for h in heads:
                at = slice(h * HD, (h + 1) * HD)
                wide = jnp.concatenate([high[:, at], low[:, at], high[:, at]], axis=1)
                q_wide[h, some, half] = wide[: BATCH * CH].reshape(per_block)
                k_wide[h, some, half] = wide[BATCH * CH :].reshape(per_block)

    def project(h, state, bias, wide):
        high, low = halves(state)
        return dot(wide, jnp.concatenate([high, high, low], axis=0)) + bias

    for h in heads:
        at = slice(h * HD, (h + 1) * HD)
        start = weights[1, h].astype(f32)
        w2s[at, :] = start - jnp.mean(start, axis=0, keepdims=True)
        first = weights[0, h]
        w1s[at, :] = first.astype(f32)
        z1s[at, :] = dot(k_wide[h, 0, 0], jnp.concatenate([first, first, jnp.zeros_like(first)], axis=0))
    for ref in (b1s, b2s, q1s, a_prev, w2_prev, g2_prev, b2_prev):
        ref[...] = jnp.zeros_like(ref)

    gate = jnp.tanh(gate_ref[...])

    def query_first():
        high, low = halves(gelu_parts(q1s[...], False)[0])
        near = dot_nt(high, a_prev[...])
        deep = dot_nt(jnp.concatenate([high, low], axis=0), w2_prev[...])
        return near, deep, g2_prev[...], b2_prev[...]

    def query_last(state, source, half):
        near, deep, grad, bias = state
        near = jnp.where(causal, join_heads(near) + 1.0, 0.0).astype(bf16)
        out = join_heads(deep[:WIDTH] + deep[WIDTH:]) + bias - dot(near, grad)
        inner = xq[source, half] + out * lax.rsqrt(head_means(out * out, spread) + EPS)
        mixed[source, :, half * WIDTH : (half + 1) * WIDTH] = (attended[source, half] + gate * inner).astype(bf16)

    def one_block(now, later, before):
        z1, w1_now, w2_now, b1, b2 = z1s[...], w1s[...], w2s[...], b1s[...], b2s[...]
        goal = target[*now]
        query = query_first()

        keys = stack_heads(k_low[*now])
        cross = dot_nt(jnp.concatenate([q_low[*now], k_low[*later]], axis=0), keys) + 1.0
        cross = jnp.concatenate([jnp.where(causal, cross[:CH], 0.0), cross[CH:]], axis=0).astype(bf16)
        cross = stack_heads(cross)
        ahead = [
            project(
                h,
                w1_now[h * HD : (h + 1) * HD],
                b1[h],
                jnp.concatenate([q_wide[h, *now], k_wide[h, *later]], axis=0),
            )
            for h in heads
        ]

        act, slope = gelu_parts(z1, True)
        act_low = act.astype(bf16)
        w2_low = w2_now.astype(bf16)
        c = join_heads(dot_nt(act_low, w2_low)) + b2
        means = dot(jnp.concatenate([c * c, c * goal], axis=0).astype(bf16), spread)
        r = lax.rsqrt(means[:CH] + EPS)
        grad = (etas * r) * (c * (r * (EPS * r * r + means[CH:] * r)) - goal)
        grad_low = stack_heads(grad.astype(bf16))
        deep = dot(grad_low, w2_low) * slope
        deep_low = deep.astype(bf16)
        moved = dot(cross, deep_low)
        new_w2 = w2_now - dot_tn(grad_low, act_low)
        new_w1 = w1_now - dot_tn(keys, deep_low)
        new_b2 = b2 - jnp.sum(grad, axis=0, keepdims=True)
        new_b1 = [b1[h] - jnp.sum(deep[h * CH : (h + 1) * CH], axis=0, keepdims=True) for h in heads]
        query_last(query, *before)

        for h in heads:
            both = ahead[h] - moved[2 * h * CH : 2 * (h + 1) * CH]
            q1s[h * CH : (h + 1) * CH, :] = both[:CH]
            z1s[h * CH : (h + 1) * CH, :] = both[CH:]
            b1s[h] = new_b1[h]
        a_prev[...] = act_low
        w2_prev[...] = w2_low
        g2_prev[...] = grad_low
        b2_prev[...] = b2
        w1s[...] = new_w1
        w2s[...] = new_w2
        b2s[...] = new_b2

    def blocks(source, carry):
        last, ahead = jnp.maximum(source - 1, 0), jnp.minimum(source + 1, PARTS - 1)
        one_block((source, 0), (source, 1), (last, 1))
        one_block((source, 1), (ahead, 0), (source, 0))
        return carry

    lax.fori_loop(0, PARTS, blocks, 0)
    query_last(query_first(), PARTS - 1, 1)


VMEM = pl.BlockSpec(memory_space=pltpu.VMEM)
SMEM = pl.BlockSpec(memory_space=pltpu.SMEM)


def run_heads(rate, pieces, seg, weights, gate):
    blocks = (PARTS, 2, CH, WIDTH)
    return pl.pallas_call(
        heads_kernel,
        out_shape=jax.ShapeDtypeStruct((PARTS, CH, 2 * WIDTH), bf16),
        in_specs=[SMEM] + [VMEM] * 4,
        out_specs=VMEM,
        scratch_shapes=[
            pltpu.VMEM(blocks, bf16),
            pltpu.VMEM(blocks, bf16),
            pltpu.VMEM((LOCAL,) + blocks, bf16),
            pltpu.VMEM((LOCAL,) + blocks, bf16),
            pltpu.VMEM(blocks, f32),
            pltpu.VMEM(blocks, f32),
            pltpu.VMEM(blocks, f32),
            pltpu.VMEM((WIDTH, FFI), f32),
            pltpu.VMEM((WIDTH, FFI), f32),
            pltpu.VMEM((LOCAL, 1, FFI), f32),
            pltpu.VMEM((1, WIDTH), f32),
            pltpu.VMEM((WIDTH, FFI), f32),
            pltpu.VMEM((WIDTH, FFI), f32),
            pltpu.VMEM((WIDTH, FFI), bf16),
            pltpu.VMEM((WIDTH, FFI), bf16),
            pltpu.VMEM((WIDTH, WIDTH), bf16),
            pltpu.VMEM((1, WIDTH), f32),
        ],
        compiler_params=pltpu.CompilerParams(vmem_limit_bytes=32 * MIB),
        cost_estimate=pl.CostEstimate(flops=4_000_000_000, bytes_accessed=100_000_000, transcendentals=0),
        name="run_heads",
    )(rate, pieces, seg, weights, gate)


def project_kernel(mixed, *rest):
    own, sib, out, groups = rest[:4], rest[4:8], rest[8], rest[9]
    core, dp = lax.rem(lax.axis_index("seq"), 2), lax.axis_index("dp")
    y, x = dp // 8, lax.rem(dp // 2, 4)
    for source in range(PARTS):
        for pair in range(2):
            for half in range(2):
                at = half * WIDTH + pair * 2 * ROWS
                groups[2 * source + pair, half * CH : (half + 1) * CH, :] = mixed[source, :, at : at + 2 * ROWS]
    for side, blocks in enumerate((own, sib)):
        axis = core if side == 0 else 1 - core
        left = []
        for far in STEPS:
            for near in STEPS:
                dx = jnp.where(axis == 0, near, far)
                dy = jnp.where(axis == 0, far, near)
                left.append(groups[lax.rem(y + 4 - dy, 4) * 4 + lax.rem(x + 4 - dx, 4)])
        left = jnp.concatenate(left, axis=1)
        wide = blocks[0].shape[1]
        for at in range(0, wide, 256):
            right = jnp.concatenate([block[:, at : at + 256] for block in blocks], axis=0)
            out[:, pl.ds(pl.multiple_of(axis * wide + at, 256), 256)] = dot(left, right).astype(bf16)


def run_project(mixed, own, sib):
    wide = own[0].shape[1]
    return pl.pallas_call(
        project_kernel,
        out_shape=jax.ShapeDtypeStruct((TOK, 2 * wide), bf16),
        in_specs=[VMEM] * 9,
        out_specs=VMEM,
        scratch_shapes=[pltpu.VMEM((2 * PARTS, TOK, 2 * ROWS), bf16)],
        compiler_params=pltpu.CompilerParams(vmem_limit_bytes=20 * MIB),
        name="project_rows",
    )(mixed, *own, *sib)


ROWS = HH // 32
STEPS = (0, 1, 3, 2)


def where_is(index):
    dp, seq = divmod(index, PARTS)
    return dp // 8, (dp // 2) % 4, dp % 2, seq // 2, seq % 2


def index_of(y, x, z, group, core):
    return ((y % 4) * 8 + (x % 4) * 2 + z % 2) * PARTS + (group % 4) * 2 + core % 2


def move(array, place):
    pairs = [(i, index_of(*place(*where_is(i)))) for i in range(32 * PARTS)]
    return lax.ppermute(array, ("dp", "seq"), pairs)


def turn(array, step):
    return lax.ppermute(array, "seq", [(i, (i + step) % PARTS) for i in range(PARTS)])


def near_axis(step):
    return lambda y, x, z, group, core: (y + step * core, x + step * (1 - core), z, group, core)


def far_axis(step):
    return lambda y, x, z, group, core: (y + step * (1 - core), x + step * core, z, group, core)


def flip_z(y, x, z, group, core):
    return y, x, 1 - z, group, core


def flip_core(y, x, z, group, core):
    return y, x, z, group, 1 - core


def on_device(
    queries, key_states, value_states, segment_ids, inner_first, inner_second, inner_rate, branch_gate, out_weight
):
    seq, dp = lax.axis_index("seq"), lax.axis_index("dp")
    pieces, slab = pack(queries[0], key_states[0], value_states[0], out_weight)
    other = move(slab, flip_z)
    upper = dp % 2 == 1
    slab = jnp.concatenate([jnp.where(upper, other, slab), jnp.where(upper, slab, other)], axis=0)

    pieces = lax.all_to_all(pieces, "seq", split_axis=0, concat_axis=0, tiled=True)
    near = [move(slab, near_axis(step)) for step in STEPS[1:]]
    slab = jnp.concatenate([slab] + near, axis=0)
    own = [slab] + [move(slab, far_axis(step)) for step in STEPS[1:]]
    sib = [move(slab, flip_core)]

    weights = jnp.stack([lax.dynamic_slice_in_dim(w, seq * LOCAL, LOCAL, 0) for w in (inner_first, inner_second)])
    gate = lax.dynamic_slice_in_dim(branch_gate, seq * WIDTH, WIDTH, 0)[None]
    pieces, slab, gate, weights = lax.optimization_barrier((pieces, slab, gate, weights))
    mixed = run_heads(inner_rate, pieces, segment_ids, weights, gate)
    own = list(lax.optimization_barrier((tuple(own), mixed))[0])
    mixed = lax.all_to_all(mixed, "seq", split_axis=0, concat_axis=0, tiled=True)
    sib = [move(block, flip_core) for block in own]
    return run_project(mixed, own, sib)[None]


def solution(mesh):
    in_specs = (
        P("dp", "seq", None),
        P("dp", "seq", None),
        P("dp", "seq", None),
        P("dp", None),
        P(),
        P(),
        P(),
        P(),
        P("dp", None),
    )
    return jax.shard_map(
        on_device, mesh=mesh, in_specs=in_specs, out_specs=P("dp", "seq", None), check_vma=False
    )
```

time: 293 us -> 91.9 us (0.31)
  matrix products: 82 us -> 0 us
  local copies, waits for them, and re-layouts: 75.2 us -> 2.72 us
  other arithmetic: 36.5 us -> 0.8 us
  Pallas kernels: 0 us -> 30.1 us
  waiting for transfers between devices: 41 us -> 15.6 us
  between operations: 13.7 us -> 0.1 us
  starting transfers between devices: 19.9 us -> 25.7 us
  loops' own time: 5.48 us -> 0 us
    dot_general x189 -> x0, matrix products: 82 us -> none  [the longest x176 68.4 us: dense(): return jnp.einsum(form, left, right, precision=lax.Precision.HIGHEST)]
    dynamic_slice x108 -> x1, local copies, waits for them, and re-layouts: 54.1 us -> 0.77 us  [on_device(): gate = lax.dynamic_slice_in_dim(branch_gate, seq * WIDTH, WIDTH, 0)[None]]
    all_to_all x3 -> x1, waiting for transfers between devices: 40.3 us -> 8.54 us  [on_device(): lax.all_to_all(pieces, 'seq', split_axis=0, concat_axis=0, tiled=True)]
    pallas_call x0 -> x3, Pallas kernels: none -> 30.1 us  [the longest x1 23.2 us: run_heads(): pl.pallas_call(heads_kernel, out_shape=jax.ShapeDtypeStruct((PARTS, CH, 2...]
    reduce_sum x88 -> x0, other arithmetic: 19.1 us -> none  [the longest x32 5.67 us: inner_norm(): spread = jnp.mean(center * center, axis=-1, keepdims=True)]
    ppermute x0 -> x11, starting transfers between devices: none -> 17 us  [move(): return lax.ppermute(array, ('dp', 'seq'), pairs)]
    dynamic_update_slice x16 -> x0, other arithmetic: 12.2 us -> none  [inner_run(): lax.scan(advance, unpack(state), (split(query_part), split(key_part), spl...]
    all_to_all x3 -> x1, starting transfers between devices: 19.9 us -> 8.64 us  [on_device(): lax.all_to_all(pieces, 'seq', split_axis=0, concat_axis=0, tiled=True)]
  transfers between devices with their start and end apart: 4 -> 12, of which waited for: 3 -> 4; matrix products, arithmetic and copies ran while one was open for 64% -> 3% of each run, Pallas kernels for 0% -> 25%
where the time goes in v3:
time: 91.9 us; the launch traced here: 91.5 us
  Pallas kernels  30.1 us (33%)
  starting transfers between devices  25.7 us (28%)
  blocking collectives  16.5 us (18%)
  waiting for transfers between devices  15.6 us (17%)
  local copies, waits for them, and re-layouts  2.72 us (3%)
    pallas_call x1, Pallas kernels, run_heads(): pl.pallas_call(heads_kernel, out_shape=jax.ShapeDtypeStruct((PARTS, CH, 2...  23.2 us
    ppermute x11, starting transfers between devices, move(): return lax.ppermute(array, ('dp', 'seq'), pairs)  17 us
    all_to_all x1, blocking collectives, on_device(): lax.all_to_all(mixed, 'seq', split_axis=0, concat_axis=0, tiled=True)  16.5 us
    all_to_all x1, starting transfers between devices, on_device(): lax.all_to_all(pieces, 'seq', split_axis=0, concat_axis=0, tiled=True)  8.64 us
    all_to_all x1, waiting for transfers between devices, on_device(): lax.all_to_all(pieces, 'seq', split_axis=0, concat_axis=0, tiled=True)  8.54 us
    ppermute x11, waiting for transfers between devices, move(): return lax.ppermute(array, ('dp', 'seq'), pairs)  7.07 us
    pallas_call x1, Pallas kernels, run_project(): pl.pallas_call(project_kernel, out_shape=jax.ShapeDtypeStruct((TOK, 2 * w...  4.22 us
    pallas_call x1, Pallas kernels, pack(): pl.pallas_call(pack_kernel, out_shape=[jax.ShapeDtypeStruct((PARTS, CH, 6...  2.64 us
  transfers between devices with their start and end apart: 12, of which 4 were waited for; matrix products, arithmetic and copies ran while one was open for 3% of the time, Pallas kernels for 25%

profile of v3, /device:TPU:1, one launch (start us, length us, event | category | flops | bytes accessed | tf_op | source)
XLA Modules:
  0.0 91.5 jit_solution(11605425168555893707)
XLA Ops:
  0.0 2.6 %pack_rows.1 = (bf16[8,64,1152]{2,1,0:T(8,128)(2,1)}, bf16[48,1536]{1,0:T(8,128)(2,1)}) custom-call(bf16[128,1536]{1,0:T(8,128)(2,1)} %bitcast.10, bf16[128,1536]{1,0:T(8,128)(2,1)} %bitcast.11, bf16[128,1536]{1,0:T(8,128)(2,1)} %bitcast.12, bf16[48,3072]{1,0:T(8,128)(2,1)} %weight_ref.1), custom_call_target="tpu_custom_call" | custom-call | tf_op jit(solution)/shard_map/pack_rows/pallas_call | solution.py:60
  2.6 2.5 %collective-permute-start = (bf16[48,1536]{1,0:T(8,128)(2,1)}, bf16[48,1536]{1,0:T(8,128)(2,1)S(1)}, u32[]{:S(2)}, u32[]{:S(2)}) collective-permute-start(bf16[48,1536]{1,0:T(8,128)(2,1)} %get-tuple-element.15), channel_id=1, source_target_pairs={{0,8},{1,9},{2,10},{3,11},{4,12},{5,13},{6,14},{7,15},{8,0},{9,1},... | collective-permute-start | bytes 442376 | tf_op jit(solution)/shard_map/ppermute | solution.py:349
  5.1 8.6 %all-to-all-start = ((bf16[8,64,1152]{2,1,0:T(8,128)(2,1)}), bf16[8,64,1152]{2,1,0:T(8,128)(2,1)S(1)}, u32[]{:S(2)}, u32[]{:S(2)}) async-start(bf16[8,64,1152]{2,1,0:T(8,128)(2,1)} %get-tuple-element.14), calls=%async_computation | async-start | bytes 2359296 | tf_op jit(solution)/shard_map/all_to_all | solution.py:381
  13.8 0.0 collective-permute-done
  13.9 1.4 %collective-permute-start.1 = (bf16[96,1536]{1,0:T(8,128)(2,1)S(1)}, bf16[96,1536]{1,0:T(8,128)(2,1)S(1)}, u32[]{:S(2)}, u32[]{:S(2)}) collective-permute-start(bf16[96,1536]{1,0:T(8,128)(2,1)S(1)} %pad_maximum_fusion), channel_id=1, source_target_pairs={{0,16},{1,65},{2,18},{3,67},{4,20},{5,69},{6,22},{7,71},{8,24},{9,... | collective-permute-start | bytes 884744 | tf_op jit(solution)/shard_map/ppermute | solution.py:349
  15.3 1.5 %collective-permute-start.2 = (bf16[96,1536]{1,0:T(8,128)(2,1)S(1)}, bf16[96,1536]{1,0:T(8,128)(2,1)S(1)}, u32[]{:S(2)}, u32[]{:S(2)}) collective-permute-start(bf16[96,1536]{1,0:T(8,128)(2,1)S(1)} %pad_maximum_fusion), channel_id=1, source_target_pairs={{0,48},{1,193},{2,50},{3,195},{4,52},{5,197},{6,54},{7,199},{8,56}... | collective-permute-start | bytes 884744 | tf_op jit(solution)/shard_map/ppermute | solution.py:349
  16.8 1.6 %collective-permute-start.3 = (bf16[96,1536]{1,0:T(8,128)(2,1)S(1)}, bf16[96,1536]{1,0:T(8,128)(2,1)S(1)}, u32[]{:S(2)}, u32[]{:S(2)}) collective-permute-start(bf16[96,1536]{1,0:T(8,128)(2,1)S(1)} %pad_maximum_fusion), channel_id=1, source_target_pairs={{0,32},{1,129},{2,34},{3,131},{4,36},{5,133},{6,38},{7,135},{8,40}... | collective-permute-start | bytes 884744 | tf_op jit(solution)/shard_map/ppermute | solution.py:349
  18.3 2.8 %collective-permute-done.1 = bf16[96,1536]{1,0:T(8,128)(2,1)S(1)} collective-permute-done((bf16[96,1536]{1,0:T(8,128)(2,1)S(1)}, bf16[96,1536]{1,0:T(8,128)(2,1)S(1)}, u32[]{:S(2)}, u32[]{:S(2)}) %collective-permute-start.1) | collective-permute-done | bytes 294944 | tf_op jit(solution)/shard_map/ppermute | solution.py:349
  21.1 2.5 %collective-permute-done.2 = bf16[96,1536]{1,0:T(8,128)(2,1)S(1)} collective-permute-done((bf16[96,1536]{1,0:T(8,128)(2,1)S(1)}, bf16[96,1536]{1,0:T(8,128)(2,1)S(1)}, u32[]{:S(2)}, u32[]{:S(2)}) %collective-permute-start.2) | collective-permute-done | bytes 294944 | tf_op jit(solution)/shard_map/ppermute | solution.py:349
  23.6 1.8 %collective-permute-done.3 = bf16[96,1536]{1,0:T(8,128)(2,1)S(1)} collective-permute-done((bf16[96,1536]{1,0:T(8,128)(2,1)S(1)}, bf16[96,1536]{1,0:T(8,128)(2,1)S(1)}, u32[]{:S(2)}, u32[]{:S(2)}) %collective-permute-start.3) | collective-permute-done | bytes 294944 | tf_op jit(solution)/shard_map/ppermute | solution.py:349
  25.5 2.8 %collective-permute-start.6 = (bf16[384,1536]{1,0:T(8,128)(2,1)S(1)}, bf16[384,1536]{1,0:T(8,128)(2,1)S(1)}, u32[]{:S(2)}, u32[]{:S(2)}) collective-permute-start(bf16[384,1536]{1,0:T(8,128)(2,1)S(1)} %constant_dynamic-update-slice_fusion.rest_0_), channel_id=1, source_target_pairs={{0,128},{1,33},{2,130},{3,35},{4,132},{5,37},{6,134},{7,39},{8,136... | collective-permute-start | bytes 3538952 | tf_op jit(solution)/shard_map/ppermute | solution.py:349
  28.3 0.9 collective-permute-start.5
  29.2 0.6 collective-permute-start.4
  29.8 0.8 dynamic_slice.9
  30.5 1.0 %dynamic-slice_bitcast_fusion = (bf16[1,3,64,256]{3,2,1,0:T(8,128)(2,1)S(1)}, bf16[1,3,64,256]{3,2,1,0:T(8,128)(2,1)S(1)}) fusion(bf16[24,64,256]{2,1,0:T(8,128)(2,1)} %param.14, s32[]{:T(128)S(6)} %select_n.31, bf16[24,64,256]{2,1,0:T(8,128)(2,1)} %param.13), kind=kLoop, calls=%fused_computation.4 | loop fusion | bytes 393220 | tf_op jit(solution)/shard_map/stack | solution.py:387
  31.5 0.7 pad_maximum_fusion.1.weights
  32.2 8.5 %all-to-all-done.x = bf16[8,64,1152]{2,1,0:T(8,128)(2,1)S(1)} async-done(((bf16[8,64,1152]{2,1,0:T(8,128)(2,1)}), bf16[8,64,1152]{2,1,0:T(8,128)(2,1)S(1)}, u32[]{:S(2)}, u32[]{:S(2)}) %all-to-all-start) | async-done | bytes 1179680 | tf_op jit(solution)/shard_map/all_to_all | solution.py:381
  40.7 0.9 %copy-done = bf16[2,3,64,256]{3,2,1,0:T(8,128)(2,1)S(1)} copy-done((bf16[2,3,64,256]{3,2,1,0:T(8,128)(2,1)S(1)}, bf16[2,3,64,256]{3,2,1,0:T(8,128)(2,1)}, u32[]{:S(2)}) %copy-start) | copy-done | bytes 196632
  41.7 23.2 %run_heads.1 = bf16[8,64,384]{2,1,0:T(8,128)(2,1)S(1)} custom-call(f32[24]{0:T(128)S(1)} %copy-done.2, bf16[8,64,1152]{2,1,0:T(8,128)(2,1)S(1)} %all-to-all-done.x, s32[1,1024]{1,0:T(1,128)S(1)} %copy-done.1, bf16[2,3,64,256]{3,2,1,0:T(8,128)(2,1)S(1)} %copy-done, f32[1,192]{1,0:T(1,128)S(1)} %bitcast.9), custom_call_target="tpu_custom_call" | custom-call | flops 4000000000 | bytes 100000000 | tf_op jit(solution)/shard_map/run_heads/pallas_call | solution.py:267
  64.9 0.0 collective-permute-done.6.rest_3_
  64.9 0.0 collective-permute-done.5.rest_2_
  64.9 0.0 collective-permute-done.4.rest_1_
  64.9 5.2 %collective-permute-start.7 = (bf16[384,1536]{1,0:T(8,128)(2,1)S(1)}, bf16[384,1536]{1,0:T(8,128)(2,1)S(1)}, u32[]{:S(2)}, u32[]{:S(2)}) collective-permute-start(bf16[384,1536]{1,0:T(8,128)(2,1)S(1)} %constant_dynamic-update-slice_fusion.rest_0_), channel_id=1, source_target_pairs={{0,1},{1,0},{2,3},{3,2},{4,5},{5,4},{6,7},{7,6},{8,9},{9,8},{10,11... | collective-permute-start | bytes 3538952 | tf_op jit(solution)/shard_map/ppermute | solution.py:349
  70.2 0.1 collective-permute-start.8
  70.3 0.4 collective-permute-start.9
  70.7 0.1 collective-permute-start.10
  70.8 16.5 %all_to_all.10.mixed = bf16[8,64,384]{2,1,0:T(8,128)(2,1)S(1)} all-to-all(bf16[8,64,384]{2,1,0:T(8,128)(2,1)S(1)} %run_heads.1), channel_id=1, replica_groups=mesh['dp'=32,'seq'=8] {'seq'}, dimensions={0} | all-to-all | bytes 786432 | tf_op jit(solution)/shard_map/all_to_all | solution.py:392
  87.3 0.0 collective-permute-done.7.rest_4_
  87.3 0.0 collective-permute-done.8.rest_5_
  87.3 0.0 collective-permute-done.9.rest_6_
  87.3 0.0 collective-permute-done.10.rest_7_
  87.3 4.2 %project_rows.1 = bf16[128,3072]{1,0:T(8,128)(2,1)} custom-call(bf16[8,64,384]{2,1,0:T(8,128)(2,1)S(1)} %all_to_all.10.mixed, bf16[384,1536]{1,0:T(8,128)(2,1)S(1)} %constant_dynamic-update-slice_fusion.rest_0_, bf16[384,1536]{1,0:T(8,128)(2,1)} %collective-permute-done.4.rest_1_, bf16[384,1536]{1,0:T(8,128)(2,1)} %collective-permute-done.5.rest_2_, ...), custom_call_target="tpu_custom_call" | custom-call | tf_op jit(solution)/shard_map/project_rows/pallas_call | solution.py:323
  (13 shorter events, 0.2 us)
Async XLA Ops:
  2.6 11.1 %collective-permute-start = (bf16[48,1536]{1,0:T(8,128)(2,1)}, bf16[48,1536]{1,0:T(8,128)(2,1)S(1)}, u32[]{:S(2)}, u32[]{:S(2)}) collective-permute-start(bf16[48,1536]{1,0:T(8,128)(2,1)} %get-tuple-element.15), channel_id=1, source_target_pairs={{0,8},{1,9},{2,10},{3,11},{4,12},{5,13},{6,14},{7,15},{8,0},{9,1},... | collective-permute-start | bytes 442376 | tf_op jit(solution)/shard_map/ppermute | solution.py:349
  5.1 8.7 %copy-start.3 = (bf16[48,1536]{1,0:T(8,128)(2,1)S(1)}, bf16[48,1536]{1,0:T(8,128)(2,1)}, u32[]{:S(2)}) copy-start(bf16[48,1536]{1,0:T(8,128)(2,1)} %get-tuple-element.15) | copy-start | bytes 442372
  5.1 35.6 %all-to-all-start = ((bf16[8,64,1152]{2,1,0:T(8,128)(2,1)}), bf16[8,64,1152]{2,1,0:T(8,128)(2,1)S(1)}, u32[]{:S(2)}, u32[]{:S(2)}) async-start(bf16[8,64,1152]{2,1,0:T(8,128)(2,1)} %get-tuple-element.14), calls=%async_computation | async-start | bytes 2359296 | tf_op jit(solution)/shard_map/all_to_all | solution.py:381
  13.9 7.2 %collective-permute-start.1 = (bf16[96,1536]{1,0:T(8,128)(2,1)S(1)}, bf16[96,1536]{1,0:T(8,128)(2,1)S(1)}, u32[]{:S(2)}, u32[]{:S(2)}) collective-permute-start(bf16[96,1536]{1,0:T(8,128)(2,1)S(1)} %pad_maximum_fusion), channel_id=1, source_target_pairs={{0,16},{1,65},{2,18},{3,67},{4,20},{5,69},{6,22},{7,71},{8,24},{9,... | collective-permute-start | bytes 884744 | tf_op jit(solution)/shard_map/ppermute | solution.py:349
  15.3 8.4 %collective-permute-start.2 = (bf16[96,1536]{1,0:T(8,128)(2,1)S(1)}, bf16[96,1536]{1,0:T(8,128)(2,1)S(1)}, u32[]{:S(2)}, u32[]{:S(2)}) collective-permute-start(bf16[96,1536]{1,0:T(8,128)(2,1)S(1)} %pad_maximum_fusion), channel_id=1, source_target_pairs={{0,48},{1,193},{2,50},{3,195},{4,52},{5,197},{6,54},{7,199},{8,56}... | collective-permute-start | bytes 884744 | tf_op jit(solution)/shard_map/ppermute | solution.py:349
  16.8 8.7 %collective-permute-start.3 = (bf16[96,1536]{1,0:T(8,128)(2,1)S(1)}, bf16[96,1536]{1,0:T(8,128)(2,1)S(1)}, u32[]{:S(2)}, u32[]{:S(2)}) collective-permute-start(bf16[96,1536]{1,0:T(8,128)(2,1)S(1)} %pad_maximum_fusion), channel_id=1, source_target_pairs={{0,32},{1,129},{2,34},{3,131},{4,36},{5,133},{6,38},{7,135},{8,40}... | collective-permute-start | bytes 884744 | tf_op jit(solution)/shard_map/ppermute | solution.py:349
  21.1 19.6 %copy-start.1 = (s32[1,1024]{1,0:T(1,128)S(1)}, s32[1,1024]{1,0:T(1,128)}, u32[]{:S(2)}) copy-start(s32[1,1024]{1,0:T(1,128)} %seg_ref.1) | copy-start | bytes 12292
  21.1 19.6 %copy-start.2 = (f32[24]{0:T(128)S(1)}, f32[24]{0:T(128)}, u32[]{:S(2)}) copy-start(f32[24]{0:T(128)} %rate_ref.1) | copy-start | bytes 292
  25.5 39.4 %collective-permute-start.6 = (bf16[384,1536]{1,0:T(8,128)(2,1)S(1)}, bf16[384,1536]{1,0:T(8,128)(2,1)S(1)}, u32[]{:S(2)}, u32[]{:S(2)}) collective-permute-start(bf16[384,1536]{1,0:T(8,128)(2,1)S(1)} %constant_dynamic-update-slice_fusion.rest_0_), channel_id=1, source_target_pairs={{0,128},{1,33},{2,130},{3,35},{4,132},{5,37},{6,134},{7,39},{8,136... | collective-permute-start | bytes 3538952 | tf_op jit(solution)/shard_map/ppermute | solution.py:349
  28.3 36.6 %collective-permute-start.5 = (bf16[384,1536]{1,0:T(8,128)(2,1)S(1)}, bf16[384,1536]{1,0:T(8,128)(2,1)}, u32[]{:S(2)}, u32[]{:S(2)}) collective-permute-start(bf16[384,1536]{1,0:T(8,128)(2,1)S(1)} %constant_dynamic-update-slice_fusion.rest_0_), channel_id=1, source_target_pairs={{0,192},{1,49},{2,194},{3,51},{4,196},{5,53},{6,198},{7,55},{8,200... | collective-permute-start | bytes 3538952 | tf_op jit(solution)/shard_map/ppermute | solution.py:349
  29.2 35.8 %collective-permute-start.4 = (bf16[384,1536]{1,0:T(8,128)(2,1)S(1)}, bf16[384,1536]{1,0:T(8,128)(2,1)}, u32[]{:S(2)}, u32[]{:S(2)}) collective-permute-start(bf16[384,1536]{1,0:T(8,128)(2,1)S(1)} %constant_dynamic-update-slice_fusion.rest_0_), channel_id=1, source_target_pairs={{0,64},{1,17},{2,66},{3,19},{4,68},{5,21},{6,70},{7,23},{8,72},{9,... | collective-permute-start | bytes 3538952 | tf_op jit(solution)/shard_map/ppermute | solution.py:349
  40.7 0.9 %copy-start = (bf16[2,3,64,256]{3,2,1,0:T(8,128)(2,1)S(1)}, bf16[2,3,64,256]{3,2,1,0:T(8,128)(2,1)}, u32[]{:S(2)}) copy-start(bf16[2,3,64,256]{3,2,1,0:T(8,128)(2,1)} %pad_maximum_fusion.1.weights) | copy-start | bytes 589828
  64.9 22.3 %collective-permute-start.7 = (bf16[384,1536]{1,0:T(8,128)(2,1)S(1)}, bf16[384,1536]{1,0:T(8,128)(2,1)S(1)}, u32[]{:S(2)}, u32[]{:S(2)}) collective-permute-start(bf16[384,1536]{1,0:T(8,128)(2,1)S(1)} %constant_dynamic-update-slice_fusion.rest_0_), channel_id=1, source_target_pairs={{0,1},{1,0},{2,3},{3,2},{4,5},{5,4},{6,7},{7,6},{8,9},{9,8},{10,11... | collective-permute-start | bytes 3538952 | tf_op jit(solution)/shard_map/ppermute | solution.py:349
  70.2 17.1 %collective-permute-start.8 = (bf16[384,1536]{1,0:T(8,128)(2,1)}, bf16[384,1536]{1,0:T(8,128)(2,1)S(1)}, u32[]{:S(2)}, u32[]{:S(2)}) collective-permute-start(bf16[384,1536]{1,0:T(8,128)(2,1)} %collective-permute-done.4.rest_1_), channel_id=1, source_target_pairs={{0,1},{1,0},{2,3},{3,2},{4,5},{5,4},{6,7},{7,6},{8,9},{9,8},{10,11... | collective-permute-start | bytes 3538952 | tf_op jit(solution)/shard_map/ppermute | solution.py:349
  70.3 17.0 %collective-permute-start.9 = (bf16[384,1536]{1,0:T(8,128)(2,1)}, bf16[384,1536]{1,0:T(8,128)(2,1)S(1)}, u32[]{:S(2)}, u32[]{:S(2)}) collective-permute-start(bf16[384,1536]{1,0:T(8,128)(2,1)} %collective-permute-done.5.rest_2_), channel_id=1, source_target_pairs={{0,1},{1,0},{2,3},{3,2},{4,5},{5,4},{6,7},{7,6},{8,9},{9,8},{10,11... | collective-permute-start | bytes 3538952 | tf_op jit(solution)/shard_map/ppermute | solution.py:349
  70.7 16.6 %collective-permute-start.10 = (bf16[384,1536]{1,0:T(8,128)(2,1)S(1)}, bf16[384,1536]{1,0:T(8,128)(2,1)S(1)}, u32[]{:S(2)}, u32[]{:S(2)}) collective-permute-start(bf16[384,1536]{1,0:T(8,128)(2,1)S(1)} %collective-permute-done.6.rest_3_), channel_id=1, source_target_pairs={{0,1},{1,0},{2,3},{3,2},{4,5},{5,4},{6,7},{7,6},{8,9},{9,8},{10,11... | collective-permute-start | bytes 3538952 | tf_op jit(solution)/shard_map/ppermute | solution.py:349

commit v4 on v3

--- a/solution.py
+++ b/solution.py
@@ -254,12 +254,13 @@
         one_block((source, 1), (ahead, 0), (source, 0))
         return carry
 
-    lax.fori_loop(0, PARTS, blocks, 0)
+    lax.fori_loop(0, PARTS, blocks, 0, unroll=2)
     query_last(query_first(), PARTS - 1, 1)
 
 
 VMEM = pl.BlockSpec(memory_space=pltpu.VMEM)
 SMEM = pl.BlockSpec(memory_space=pltpu.SMEM)
+HBM = pl.BlockSpec(memory_space=pltpu.HBM)
 
 
 def run_heads(rate, pieces, seg, weights, gate):
@@ -288,14 +289,17 @@
             pltpu.VMEM((WIDTH, WIDTH), bf16),
             pltpu.VMEM((1, WIDTH), f32),
         ],
-        compiler_params=pltpu.CompilerParams(vmem_limit_bytes=32 * MIB),
+        compiler_params=pltpu.CompilerParams(vmem_limit_bytes=20 * MIB),
         cost_estimate=pl.CostEstimate(flops=4_000_000_000, bytes_accessed=100_000_000, transcendentals=0),
         name="run_heads",
     )(rate, pieces, seg, weights, gate)
 
 
+STRIP = 512
+
+
 def project_kernel(mixed, *rest):
-    own, sib, out, groups = rest[:4], rest[4:8], rest[8], rest[9]
+    own, sib, out, groups, made, sems = rest[:4], rest[4:8], *rest[8:]
     core, dp = lax.rem(lax.axis_index("seq"), 2), lax.axis_index("dp")
     y, x = dp // 8, lax.rem(dp // 2, 4)
     for source in range(PARTS):
@@ -303,6 +307,7 @@
             for half in range(2):
                 at = half * WIDTH + pair * 2 * ROWS
                 groups[2 * source + pair, half * CH : (half + 1) * CH, :] = mixed[source, :, at : at + 2 * ROWS]
+    copies = []
     for side, blocks in enumerate((own, sib)):
         axis = core if side == 0 else 1 - core
         left = []
@@ -313,9 +318,15 @@
                 left.append(groups[lax.rem(y + 4 - dy, 4) * 4 + lax.rem(x + 4 - dx, 4)])
         left = jnp.concatenate(left, axis=1)
         wide = blocks[0].shape[1]
-        for at in range(0, wide, 256):
-            right = jnp.concatenate([block[:, at : at + 256] for block in blocks], axis=0)
-            out[:, pl.ds(pl.multiple_of(axis * wide + at, 256), 256)] = dot(left, right).astype(bf16)
+        for at in range(0, wide, STRIP):
+            right = jnp.concatenate([block[:, at : at + STRIP] for block in blocks], axis=0)
+            strip = slice(side * wide + at, side * wide + at + STRIP)
+            made[:, strip] = dot(left, right).astype(bf16)
+            to = pl.ds(pl.multiple_of(axis * wide + at, STRIP), STRIP)
+            copies.append(pltpu.make_async_copy(made.at[:, strip], out.at[:, to], sems.at[len(copies)]))
+            copies[-1].start()
+    for copy in copies:
+        copy.wait()
 
 
 def run_project(mixed, own, sib):
@@ -324,9 +335,13 @@
         project_kernel,
         out_shape=jax.ShapeDtypeStruct((TOK, 2 * wide), bf16),
         in_specs=[VMEM] * 9,
-        out_specs=VMEM,
-        scratch_shapes=[pltpu.VMEM((2 * PARTS, TOK, 2 * ROWS), bf16)],
-        compiler_params=pltpu.CompilerParams(vmem_limit_bytes=20 * MIB),
+        out_specs=HBM,
+        scratch_shapes=[
+            pltpu.VMEM((2 * PARTS, TOK, 2 * ROWS), bf16),
+            pltpu.VMEM((TOK, 2 * wide), bf16),
+            pltpu.SemaphoreType.DMA((2 * wide // STRIP,)),
+        ],
+        compiler_params=pltpu.CompilerParams(vmem_limit_bytes=16 * MIB),
         name="project_rows",
     )(mixed, *own, *sib)
 

time: 91.9 us -> 90.9 us (0.989)
  Pallas kernels: 30.1 us -> 29 us
    pallas_call x1, Pallas kernels: 23.2 us -> 22.3 us  [run_heads(): pl.pallas_call(heads_kernel, out_shape=jax.ShapeDtypeStruct((PARTS, CH, 2...]
where the time goes in v4:
time: 90.9 us; the launch traced here: 90.6 us
  Pallas kernels  29 us (32%)
  starting transfers between devices  25.7 us (28%)
  blocking collectives  16.5 us (18%)
  waiting for transfers between devices  15.6 us (17%)
  local copies, waits for them, and re-layouts  2.72 us (3%)
    pallas_call x1, Pallas kernels, run_heads(): pl.pallas_call(heads_kernel, out_shape=jax.ShapeDtypeStruct((PARTS, CH, 2...  22.3 us
    ppermute x11, starting transfers between devices, move(): return lax.ppermute(array, ('dp', 'seq'), pairs)  17 us
    all_to_all x1, blocking collectives, on_device(): lax.all_to_all(mixed, 'seq', split_axis=0, concat_axis=0, tiled=True)  16.5 us
    all_to_all x1, starting transfers between devices, on_device(): lax.all_to_all(pieces, 'seq', split_axis=0, concat_axis=0, tiled=True)  8.64 us
    all_to_all x1, waiting for transfers between devices, on_device(): lax.all_to_all(pieces, 'seq', split_axis=0, concat_axis=0, tiled=True)  8.54 us
    ppermute x11, waiting for transfers between devices, move(): return lax.ppermute(array, ('dp', 'seq'), pairs)  7.07 us
    pallas_call x1, Pallas kernels, run_project(): pl.pallas_call(project_kernel, out_shape=jax.ShapeDtypeStruct((TOK, 2 * w...  4.05 us
    pallas_call x1, Pallas kernels, pack(): pl.pallas_call(pack_kernel, out_shape=[jax.ShapeDtypeStruct((PARTS, CH, 6...  2.64 us
  transfers between devices with their start and end apart: 12, of which 4 were waited for; matrix products, arithmetic and copies ran while one was open for 3% of the time, Pallas kernels for 25%

profile of v4, /device:TPU:1, one launch (start us, length us, event | category | flops | bytes accessed | tf_op | source)
XLA Modules:
  0.0 90.6 jit_solution(2128022938386364765)
XLA Ops:
  0.0 2.6 %pack_rows.1 = (bf16[8,64,1152]{2,1,0:T(8,128)(2,1)}, bf16[48,1536]{1,0:T(8,128)(2,1)}) custom-call(bf16[128,1536]{1,0:T(8,128)(2,1)} %bitcast.10, bf16[128,1536]{1,0:T(8,128)(2,1)} %bitcast.11, bf16[128,1536]{1,0:T(8,128)(2,1)} %bitcast.12, bf16[48,3072]{1,0:T(8,128)(2,1)} %weight_ref.1), custom_call_target="tpu_custom_call" | custom-call | tf_op jit(solution)/shard_map/pack_rows/pallas_call | solution.py:60
  2.6 2.5 %collective-permute-start = (bf16[48,1536]{1,0:T(8,128)(2,1)}, bf16[48,1536]{1,0:T(8,128)(2,1)S(1)}, u32[]{:S(2)}, u32[]{:S(2)}) collective-permute-start(bf16[48,1536]{1,0:T(8,128)(2,1)} %get-tuple-element.15), channel_id=1, source_target_pairs={{0,8},{1,9},{2,10},{3,11},{4,12},{5,13},{6,14},{7,15},{8,0},{9,1},... | collective-permute-start | bytes 442376 | tf_op jit(solution)/shard_map/ppermute | solution.py:364
  5.1 8.6 %all-to-all-start = ((bf16[8,64,1152]{2,1,0:T(8,128)(2,1)}), bf16[8,64,1152]{2,1,0:T(8,128)(2,1)S(1)}, u32[]{:S(2)}, u32[]{:S(2)}) async-start(bf16[8,64,1152]{2,1,0:T(8,128)(2,1)} %get-tuple-element.14), calls=%async_computation | async-start | bytes 2359296 | tf_op jit(solution)/shard_map/all_to_all | solution.py:396
  13.8 0.0 collective-permute-done
  13.9 1.4 %collective-permute-start.1 = (bf16[96,1536]{1,0:T(8,128)(2,1)S(1)}, bf16[96,1536]{1,0:T(8,128)(2,1)S(1)}, u32[]{:S(2)}, u32[]{:S(2)}) collective-permute-start(bf16[96,1536]{1,0:T(8,128)(2,1)S(1)} %pad_maximum_fusion), channel_id=1, source_target_pairs={{0,16},{1,65},{2,18},{3,67},{4,20},{5,69},{6,22},{7,71},{8,24},{9,... | collective-permute-start | bytes 884744 | tf_op jit(solution)/shard_map/ppermute | solution.py:364
  15.3 1.5 %collective-permute-start.2 = (bf16[96,1536]{1,0:T(8,128)(2,1)S(1)}, bf16[96,1536]{1,0:T(8,128)(2,1)S(1)}, u32[]{:S(2)}, u32[]{:S(2)}) collective-permute-start(bf16[96,1536]{1,0:T(8,128)(2,1)S(1)} %pad_maximum_fusion), channel_id=1, source_target_pairs={{0,48},{1,193},{2,50},{3,195},{4,52},{5,197},{6,54},{7,199},{8,56}... | collective-permute-start | bytes 884744 | tf_op jit(solution)/shard_map/ppermute | solution.py:364
  16.8 1.6 %collective-permute-start.3 = (bf16[96,1536]{1,0:T(8,128)(2,1)S(1)}, bf16[96,1536]{1,0:T(8,128)(2,1)S(1)}, u32[]{:S(2)}, u32[]{:S(2)}) collective-permute-start(bf16[96,1536]{1,0:T(8,128)(2,1)S(1)} %pad_maximum_fusion), channel_id=1, source_target_pairs={{0,32},{1,129},{2,34},{3,131},{4,36},{5,133},{6,38},{7,135},{8,40}... | collective-permute-start | bytes 884744 | tf_op jit(solution)/shard_map/ppermute | solution.py:364
  18.3 2.8 %collective-permute-done.1 = bf16[96,1536]{1,0:T(8,128)(2,1)S(1)} collective-permute-done((bf16[96,1536]{1,0:T(8,128)(2,1)S(1)}, bf16[96,1536]{1,0:T(8,128)(2,1)S(1)}, u32[]{:S(2)}, u32[]{:S(2)}) %collective-permute-start.1) | collective-permute-done | bytes 294944 | tf_op jit(solution)/shard_map/ppermute | solution.py:364
  21.1 2.5 %collective-permute-done.2 = bf16[96,1536]{1,0:T(8,128)(2,1)S(1)} collective-permute-done((bf16[96,1536]{1,0:T(8,128)(2,1)S(1)}, bf16[96,1536]{1,0:T(8,128)(2,1)S(1)}, u32[]{:S(2)}, u32[]{:S(2)}) %collective-permute-start.2) | collective-permute-done | bytes 294944 | tf_op jit(solution)/shard_map/ppermute | solution.py:364
  23.6 1.8 %collective-permute-done.3 = bf16[96,1536]{1,0:T(8,128)(2,1)S(1)} collective-permute-done((bf16[96,1536]{1,0:T(8,128)(2,1)S(1)}, bf16[96,1536]{1,0:T(8,128)(2,1)S(1)}, u32[]{:S(2)}, u32[]{:S(2)}) %collective-permute-start.3) | collective-permute-done | bytes 294944 | tf_op jit(solution)/shard_map/ppermute | solution.py:364
  25.5 2.8 %collective-permute-start.6 = (bf16[384,1536]{1,0:T(8,128)(2,1)S(1)}, bf16[384,1536]{1,0:T(8,128)(2,1)S(1)}, u32[]{:S(2)}, u32[]{:S(2)}) collective-permute-start(bf16[384,1536]{1,0:T(8,128)(2,1)S(1)} %constant_dynamic-update-slice_fusion.rest_0_), channel_id=1, source_target_pairs={{0,128},{1,33},{2,130},{3,35},{4,132},{5,37},{6,134},{7,39},{8,136... | collective-permute-start | bytes 3538952 | tf_op jit(solution)/shard_map/ppermute | solution.py:364
  28.3 0.9 collective-permute-start.5
  29.2 0.6 collective-permute-start.4
  29.8 0.8 dynamic_slice.9
  30.5 1.0 %dynamic-slice_bitcast_fusion = (bf16[1,3,64,256]{3,2,1,0:T(8,128)(2,1)S(1)}, bf16[1,3,64,256]{3,2,1,0:T(8,128)(2,1)S(1)}) fusion(bf16[24,64,256]{2,1,0:T(8,128)(2,1)} %param.14, s32[]{:T(128)S(6)} %select_n.31, bf16[24,64,256]{2,1,0:T(8,128)(2,1)} %param.13), kind=kLoop, calls=%fused_computation.4 | loop fusion | bytes 393220 | tf_op jit(solution)/shard_map/stack | solution.py:402
  31.5 0.7 pad_maximum_fusion.1.weights
  32.2 8.5 %all-to-all-done.x = bf16[8,64,1152]{2,1,0:T(8,128)(2,1)S(1)} async-done(((bf16[8,64,1152]{2,1,0:T(8,128)(2,1)}), bf16[8,64,1152]{2,1,0:T(8,128)(2,1)S(1)}, u32[]{:S(2)}, u32[]{:S(2)}) %all-to-all-start) | async-done | bytes 1179680 | tf_op jit(solution)/shard_map/all_to_all | solution.py:396
  40.7 0.9 %copy-done = bf16[2,3,64,256]{3,2,1,0:T(8,128)(2,1)S(1)} copy-done((bf16[2,3,64,256]{3,2,1,0:T(8,128)(2,1)S(1)}, bf16[2,3,64,256]{3,2,1,0:T(8,128)(2,1)}, u32[]{:S(2)}) %copy-start) | copy-done | bytes 196632
  41.7 22.3 %run_heads.1 = bf16[8,64,384]{2,1,0:T(8,128)(2,1)S(1)} custom-call(f32[24]{0:T(128)S(1)} %copy-done.2, bf16[8,64,1152]{2,1,0:T(8,128)(2,1)S(1)} %all-to-all-done.x, s32[1,1024]{1,0:T(1,128)S(1)} %copy-done.1, bf16[2,3,64,256]{3,2,1,0:T(8,128)(2,1)S(1)} %copy-done, f32[1,192]{1,0:T(1,128)S(1)} %bitcast.9), custom_call_target="tpu_custom_call" | custom-call | flops 4000000000 | bytes 100000000 | tf_op jit(solution)/shard_map/run_heads/pallas_call | solution.py:268
  64.0 0.0 collective-permute-done.6.rest_3_
  64.0 0.0 collective-permute-done.5.rest_2_
  64.0 0.0 collective-permute-done.4.rest_1_
  64.0 5.2 %collective-permute-start.7 = (bf16[384,1536]{1,0:T(8,128)(2,1)S(1)}, bf16[384,1536]{1,0:T(8,128)(2,1)S(1)}, u32[]{:S(2)}, u32[]{:S(2)}) collective-permute-start(bf16[384,1536]{1,0:T(8,128)(2,1)S(1)} %constant_dynamic-update-slice_fusion.rest_0_), channel_id=1, source_target_pairs={{0,1},{1,0},{2,3},{3,2},{4,5},{5,4},{6,7},{7,6},{8,9},{9,8},{10,11... | collective-permute-start | bytes 3538952 | tf_op jit(solution)/shard_map/ppermute | solution.py:364
  69.2 0.1 collective-permute-start.8
  69.3 0.4 collective-permute-start.9
  69.7 0.1 collective-permute-start.10
  69.8 16.5 %all_to_all.10.mixed = bf16[8,64,384]{2,1,0:T(8,128)(2,1)S(1)} all-to-all(bf16[8,64,384]{2,1,0:T(8,128)(2,1)S(1)} %run_heads.1), channel_id=1, replica_groups=mesh['dp'=32,'seq'=8] {'seq'}, dimensions={0} | all-to-all | bytes 786432 | tf_op jit(solution)/shard_map/all_to_all | solution.py:407
  86.3 0.0 collective-permute-done.7.rest_4_
  86.3 0.0 collective-permute-done.8.rest_5_
  86.3 0.0 collective-permute-done.9.rest_6_
  86.3 0.0 collective-permute-done.10.rest_7_
  86.4 4.0 %project_rows.1 = bf16[128,3072]{1,0:T(8,128)(2,1)} custom-call(bf16[8,64,384]{2,1,0:T(8,128)(2,1)S(1)} %all_to_all.10.mixed, bf16[384,1536]{1,0:T(8,128)(2,1)S(1)} %constant_dynamic-update-slice_fusion.rest_0_, bf16[384,1536]{1,0:T(8,128)(2,1)} %collective-permute-done.4.rest_1_, bf16[384,1536]{1,0:T(8,128)(2,1)} %collective-permute-done.5.rest_2_, ...), custom_call_target="tpu_custom_call" | custom-call | tf_op jit(solution)/shard_map/project_rows/pallas_call | solution.py:334
  (13 shorter events, 0.2 us)
Async XLA Ops:
  2.6 11.1 %collective-permute-start = (bf16[48,1536]{1,0:T(8,128)(2,1)}, bf16[48,1536]{1,0:T(8,128)(2,1)S(1)}, u32[]{:S(2)}, u32[]{:S(2)}) collective-permute-start(bf16[48,1536]{1,0:T(8,128)(2,1)} %get-tuple-element.15), channel_id=1, source_target_pairs={{0,8},{1,9},{2,10},{3,11},{4,12},{5,13},{6,14},{7,15},{8,0},{9,1},... | collective-permute-start | bytes 442376 | tf_op jit(solution)/shard_map/ppermute | solution.py:364
  5.1 8.7 %copy-start.3 = (bf16[48,1536]{1,0:T(8,128)(2,1)S(1)}, bf16[48,1536]{1,0:T(8,128)(2,1)}, u32[]{:S(2)}) copy-start(bf16[48,1536]{1,0:T(8,128)(2,1)} %get-tuple-element.15) | copy-start | bytes 442372
  5.1 35.6 %all-to-all-start = ((bf16[8,64,1152]{2,1,0:T(8,128)(2,1)}), bf16[8,64,1152]{2,1,0:T(8,128)(2,1)S(1)}, u32[]{:S(2)}, u32[]{:S(2)}) async-start(bf16[8,64,1152]{2,1,0:T(8,128)(2,1)} %get-tuple-element.14), calls=%async_computation | async-start | bytes 2359296 | tf_op jit(solution)/shard_map/all_to_all | solution.py:396
  13.9 7.2 %collective-permute-start.1 = (bf16[96,1536]{1,0:T(8,128)(2,1)S(1)}, bf16[96,1536]{1,0:T(8,128)(2,1)S(1)}, u32[]{:S(2)}, u32[]{:S(2)}) collective-permute-start(bf16[96,1536]{1,0:T(8,128)(2,1)S(1)} %pad_maximum_fusion), channel_id=1, source_target_pairs={{0,16},{1,65},{2,18},{3,67},{4,20},{5,69},{6,22},{7,71},{8,24},{9,... | collective-permute-start | bytes 884744 | tf_op jit(solution)/shard_map/ppermute | solution.py:364
  15.3 8.4 %collective-permute-start.2 = (bf16[96,1536]{1,0:T(8,128)(2,1)S(1)}, bf16[96,1536]{1,0:T(8,128)(2,1)S(1)}, u32[]{:S(2)}, u32[]{:S(2)}) collective-permute-start(bf16[96,1536]{1,0:T(8,128)(2,1)S(1)} %pad_maximum_fusion), channel_id=1, source_target_pairs={{0,48},{1,193},{2,50},{3,195},{4,52},{5,197},{6,54},{7,199},{8,56}... | collective-permute-start | bytes 884744 | tf_op jit(solution)/shard_map/ppermute | solution.py:364
  16.8 8.7 %collective-permute-start.3 = (bf16[96,1536]{1,0:T(8,128)(2,1)S(1)}, bf16[96,1536]{1,0:T(8,128)(2,1)S(1)}, u32[]{:S(2)}, u32[]{:S(2)}) collective-permute-start(bf16[96,1536]{1,0:T(8,128)(2,1)S(1)} %pad_maximum_fusion), channel_id=1, source_target_pairs={{0,32},{1,129},{2,34},{3,131},{4,36},{5,133},{6,38},{7,135},{8,40}... | collective-permute-start | bytes 884744 | tf_op jit(solution)/shard_map/ppermute | solution.py:364
  21.1 19.6 %copy-start.1 = (s32[1,1024]{1,0:T(1,128)S(1)}, s32[1,1024]{1,0:T(1,128)}, u32[]{:S(2)}) copy-start(s32[1,1024]{1,0:T(1,128)} %seg_ref.1) | copy-start | bytes 12292
  21.1 19.6 %copy-start.2 = (f32[24]{0:T(128)S(1)}, f32[24]{0:T(128)}, u32[]{:S(2)}) copy-start(f32[24]{0:T(128)} %rate_ref.1) | copy-start | bytes 292
  25.5 38.5 %collective-permute-start.6 = (bf16[384,1536]{1,0:T(8,128)(2,1)S(1)}, bf16[384,1536]{1,0:T(8,128)(2,1)S(1)}, u32[]{:S(2)}, u32[]{:S(2)}) collective-permute-start(bf16[384,1536]{1,0:T(8,128)(2,1)S(1)} %constant_dynamic-update-slice_fusion.rest_0_), channel_id=1, source_target_pairs={{0,128},{1,33},{2,130},{3,35},{4,132},{5,37},{6,134},{7,39},{8,136... | collective-permute-start | bytes 3538952 | tf_op jit(solution)/shard_map/ppermute | solution.py:364
  28.3 35.7 %collective-permute-start.5 = (bf16[384,1536]{1,0:T(8,128)(2,1)S(1)}, bf16[384,1536]{1,0:T(8,128)(2,1)}, u32[]{:S(2)}, u32[]{:S(2)}) collective-permute-start(bf16[384,1536]{1,0:T(8,128)(2,1)S(1)} %constant_dynamic-update-slice_fusion.rest_0_), channel_id=1, source_target_pairs={{0,192},{1,49},{2,194},{3,51},{4,196},{5,53},{6,198},{7,55},{8,200... | collective-permute-start | bytes 3538952 | tf_op jit(solution)/shard_map/ppermute | solution.py:364
  29.2 34.8 %collective-permute-start.4 = (bf16[384,1536]{1,0:T(8,128)(2,1)S(1)}, bf16[384,1536]{1,0:T(8,128)(2,1)}, u32[]{:S(2)}, u32[]{:S(2)}) collective-permute-start(bf16[384,1536]{1,0:T(8,128)(2,1)S(1)} %constant_dynamic-update-slice_fusion.rest_0_), channel_id=1, source_target_pairs={{0,64},{1,17},{2,66},{3,19},{4,68},{5,21},{6,70},{7,23},{8,72},{9,... | collective-permute-start | bytes 3538952 | tf_op jit(solution)/shard_map/ppermute | solution.py:364
  40.7 0.9 %copy-start = (bf16[2,3,64,256]{3,2,1,0:T(8,128)(2,1)S(1)}, bf16[2,3,64,256]{3,2,1,0:T(8,128)(2,1)}, u32[]{:S(2)}) copy-start(bf16[2,3,64,256]{3,2,1,0:T(8,128)(2,1)} %pad_maximum_fusion.1.weights) | copy-start | bytes 589828
  64.0 22.3 %collective-permute-start.7 = (bf16[384,1536]{1,0:T(8,128)(2,1)S(1)}, bf16[384,1536]{1,0:T(8,128)(2,1)S(1)}, u32[]{:S(2)}, u32[]{:S(2)}) collective-permute-start(bf16[384,1536]{1,0:T(8,128)(2,1)S(1)} %constant_dynamic-update-slice_fusion.rest_0_), channel_id=1, source_target_pairs={{0,1},{1,0},{2,3},{3,2},{4,5},{5,4},{6,7},{7,6},{8,9},{9,8},{10,11... | collective-permute-start | bytes 3538952 | tf_op jit(solution)/shard_map/ppermute | solution.py:364
  69.2 17.1 %collective-permute-start.8 = (bf16[384,1536]{1,0:T(8,128)(2,1)}, bf16[384,1536]{1,0:T(8,128)(2,1)S(1)}, u32[]{:S(2)}, u32[]{:S(2)}) collective-permute-start(bf16[384,1536]{1,0:T(8,128)(2,1)} %collective-permute-done.4.rest_1_), channel_id=1, source_target_pairs={{0,1},{1,0},{2,3},{3,2},{4,5},{5,4},{6,7},{7,6},{8,9},{9,8},{10,11... | collective-permute-start | bytes 3538952 | tf_op jit(solution)/shard_map/ppermute | solution.py:364
  69.3 17.0 %collective-permute-start.9 = (bf16[384,1536]{1,0:T(8,128)(2,1)}, bf16[384,1536]{1,0:T(8,128)(2,1)S(1)}, u32[]{:S(2)}, u32[]{:S(2)}) collective-permute-start(bf16[384,1536]{1,0:T(8,128)(2,1)} %collective-permute-done.5.rest_2_), channel_id=1, source_target_pairs={{0,1},{1,0},{2,3},{3,2},{4,5},{5,4},{6,7},{7,6},{8,9},{9,8},{10,11... | collective-permute-start | bytes 3538952 | tf_op jit(solution)/shard_map/ppermute | solution.py:364
  69.7 16.6 %collective-permute-start.10 = (bf16[384,1536]{1,0:T(8,128)(2,1)S(1)}, bf16[384,1536]{1,0:T(8,128)(2,1)S(1)}, u32[]{:S(2)}, u32[]{:S(2)}) collective-permute-start(bf16[384,1536]{1,0:T(8,128)(2,1)S(1)} %collective-permute-done.6.rest_3_), channel_id=1, source_target_pairs={{0,1},{1,0},{2,3},{3,2},{4,5},{5,4},{6,7},{7,6},{8,9},{9,8},{10,11... | collective-permute-start | bytes 3538952 | tf_op jit(solution)/shard_map/ppermute | solution.py:364

commit v5 on v4

--- a/solution.py
+++ b/solution.py
@@ -107,7 +107,7 @@
 def heads_kernel(
     rate_ref, x, seg_ref, weights, gate_ref, mixed,
     q_low, k_low, q_wide, k_wide, xq, target, attended, w1s, w2s, b1s, b2s, z1s, q1s, a_prev,
-    w2_prev, g2_prev, b2_prev,
+    w2_prev, g2_prev, b2_prev, summed,
 ):
     me = lax.axis_index("seq")
     heads = range(LOCAL)
@@ -135,19 +135,22 @@
         return x[:, :, at : at + HD].reshape(half_rows, HD)
 
     ones = jnp.ones((half_rows, HD), bf16)
-    for h in heads:
-        keys = [jnp.concatenate([columns(1, h, half), segs[half]], axis=1) for half in range(2)]
-        values = [jnp.concatenate([columns(2, h, half), ones], axis=1) for half in range(2)]
-        keys, values = jnp.concatenate(keys, axis=0), jnp.concatenate(values, axis=0)
-        for half in range(2):
-            q = jnp.concatenate([(columns(0, h, half) * 0.125).astype(bf16), segs[half]], axis=1)
-            scores = dot_nt(q, keys)
-            top = jnp.max(scores, axis=-1, keepdims=True)
-            got = dot(jnp.exp(scores - top).astype(bf16), values)
-            got = got[:, :HD] / got[:, HD:]
-            attended[:, half, :, h * HD : (h + 1) * HD] = got.reshape(PARTS, CH, HD)
-
-    for begin in range(0, PARTS, BATCH):
+    gathered = {}
+
+    def attend(h, half):
+        if h not in gathered:
+            keys = [jnp.concatenate([columns(1, h, part), segs[part]], axis=1) for part in range(2)]
+            values = [jnp.concatenate([columns(2, h, part), ones], axis=1) for part in range(2)]
+            gathered[h] = jnp.concatenate(keys, axis=0), jnp.concatenate(values, axis=0)
+        keys, values = gathered[h]
+        q = jnp.concatenate([(columns(0, h, half) * 0.125).astype(bf16), segs[half]], axis=1)
+        scores = dot_nt(q, keys)
+        top = jnp.max(scores, axis=-1, keepdims=True)
+        got = dot(jnp.exp(scores - top).astype(bf16), values)
+        got = got[:, :HD] / got[:, HD:]
+        attended[:, half, :, h * HD : (h + 1) * HD] = got.reshape(PARTS, CH, HD)
+
+    def prepare(begin):
         some = slice(begin, begin + BATCH)
         for half in range(2):
             q, k, v = (
@@ -170,6 +173,8 @@
                 q_wide[h, some, half] = wide[: BATCH * CH].reshape(per_block)
                 k_wide[h, some, half] = wide[BATCH * CH :].reshape(per_block)
 
+    prepare(0)
+
     def project(h, state, bias, wide):
         high, low = halves(state)
         return dot(wide, jnp.concatenate([high, high, low], axis=0)) + bias
@@ -197,7 +202,7 @@
         near = jnp.where(causal, join_heads(near) + 1.0, 0.0).astype(bf16)
         out = join_heads(deep[:WIDTH] + deep[WIDTH:]) + bias - dot(near, grad)
         inner = xq[source, half] + out * lax.rsqrt(head_means(out * out, spread) + EPS)
-        mixed[source, :, half * WIDTH : (half + 1) * WIDTH] = (attended[source, half] + gate * inner).astype(bf16)
+        summed[source, half] = gate * inner
 
     def one_block(now, later, before):
         z1, w1_now, w2_now, b1, b2 = z1s[...], w1s[...], w2s[...], b1s[...], b2s[...]
@@ -248,14 +253,18 @@
         w2s[...] = new_w2
         b2s[...] = new_b2
 
-    def blocks(source, carry):
-        last, ahead = jnp.maximum(source - 1, 0), jnp.minimum(source + 1, PARTS - 1)
+    units = [(h, half) for h in heads for half in range(2)]
+    for source in range(PARTS):
+        last, ahead = max(source - 1, 0), min(source + 1, PARTS - 1)
         one_block((source, 0), (source, 1), (last, 1))
+        if ahead % BATCH == 0 and ahead > source:
+            prepare(ahead)
         one_block((source, 1), (ahead, 0), (source, 0))
-        return carry
-
-    lax.fori_loop(0, PARTS, blocks, 0, unroll=2)
+        if source < len(units):
+            attend(*units[source])
     query_last(query_first(), PARTS - 1, 1)
+    for half in range(2):
+        mixed[:, :, half * WIDTH : (half + 1) * WIDTH] = (attended[:, half] + summed[:, half]).astype(bf16)
 
 
 VMEM = pl.BlockSpec(memory_space=pltpu.VMEM)
@@ -288,6 +297,7 @@
             pltpu.VMEM((WIDTH, FFI), bf16),
             pltpu.VMEM((WIDTH, WIDTH), bf16),
             pltpu.VMEM((1, WIDTH), f32),
+            pltpu.VMEM(blocks, f32),
         ],
         compiler_params=pltpu.CompilerParams(vmem_limit_bytes=20 * MIB),
         cost_estimate=pl.CostEstimate(flops=4_000_000_000, bytes_accessed=100_000_000, transcendentals=0),

time: 90.9 us -> 89.5 us (0.985)
  Pallas kernels: 29 us -> 27.6 us
    pallas_call x1, Pallas kernels: 22.3 us -> 20.9 us  [run_heads(): pl.pallas_call(heads_kernel, out_shape=jax.ShapeDtypeStruct((PARTS, CH, 2...]
  transfers between devices with their start and end apart: 12 -> 12, of which waited for: 4 -> 4; matrix products, arithmetic and copies ran while one was open for 3% -> 3% of each run, Pallas kernels for 25% -> 23%
where the time goes in v5:
time: 89.5 us; the launch traced here: 89.2 us
  Pallas kernels  27.6 us (31%)
  starting transfers between devices  25.7 us (29%)
  blocking collectives  16.5 us (18%)
  waiting for transfers between devices  15.6 us (17%)
  local copies, waits for them, and re-layouts  2.72 us (3%)
    pallas_call x1, Pallas kernels, run_heads(): pl.pallas_call(heads_kernel, out_shape=jax.ShapeDtypeStruct((PARTS, CH, 2...  20.9 us
    ppermute x11, starting transfers between devices, move(): return lax.ppermute(array, ('dp', 'seq'), pairs)  17 us
    all_to_all x1, blocking collectives, on_device(): lax.all_to_all(mixed, 'seq', split_axis=0, concat_axis=0, tiled=True)  16.5 us
    all_to_all x1, starting transfers between devices, on_device(): lax.all_to_all(pieces, 'seq', split_axis=0, concat_axis=0, tiled=True)  8.64 us
    all_to_all x1, waiting for transfers between devices, on_device(): lax.all_to_all(pieces, 'seq', split_axis=0, concat_axis=0, tiled=True)  8.54 us
    ppermute x11, waiting for transfers between devices, move(): return lax.ppermute(array, ('dp', 'seq'), pairs)  7.07 us
    pallas_call x1, Pallas kernels, run_project(): pl.pallas_call(project_kernel, out_shape=jax.ShapeDtypeStruct((TOK, 2 * w...  4.05 us
    pallas_call x1, Pallas kernels, pack(): pl.pallas_call(pack_kernel, out_shape=[jax.ShapeDtypeStruct((PARTS, CH, 6...  2.64 us
  transfers between devices with their start and end apart: 12, of which 4 were waited for; matrix products, arithmetic and copies ran while one was open for 3% of the time, Pallas kernels for 23%

profile of v5, /device:TPU:1, one launch (start us, length us, event | category | flops | bytes accessed | tf_op | source)
XLA Modules:
  0.0 89.2 jit_solution(14388691493464684065)
XLA Ops:
  0.0 2.6 %pack_rows.1 = (bf16[8,64,1152]{2,1,0:T(8,128)(2,1)}, bf16[48,1536]{1,0:T(8,128)(2,1)}) custom-call(bf16[128,1536]{1,0:T(8,128)(2,1)} %bitcast.10, bf16[128,1536]{1,0:T(8,128)(2,1)} %bitcast.11, bf16[128,1536]{1,0:T(8,128)(2,1)} %bitcast.12, bf16[48,3072]{1,0:T(8,128)(2,1)} %weight_ref.1), custom_call_target="tpu_custom_call" | custom-call | tf_op jit(solution)/shard_map/pack_rows/pallas_call | solution.py:60
  2.6 2.5 %collective-permute-start = (bf16[48,1536]{1,0:T(8,128)(2,1)}, bf16[48,1536]{1,0:T(8,128)(2,1)S(1)}, u32[]{:S(2)}, u32[]{:S(2)}) collective-permute-start(bf16[48,1536]{1,0:T(8,128)(2,1)} %get-tuple-element.15), channel_id=1, source_target_pairs={{0,8},{1,9},{2,10},{3,11},{4,12},{5,13},{6,14},{7,15},{8,0},{9,1},... | collective-permute-start | bytes 442376 | tf_op jit(solution)/shard_map/ppermute | solution.py:374
  5.1 8.6 %all-to-all-start = ((bf16[8,64,1152]{2,1,0:T(8,128)(2,1)}), bf16[8,64,1152]{2,1,0:T(8,128)(2,1)S(1)}, u32[]{:S(2)}, u32[]{:S(2)}) async-start(bf16[8,64,1152]{2,1,0:T(8,128)(2,1)} %get-tuple-element.14), calls=%async_computation | async-start | bytes 2359296 | tf_op jit(solution)/shard_map/all_to_all | solution.py:406
  13.8 0.0 collective-permute-done
  13.9 1.4 %collective-permute-start.1 = (bf16[96,1536]{1,0:T(8,128)(2,1)S(1)}, bf16[96,1536]{1,0:T(8,128)(2,1)S(1)}, u32[]{:S(2)}, u32[]{:S(2)}) collective-permute-start(bf16[96,1536]{1,0:T(8,128)(2,1)S(1)} %pad_maximum_fusion), channel_id=1, source_target_pairs={{0,16},{1,65},{2,18},{3,67},{4,20},{5,69},{6,22},{7,71},{8,24},{9,... | collective-permute-start | bytes 884744 | tf_op jit(solution)/shard_map/ppermute | solution.py:374
  15.3 1.5 %collective-permute-start.2 = (bf16[96,1536]{1,0:T(8,128)(2,1)S(1)}, bf16[96,1536]{1,0:T(8,128)(2,1)S(1)}, u32[]{:S(2)}, u32[]{:S(2)}) collective-permute-start(bf16[96,1536]{1,0:T(8,128)(2,1)S(1)} %pad_maximum_fusion), channel_id=1, source_target_pairs={{0,48},{1,193},{2,50},{3,195},{4,52},{5,197},{6,54},{7,199},{8,56}... | collective-permute-start | bytes 884744 | tf_op jit(solution)/shard_map/ppermute | solution.py:374
  16.8 1.6 %collective-permute-start.3 = (bf16[96,1536]{1,0:T(8,128)(2,1)S(1)}, bf16[96,1536]{1,0:T(8,128)(2,1)S(1)}, u32[]{:S(2)}, u32[]{:S(2)}) collective-permute-start(bf16[96,1536]{1,0:T(8,128)(2,1)S(1)} %pad_maximum_fusion), channel_id=1, source_target_pairs={{0,32},{1,129},{2,34},{3,131},{4,36},{5,133},{6,38},{7,135},{8,40}... | collective-permute-start | bytes 884744 | tf_op jit(solution)/shard_map/ppermute | solution.py:374
  18.3 2.8 %collective-permute-done.1 = bf16[96,1536]{1,0:T(8,128)(2,1)S(1)} collective-permute-done((bf16[96,1536]{1,0:T(8,128)(2,1)S(1)}, bf16[96,1536]{1,0:T(8,128)(2,1)S(1)}, u32[]{:S(2)}, u32[]{:S(2)}) %collective-permute-start.1) | collective-permute-done | bytes 294944 | tf_op jit(solution)/shard_map/ppermute | solution.py:374
  21.1 2.5 %collective-permute-done.2 = bf16[96,1536]{1,0:T(8,128)(2,1)S(1)} collective-permute-done((bf16[96,1536]{1,0:T(8,128)(2,1)S(1)}, bf16[96,1536]{1,0:T(8,128)(2,1)S(1)}, u32[]{:S(2)}, u32[]{:S(2)}) %collective-permute-start.2) | collective-permute-done | bytes 294944 | tf_op jit(solution)/shard_map/ppermute | solution.py:374
  23.6 1.8 %collective-permute-done.3 = bf16[96,1536]{1,0:T(8,128)(2,1)S(1)} collective-permute-done((bf16[96,1536]{1,0:T(8,128)(2,1)S(1)}, bf16[96,1536]{1,0:T(8,128)(2,1)S(1)}, u32[]{:S(2)}, u32[]{:S(2)}) %collective-permute-start.3) | collective-permute-done | bytes 294944 | tf_op jit(solution)/shard_map/ppermute | solution.py:374
  25.5 2.8 %collective-permute-start.6 = (bf16[384,1536]{1,0:T(8,128)(2,1)S(1)}, bf16[384,1536]{1,0:T(8,128)(2,1)S(1)}, u32[]{:S(2)}, u32[]{:S(2)}) collective-permute-start(bf16[384,1536]{1,0:T(8,128)(2,1)S(1)} %constant_dynamic-update-slice_fusion.rest_0_), channel_id=1, source_target_pairs={{0,128},{1,33},{2,130},{3,35},{4,132},{5,37},{6,134},{7,39},{8,136... | collective-permute-start | bytes 3538952 | tf_op jit(solution)/shard_map/ppermute | solution.py:374
  28.3 0.9 collective-permute-start.5
  29.2 0.6 collective-permute-start.4
  29.8 0.8 dynamic_slice.9
  30.5 1.0 %dynamic-slice_bitcast_fusion = (bf16[1,3,64,256]{3,2,1,0:T(8,128)(2,1)S(1)}, bf16[1,3,64,256]{3,2,1,0:T(8,128)(2,1)S(1)}) fusion(bf16[24,64,256]{2,1,0:T(8,128)(2,1)} %param.14, s32[]{:T(128)S(6)} %select_n.31, bf16[24,64,256]{2,1,0:T(8,128)(2,1)} %param.13), kind=kLoop, calls=%fused_computation.4 | loop fusion | bytes 393220 | tf_op jit(solution)/shard_map/stack | solution.py:412
  31.5 0.7 pad_maximum_fusion.1.weights
  32.2 8.5 %all-to-all-done.x = bf16[8,64,1152]{2,1,0:T(8,128)(2,1)S(1)} async-done(((bf16[8,64,1152]{2,1,0:T(8,128)(2,1)}), bf16[8,64,1152]{2,1,0:T(8,128)(2,1)S(1)}, u32[]{:S(2)}, u32[]{:S(2)}) %all-to-all-start) | async-done | bytes 1179680 | tf_op jit(solution)/shard_map/all_to_all | solution.py:406
  40.7 0.9 %copy-done = bf16[2,3,64,256]{3,2,1,0:T(8,128)(2,1)S(1)} copy-done((bf16[2,3,64,256]{3,2,1,0:T(8,128)(2,1)S(1)}, bf16[2,3,64,256]{3,2,1,0:T(8,128)(2,1)}, u32[]{:S(2)}) %copy-start) | copy-done | bytes 196632
  41.7 20.9 %run_heads.1 = bf16[8,64,384]{2,1,0:T(8,128)(2,1)S(1)} custom-call(f32[24]{0:T(128)S(1)} %copy-done.2, bf16[8,64,1152]{2,1,0:T(8,128)(2,1)S(1)} %all-to-all-done.x, s32[1,1024]{1,0:T(1,128)S(1)} %copy-done.1, bf16[2,3,64,256]{3,2,1,0:T(8,128)(2,1)S(1)} %copy-done, f32[1,192]{1,0:T(1,128)S(1)} %bitcast.9), custom_call_target="tpu_custom_call" | custom-call | flops 4000000000 | bytes 100000000 | tf_op jit(solution)/shard_map/run_heads/pallas_call | solution.py:277
  62.5 0.0 collective-permute-done.6.rest_3_
  62.5 0.0 collective-permute-done.5.rest_2_
  62.6 0.0 collective-permute-done.4.rest_1_
  62.6 5.2 %collective-permute-start.7 = (bf16[384,1536]{1,0:T(8,128)(2,1)S(1)}, bf16[384,1536]{1,0:T(8,128)(2,1)S(1)}, u32[]{:S(2)}, u32[]{:S(2)}) collective-permute-start(bf16[384,1536]{1,0:T(8,128)(2,1)S(1)} %constant_dynamic-update-slice_fusion.rest_0_), channel_id=1, source_target_pairs={{0,1},{1,0},{2,3},{3,2},{4,5},{5,4},{6,7},{7,6},{8,9},{9,8},{10,11... | collective-permute-start | bytes 3538952 | tf_op jit(solution)/shard_map/ppermute | solution.py:374
  67.8 0.1 collective-permute-start.8
  67.9 0.4 collective-permute-start.9
  68.3 0.1 collective-permute-start.10
  68.4 16.5 %all_to_all.10.mixed = bf16[8,64,384]{2,1,0:T(8,128)(2,1)S(1)} all-to-all(bf16[8,64,384]{2,1,0:T(8,128)(2,1)S(1)} %run_heads.1), channel_id=1, replica_groups=mesh['dp'=32,'seq'=8] {'seq'}, dimensions={0} | all-to-all | bytes 786432 | tf_op jit(solution)/shard_map/all_to_all | solution.py:417
  84.9 0.0 collective-permute-done.7.rest_4_
  84.9 0.0 collective-permute-done.8.rest_5_
  84.9 0.0 collective-permute-done.9.rest_6_
  84.9 0.0 collective-permute-done.10.rest_7_
  84.9 4.1 %project_rows.1 = bf16[128,3072]{1,0:T(8,128)(2,1)} custom-call(bf16[8,64,384]{2,1,0:T(8,128)(2,1)S(1)} %all_to_all.10.mixed, bf16[384,1536]{1,0:T(8,128)(2,1)S(1)} %constant_dynamic-update-slice_fusion.rest_0_, bf16[384,1536]{1,0:T(8,128)(2,1)} %collective-permute-done.4.rest_1_, bf16[384,1536]{1,0:T(8,128)(2,1)} %collective-permute-done.5.rest_2_, ...), custom_call_target="tpu_custom_call" | custom-call | tf_op jit(solution)/shard_map/project_rows/pallas_call | solution.py:344
  (13 shorter events, 0.2 us)
Async XLA Ops:
  2.6 11.1 %collective-permute-start = (bf16[48,1536]{1,0:T(8,128)(2,1)}, bf16[48,1536]{1,0:T(8,128)(2,1)S(1)}, u32[]{:S(2)}, u32[]{:S(2)}) collective-permute-start(bf16[48,1536]{1,0:T(8,128)(2,1)} %get-tuple-element.15), channel_id=1, source_target_pairs={{0,8},{1,9},{2,10},{3,11},{4,12},{5,13},{6,14},{7,15},{8,0},{9,1},... | collective-permute-start | bytes 442376 | tf_op jit(solution)/shard_map/ppermute | solution.py:374
  5.1 8.7 %copy-start.3 = (bf16[48,1536]{1,0:T(8,128)(2,1)S(1)}, bf16[48,1536]{1,0:T(8,128)(2,1)}, u32[]{:S(2)}) copy-start(bf16[48,1536]{1,0:T(8,128)(2,1)} %get-tuple-element.15) | copy-start | bytes 442372
  5.1 35.6 %all-to-all-start = ((bf16[8,64,1152]{2,1,0:T(8,128)(2,1)}), bf16[8,64,1152]{2,1,0:T(8,128)(2,1)S(1)}, u32[]{:S(2)}, u32[]{:S(2)}) async-start(bf16[8,64,1152]{2,1,0:T(8,128)(2,1)} %get-tuple-element.14), calls=%async_computation | async-start | bytes 2359296 | tf_op jit(solution)/shard_map/all_to_all | solution.py:406
  13.9 7.2 %collective-permute-start.1 = (bf16[96,1536]{1,0:T(8,128)(2,1)S(1)}, bf16[96,1536]{1,0:T(8,128)(2,1)S(1)}, u32[]{:S(2)}, u32[]{:S(2)}) collective-permute-start(bf16[96,1536]{1,0:T(8,128)(2,1)S(1)} %pad_maximum_fusion), channel_id=1, source_target_pairs={{0,16},{1,65},{2,18},{3,67},{4,20},{5,69},{6,22},{7,71},{8,24},{9,... | collective-permute-start | bytes 884744 | tf_op jit(solution)/shard_map/ppermute | solution.py:374
  15.3 8.4 %collective-permute-start.2 = (bf16[96,1536]{1,0:T(8,128)(2,1)S(1)}, bf16[96,1536]{1,0:T(8,128)(2,1)S(1)}, u32[]{:S(2)}, u32[]{:S(2)}) collective-permute-start(bf16[96,1536]{1,0:T(8,128)(2,1)S(1)} %pad_maximum_fusion), channel_id=1, source_target_pairs={{0,48},{1,193},{2,50},{3,195},{4,52},{5,197},{6,54},{7,199},{8,56}... | collective-permute-start | bytes 884744 | tf_op jit(solution)/shard_map/ppermute | solution.py:374
  16.8 8.7 %collective-permute-start.3 = (bf16[96,1536]{1,0:T(8,128)(2,1)S(1)}, bf16[96,1536]{1,0:T(8,128)(2,1)S(1)}, u32[]{:S(2)}, u32[]{:S(2)}) collective-permute-start(bf16[96,1536]{1,0:T(8,128)(2,1)S(1)} %pad_maximum_fusion), channel_id=1, source_target_pairs={{0,32},{1,129},{2,34},{3,131},{4,36},{5,133},{6,38},{7,135},{8,40}... | collective-permute-start | bytes 884744 | tf_op jit(solution)/shard_map/ppermute | solution.py:374
  21.1 19.6 %copy-start.1 = (s32[1,1024]{1,0:T(1,128)S(1)}, s32[1,1024]{1,0:T(1,128)}, u32[]{:S(2)}) copy-start(s32[1,1024]{1,0:T(1,128)} %seg_ref.1) | copy-start | bytes 12292
  21.1 19.6 %copy-start.2 = (f32[24]{0:T(128)S(1)}, f32[24]{0:T(128)}, u32[]{:S(2)}) copy-start(f32[24]{0:T(128)} %rate_ref.1) | copy-start | bytes 292
  25.5 37.1 %collective-permute-start.6 = (bf16[384,1536]{1,0:T(8,128)(2,1)S(1)}, bf16[384,1536]{1,0:T(8,128)(2,1)S(1)}, u32[]{:S(2)}, u32[]{:S(2)}) collective-permute-start(bf16[384,1536]{1,0:T(8,128)(2,1)S(1)} %constant_dynamic-update-slice_fusion.rest_0_), channel_id=1, source_target_pairs={{0,128},{1,33},{2,130},{3,35},{4,132},{5,37},{6,134},{7,39},{8,136... | collective-permute-start | bytes 3538952 | tf_op jit(solution)/shard_map/ppermute | solution.py:374
  28.3 34.3 %collective-permute-start.5 = (bf16[384,1536]{1,0:T(8,128)(2,1)S(1)}, bf16[384,1536]{1,0:T(8,128)(2,1)}, u32[]{:S(2)}, u32[]{:S(2)}) collective-permute-start(bf16[384,1536]{1,0:T(8,128)(2,1)S(1)} %constant_dynamic-update-slice_fusion.rest_0_), channel_id=1, source_target_pairs={{0,192},{1,49},{2,194},{3,51},{4,196},{5,53},{6,198},{7,55},{8,200... | collective-permute-start | bytes 3538952 | tf_op jit(solution)/shard_map/ppermute | solution.py:374
  29.2 33.4 %collective-permute-start.4 = (bf16[384,1536]{1,0:T(8,128)(2,1)S(1)}, bf16[384,1536]{1,0:T(8,128)(2,1)}, u32[]{:S(2)}, u32[]{:S(2)}) collective-permute-start(bf16[384,1536]{1,0:T(8,128)(2,1)S(1)} %constant_dynamic-update-slice_fusion.rest_0_), channel_id=1, source_target_pairs={{0,64},{1,17},{2,66},{3,19},{4,68},{5,21},{6,70},{7,23},{8,72},{9,... | collective-permute-start | bytes 3538952 | tf_op jit(solution)/shard_map/ppermute | solution.py:374
  40.7 0.9 %copy-start = (bf16[2,3,64,256]{3,2,1,0:T(8,128)(2,1)S(1)}, bf16[2,3,64,256]{3,2,1,0:T(8,128)(2,1)}, u32[]{:S(2)}) copy-start(bf16[2,3,64,256]{3,2,1,0:T(8,128)(2,1)} %pad_maximum_fusion.1.weights) | copy-start | bytes 589828
  62.6 22.3 %collective-permute-start.7 = (bf16[384,1536]{1,0:T(8,128)(2,1)S(1)}, bf16[384,1536]{1,0:T(8,128)(2,1)S(1)}, u32[]{:S(2)}, u32[]{:S(2)}) collective-permute-start(bf16[384,1536]{1,0:T(8,128)(2,1)S(1)} %constant_dynamic-update-slice_fusion.rest_0_), channel_id=1, source_target_pairs={{0,1},{1,0},{2,3},{3,2},{4,5},{5,4},{6,7},{7,6},{8,9},{9,8},{10,11... | collective-permute-start | bytes 3538952 | tf_op jit(solution)/shard_map/ppermute | solution.py:374
  67.8 17.1 %collective-permute-start.8 = (bf16[384,1536]{1,0:T(8,128)(2,1)}, bf16[384,1536]{1,0:T(8,128)(2,1)S(1)}, u32[]{:S(2)}, u32[]{:S(2)}) collective-permute-start(bf16[384,1536]{1,0:T(8,128)(2,1)} %collective-permute-done.4.rest_1_), channel_id=1, source_target_pairs={{0,1},{1,0},{2,3},{3,2},{4,5},{5,4},{6,7},{7,6},{8,9},{9,8},{10,11... | collective-permute-start | bytes 3538952 | tf_op jit(solution)/shard_map/ppermute | solution.py:374
  67.9 17.0 %collective-permute-start.9 = (bf16[384,1536]{1,0:T(8,128)(2,1)}, bf16[384,1536]{1,0:T(8,128)(2,1)S(1)}, u32[]{:S(2)}, u32[]{:S(2)}) collective-permute-start(bf16[384,1536]{1,0:T(8,128)(2,1)} %collective-permute-done.5.rest_2_), channel_id=1, source_target_pairs={{0,1},{1,0},{2,3},{3,2},{4,5},{5,4},{6,7},{7,6},{8,9},{9,8},{10,11... | collective-permute-start | bytes 3538952 | tf_op jit(solution)/shard_map/ppermute | solution.py:374
  68.3 16.6 %collective-permute-start.10 = (bf16[384,1536]{1,0:T(8,128)(2,1)S(1)}, bf16[384,1536]{1,0:T(8,128)(2,1)S(1)}, u32[]{:S(2)}, u32[]{:S(2)}) collective-permute-start(bf16[384,1536]{1,0:T(8,128)(2,1)S(1)} %collective-permute-done.6.rest_3_), channel_id=1, source_target_pairs={{0,1},{1,0},{2,3},{3,2},{4,5},{5,4},{6,7},{7,6},{8,9},{9,8},{10,11... | collective-permute-start | bytes 3538952 | tf_op jit(solution)/shard_map/ppermute | solution.py:374

commit v6 on v5

--- a/solution.py
+++ b/solution.py
@@ -106,8 +106,7 @@
 
 def heads_kernel(
     rate_ref, x, seg_ref, weights, gate_ref, mixed,
-    q_low, k_low, q_wide, k_wide, xq, target, attended, w1s, w2s, b1s, b2s, z1s, q1s, a_prev,
-    w2_prev, g2_prev, b2_prev, summed,
+    q_low, k_low, q_wide, k_wide, xq, target, attended, summed,
 ):
     me = lax.axis_index("seq")
     heads = range(LOCAL)
@@ -179,23 +178,29 @@
         high, low = halves(state)
         return dot(wide, jnp.concatenate([high, high, low], axis=0)) + bias
 
-    for h in heads:
-        at = slice(h * HD, (h + 1) * HD)
-        start = weights[1, h].astype(f32)
-        w2s[at, :] = start - jnp.mean(start, axis=0, keepdims=True)
-        first = weights[0, h]
-        w1s[at, :] = first.astype(f32)
-        z1s[at, :] = dot(k_wide[h, 0, 0], jnp.concatenate([first, first, jnp.zeros_like(first)], axis=0))
-    for ref in (b1s, b2s, q1s, a_prev, w2_prev, g2_prev, b2_prev):
-        ref[...] = jnp.zeros_like(ref)
+    starts = [weights[1, h].astype(f32) for h in heads]
+    firsts = [weights[0, h] for h in heads]
+    state = (
+        jnp.concatenate(
+            [
+                dot(k_wide[h, 0, 0], jnp.concatenate([firsts[h], firsts[h], jnp.zeros_like(firsts[h])], axis=0))
+                for h in heads
+            ],
+            axis=0,
+        ),
+        jnp.concatenate(firsts, axis=0).astype(f32),
+        jnp.concatenate([start - jnp.mean(start, axis=0, keepdims=True) for start in starts], axis=0),
+        [jnp.zeros((1, FFI), f32) for h in heads],
+        jnp.zeros((1, WIDTH), f32),
+    )
 
     gate = jnp.tanh(gate_ref[...])
 
-    def query_first():
-        high, low = halves(gelu_parts(q1s[...], False)[0])
-        near = dot_nt(high, a_prev[...])
-        deep = dot_nt(jnp.concatenate([high, low], axis=0), w2_prev[...])
-        return near, deep, g2_prev[...], b2_prev[...]
+    def query_first(q1, act_low, w2_low, grad_low, bias):
+        high, low = halves(gelu_parts(q1, False)[0])
+        near = dot_nt(high, act_low)
+        deep = dot_nt(jnp.concatenate([high, low], axis=0), w2_low)
+        return near, deep, grad_low, bias
 
     def query_last(state, source, half):
         near, deep, grad, bias = state
@@ -204,10 +209,10 @@
         inner = xq[source, half] + out * lax.rsqrt(head_means(out * out, spread) + EPS)
         summed[source, half] = gate * inner
 
-    def one_block(now, later, before):
-        z1, w1_now, w2_now, b1, b2 = z1s[...], w1s[...], w2s[...], b1s[...], b2s[...]
+    def one_block(state, held, now, later, before):
+        z1, w1_now, w2_now, b1, b2 = state
         goal = target[*now]
-        query = query_first()
+        query = query_first(*held) if held else None
 
         keys = stack_heads(k_low[*now])
         cross = dot_nt(jnp.concatenate([q_low[*now], k_low[*later]], axis=0), keys) + 1.0
@@ -238,31 +243,25 @@
         new_w1 = w1_now - dot_tn(keys, deep_low)
         new_b2 = b2 - jnp.sum(grad, axis=0, keepdims=True)
         new_b1 = [b1[h] - jnp.sum(deep[h * CH : (h + 1) * CH], axis=0, keepdims=True) for h in heads]
-        query_last(query, *before)
-
-        for h in heads:
-            both = ahead[h] - moved[2 * h * CH : 2 * (h + 1) * CH]
-            q1s[h * CH : (h + 1) * CH, :] = both[:CH]
-            z1s[h * CH : (h + 1) * CH, :] = both[CH:]
-            b1s[h] = new_b1[h]
-        a_prev[...] = act_low
-        w2_prev[...] = w2_low
-        g2_prev[...] = grad_low
-        b2_prev[...] = b2
-        w1s[...] = new_w1
-        w2s[...] = new_w2
-        b2s[...] = new_b2
+        if held:
+            query_last(query, *before)
+
+        both = [ahead[h] - moved[2 * h * CH : 2 * (h + 1) * CH] for h in heads]
+        q1 = jnp.concatenate([rows[:CH] for rows in both], axis=0)
+        z1 = jnp.concatenate([rows[CH:] for rows in both], axis=0)
+        return (z1, new_w1, new_w2, new_b1, new_b2), (q1, act_low, w2_low, grad_low, b2)
 
     units = [(h, half) for h in heads for half in range(2)]
+    held = None
     for source in range(PARTS):
         last, ahead = max(source - 1, 0), min(source + 1, PARTS - 1)
-        one_block((source, 0), (source, 1), (last, 1))
+        state, held = one_block(state, held, (source, 0), (source, 1), (last, 1))
         if ahead % BATCH == 0 and ahead > source:
             prepare(ahead)
-        one_block((source, 1), (ahead, 0), (source, 0))
+        state, held = one_block(state, held, (source, 1), (ahead, 0), (source, 0))
         if source < len(units):
             attend(*units[source])
-    query_last(query_first(), PARTS - 1, 1)
+    query_last(query_first(*held), PARTS - 1, 1)
     for half in range(2):
         mixed[:, :, half * WIDTH : (half + 1) * WIDTH] = (attended[:, half] + summed[:, half]).astype(bf16)
 
@@ -287,16 +286,6 @@
             pltpu.VMEM(blocks, f32),
             pltpu.VMEM(blocks, f32),
             pltpu.VMEM(blocks, f32),
-            pltpu.VMEM((WIDTH, FFI), f32),
-            pltpu.VMEM((WIDTH, FFI), f32),
-            pltpu.VMEM((LOCAL, 1, FFI), f32),
-            pltpu.VMEM((1, WIDTH), f32),
-            pltpu.VMEM((WIDTH, FFI), f32),
-            pltpu.VMEM((WIDTH, FFI), f32),
-            pltpu.VMEM((WIDTH, FFI), bf16),
-            pltpu.VMEM((WIDTH, FFI), bf16),
-            pltpu.VMEM((WIDTH, WIDTH), bf16),
-            pltpu.VMEM((1, WIDTH), f32),
             pltpu.VMEM(blocks, f32),
         ],
         compiler_params=pltpu.CompilerParams(vmem_limit_bytes=20 * MIB),

time: 89.5 us -> 89.6 us (level)
  no operation moved by 1% of the time
where the time goes in v6:
time: 89.6 us; the launch traced here: 89.2 us
  Pallas kernels  27.6 us (31%)
  starting transfers between devices  25.7 us (29%)
  blocking collectives  16.5 us (18%)
  waiting for transfers between devices  15.6 us (17%)
  local copies, waits for them, and re-layouts  2.72 us (3%)
    pallas_call x1, Pallas kernels, run_heads(): pl.pallas_call(heads_kernel, out_shape=jax.ShapeDtypeStruct((PARTS, CH, 2...  20.9 us
    ppermute x11, starting transfers between devices, move(): return lax.ppermute(array, ('dp', 'seq'), pairs)  17 us
    all_to_all x1, blocking collectives, on_device(): lax.all_to_all(mixed, 'seq', split_axis=0, concat_axis=0, tiled=True)  16.5 us
    all_to_all x1, starting transfers between devices, on_device(): lax.all_to_all(pieces, 'seq', split_axis=0, concat_axis=0, tiled=True)  8.64 us
    all_to_all x1, waiting for transfers between devices, on_device(): lax.all_to_all(pieces, 'seq', split_axis=0, concat_axis=0, tiled=True)  8.54 us
    ppermute x11, waiting for transfers between devices, move(): return lax.ppermute(array, ('dp', 'seq'), pairs)  7.07 us
    pallas_call x1, Pallas kernels, run_project(): pl.pallas_call(project_kernel, out_shape=jax.ShapeDtypeStruct((TOK, 2 * w...  4.05 us
    pallas_call x1, Pallas kernels, pack(): pl.pallas_call(pack_kernel, out_shape=[jax.ShapeDtypeStruct((PARTS, CH, 6...  2.64 us
  transfers between devices with their start and end apart: 12, of which 4 were waited for; matrix products, arithmetic and copies ran while one was open for 3% of the time, Pallas kernels for 23%

profile of v6, /device:TPU:1, one launch (start us, length us, event | category | flops | bytes accessed | tf_op | source)
XLA Modules:
  0.0 89.2 jit_solution(6336583954186214989)
XLA Ops:
  0.0 2.6 %pack_rows.1 = (bf16[8,64,1152]{2,1,0:T(8,128)(2,1)}, bf16[48,1536]{1,0:T(8,128)(2,1)}) custom-call(bf16[128,1536]{1,0:T(8,128)(2,1)} %bitcast.10, bf16[128,1536]{1,0:T(8,128)(2,1)} %bitcast.11, bf16[128,1536]{1,0:T(8,128)(2,1)} %bitcast.12, bf16[48,3072]{1,0:T(8,128)(2,1)} %weight_ref.1), custom_call_target="tpu_custom_call" | custom-call | tf_op jit(solution)/shard_map/pack_rows/pallas_call | solution.py:60
  2.6 2.5 %collective-permute-start = (bf16[48,1536]{1,0:T(8,128)(2,1)}, bf16[48,1536]{1,0:T(8,128)(2,1)S(1)}, u32[]{:S(2)}, u32[]{:S(2)}) collective-permute-start(bf16[48,1536]{1,0:T(8,128)(2,1)} %get-tuple-element.15), channel_id=1, source_target_pairs={{0,8},{1,9},{2,10},{3,11},{4,12},{5,13},{6,14},{7,15},{8,0},{9,1},... | collective-permute-start | bytes 442376 | tf_op jit(solution)/shard_map/ppermute | solution.py:363
  5.1 8.6 %all-to-all-start = ((bf16[8,64,1152]{2,1,0:T(8,128)(2,1)}), bf16[8,64,1152]{2,1,0:T(8,128)(2,1)S(1)}, u32[]{:S(2)}, u32[]{:S(2)}) async-start(bf16[8,64,1152]{2,1,0:T(8,128)(2,1)} %get-tuple-element.14), calls=%async_computation | async-start | bytes 2359296 | tf_op jit(solution)/shard_map/all_to_all | solution.py:395
  13.8 0.0 collective-permute-done
  13.9 1.4 %collective-permute-start.1 = (bf16[96,1536]{1,0:T(8,128)(2,1)S(1)}, bf16[96,1536]{1,0:T(8,128)(2,1)S(1)}, u32[]{:S(2)}, u32[]{:S(2)}) collective-permute-start(bf16[96,1536]{1,0:T(8,128)(2,1)S(1)} %pad_maximum_fusion), channel_id=1, source_target_pairs={{0,16},{1,65},{2,18},{3,67},{4,20},{5,69},{6,22},{7,71},{8,24},{9,... | collective-permute-start | bytes 884744 | tf_op jit(solution)/shard_map/ppermute | solution.py:363
  15.3 1.5 %collective-permute-start.2 = (bf16[96,1536]{1,0:T(8,128)(2,1)S(1)}, bf16[96,1536]{1,0:T(8,128)(2,1)S(1)}, u32[]{:S(2)}, u32[]{:S(2)}) collective-permute-start(bf16[96,1536]{1,0:T(8,128)(2,1)S(1)} %pad_maximum_fusion), channel_id=1, source_target_pairs={{0,48},{1,193},{2,50},{3,195},{4,52},{5,197},{6,54},{7,199},{8,56}... | collective-permute-start | bytes 884744 | tf_op jit(solution)/shard_map/ppermute | solution.py:363
  16.8 1.6 %collective-permute-start.3 = (bf16[96,1536]{1,0:T(8,128)(2,1)S(1)}, bf16[96,1536]{1,0:T(8,128)(2,1)S(1)}, u32[]{:S(2)}, u32[]{:S(2)}) collective-permute-start(bf16[96,1536]{1,0:T(8,128)(2,1)S(1)} %pad_maximum_fusion), channel_id=1, source_target_pairs={{0,32},{1,129},{2,34},{3,131},{4,36},{5,133},{6,38},{7,135},{8,40}... | collective-permute-start | bytes 884744 | tf_op jit(solution)/shard_map/ppermute | solution.py:363
  18.3 2.8 %collective-permute-done.1 = bf16[96,1536]{1,0:T(8,128)(2,1)S(1)} collective-permute-done((bf16[96,1536]{1,0:T(8,128)(2,1)S(1)}, bf16[96,1536]{1,0:T(8,128)(2,1)S(1)}, u32[]{:S(2)}, u32[]{:S(2)}) %collective-permute-start.1) | collective-permute-done | bytes 294944 | tf_op jit(solution)/shard_map/ppermute | solution.py:363
  21.1 2.5 %collective-permute-done.2 = bf16[96,1536]{1,0:T(8,128)(2,1)S(1)} collective-permute-done((bf16[96,1536]{1,0:T(8,128)(2,1)S(1)}, bf16[96,1536]{1,0:T(8,128)(2,1)S(1)}, u32[]{:S(2)}, u32[]{:S(2)}) %collective-permute-start.2) | collective-permute-done | bytes 294944 | tf_op jit(solution)/shard_map/ppermute | solution.py:363
  23.6 1.8 %collective-permute-done.3 = bf16[96,1536]{1,0:T(8,128)(2,1)S(1)} collective-permute-done((bf16[96,1536]{1,0:T(8,128)(2,1)S(1)}, bf16[96,1536]{1,0:T(8,128)(2,1)S(1)}, u32[]{:S(2)}, u32[]{:S(2)}) %collective-permute-start.3) | collective-permute-done | bytes 294944 | tf_op jit(solution)/shard_map/ppermute | solution.py:363
  25.5 2.8 %collective-permute-start.6 = (bf16[384,1536]{1,0:T(8,128)(2,1)S(1)}, bf16[384,1536]{1,0:T(8,128)(2,1)S(1)}, u32[]{:S(2)}, u32[]{:S(2)}) collective-permute-start(bf16[384,1536]{1,0:T(8,128)(2,1)S(1)} %constant_dynamic-update-slice_fusion.rest_0_), channel_id=1, source_target_pairs={{0,128},{1,33},{2,130},{3,35},{4,132},{5,37},{6,134},{7,39},{8,136... | collective-permute-start | bytes 3538952 | tf_op jit(solution)/shard_map/ppermute | solution.py:363
  28.3 0.9 collective-permute-start.5
  29.2 0.6 collective-permute-start.4
  29.8 0.8 dynamic_slice.9
  30.5 1.0 %dynamic-slice_bitcast_fusion = (bf16[1,3,64,256]{3,2,1,0:T(8,128)(2,1)S(1)}, bf16[1,3,64,256]{3,2,1,0:T(8,128)(2,1)S(1)}) fusion(bf16[24,64,256]{2,1,0:T(8,128)(2,1)} %param.14, s32[]{:T(128)S(6)} %select_n.31, bf16[24,64,256]{2,1,0:T(8,128)(2,1)} %param.13), kind=kLoop, calls=%fused_computation.4 | loop fusion | bytes 393220 | tf_op jit(solution)/shard_map/stack | solution.py:401
  31.5 0.7 pad_maximum_fusion.1.weights
  32.2 8.5 %all-to-all-done.x = bf16[8,64,1152]{2,1,0:T(8,128)(2,1)S(1)} async-done(((bf16[8,64,1152]{2,1,0:T(8,128)(2,1)}), bf16[8,64,1152]{2,1,0:T(8,128)(2,1)S(1)}, u32[]{:S(2)}, u32[]{:S(2)}) %all-to-all-start) | async-done | bytes 1179680 | tf_op jit(solution)/shard_map/all_to_all | solution.py:395
  40.7 0.9 %copy-done = bf16[2,3,64,256]{3,2,1,0:T(8,128)(2,1)S(1)} copy-done((bf16[2,3,64,256]{3,2,1,0:T(8,128)(2,1)S(1)}, bf16[2,3,64,256]{3,2,1,0:T(8,128)(2,1)}, u32[]{:S(2)}) %copy-start) | copy-done | bytes 196632
  41.7 20.9 %run_heads.1 = bf16[8,64,384]{2,1,0:T(8,128)(2,1)S(1)} custom-call(f32[24]{0:T(128)S(1)} %copy-done.2, bf16[8,64,1152]{2,1,0:T(8,128)(2,1)S(1)} %all-to-all-done.x, s32[1,1024]{1,0:T(1,128)S(1)} %copy-done.1, bf16[2,3,64,256]{3,2,1,0:T(8,128)(2,1)S(1)} %copy-done, f32[1,192]{1,0:T(1,128)S(1)} %bitcast.9), custom_call_target="tpu_custom_call" | custom-call | flops 4000000000 | bytes 100000000 | tf_op jit(solution)/shard_map/run_heads/pallas_call | solution.py:276
  62.6 0.0 collective-permute-done.6.rest_3_
  62.6 0.0 collective-permute-done.5.rest_2_
  62.6 0.0 collective-permute-done.4.rest_1_
  62.6 5.2 %collective-permute-start.7 = (bf16[384,1536]{1,0:T(8,128)(2,1)S(1)}, bf16[384,1536]{1,0:T(8,128)(2,1)S(1)}, u32[]{:S(2)}, u32[]{:S(2)}) collective-permute-start(bf16[384,1536]{1,0:T(8,128)(2,1)S(1)} %constant_dynamic-update-slice_fusion.rest_0_), channel_id=1, source_target_pairs={{0,1},{1,0},{2,3},{3,2},{4,5},{5,4},{6,7},{7,6},{8,9},{9,8},{10,11... | collective-permute-start | bytes 3538952 | tf_op jit(solution)/shard_map/ppermute | solution.py:363
  67.8 0.1 collective-permute-start.8
  67.9 0.4 collective-permute-start.9
  68.4 0.1 collective-permute-start.10
  68.5 16.5 %all_to_all.10.mixed = bf16[8,64,384]{2,1,0:T(8,128)(2,1)S(1)} all-to-all(bf16[8,64,384]{2,1,0:T(8,128)(2,1)S(1)} %run_heads.1), channel_id=1, replica_groups=mesh['dp'=32,'seq'=8] {'seq'}, dimensions={0} | all-to-all | bytes 786432 | tf_op jit(solution)/shard_map/all_to_all | solution.py:406
  85.0 0.0 collective-permute-done.7.rest_4_
  85.0 0.0 collective-permute-done.8.rest_5_
  85.0 0.0 collective-permute-done.9.rest_6_
  85.0 0.0 collective-permute-done.10.rest_7_
  85.0 4.0 %project_rows.1 = bf16[128,3072]{1,0:T(8,128)(2,1)} custom-call(bf16[8,64,384]{2,1,0:T(8,128)(2,1)S(1)} %all_to_all.10.mixed, bf16[384,1536]{1,0:T(8,128)(2,1)S(1)} %constant_dynamic-update-slice_fusion.rest_0_, bf16[384,1536]{1,0:T(8,128)(2,1)} %collective-permute-done.4.rest_1_, bf16[384,1536]{1,0:T(8,128)(2,1)} %collective-permute-done.5.rest_2_, ...), custom_call_target="tpu_custom_call" | custom-call | tf_op jit(solution)/shard_map/project_rows/pallas_call | solution.py:333
  (13 shorter events, 0.2 us)
Async XLA Ops:
  2.6 11.1 %collective-permute-start = (bf16[48,1536]{1,0:T(8,128)(2,1)}, bf16[48,1536]{1,0:T(8,128)(2,1)S(1)}, u32[]{:S(2)}, u32[]{:S(2)}) collective-permute-start(bf16[48,1536]{1,0:T(8,128)(2,1)} %get-tuple-element.15), channel_id=1, source_target_pairs={{0,8},{1,9},{2,10},{3,11},{4,12},{5,13},{6,14},{7,15},{8,0},{9,1},... | collective-permute-start | bytes 442376 | tf_op jit(solution)/shard_map/ppermute | solution.py:363
  5.1 8.7 %copy-start.3 = (bf16[48,1536]{1,0:T(8,128)(2,1)S(1)}, bf16[48,1536]{1,0:T(8,128)(2,1)}, u32[]{:S(2)}) copy-start(bf16[48,1536]{1,0:T(8,128)(2,1)} %get-tuple-element.15) | copy-start | bytes 442372
  5.1 35.6 %all-to-all-start = ((bf16[8,64,1152]{2,1,0:T(8,128)(2,1)}), bf16[8,64,1152]{2,1,0:T(8,128)(2,1)S(1)}, u32[]{:S(2)}, u32[]{:S(2)}) async-start(bf16[8,64,1152]{2,1,0:T(8,128)(2,1)} %get-tuple-element.14), calls=%async_computation | async-start | bytes 2359296 | tf_op jit(solution)/shard_map/all_to_all | solution.py:395
  13.9 7.2 %collective-permute-start.1 = (bf16[96,1536]{1,0:T(8,128)(2,1)S(1)}, bf16[96,1536]{1,0:T(8,128)(2,1)S(1)}, u32[]{:S(2)}, u32[]{:S(2)}) collective-permute-start(bf16[96,1536]{1,0:T(8,128)(2,1)S(1)} %pad_maximum_fusion), channel_id=1, source_target_pairs={{0,16},{1,65},{2,18},{3,67},{4,20},{5,69},{6,22},{7,71},{8,24},{9,... | collective-permute-start | bytes 884744 | tf_op jit(solution)/shard_map/ppermute | solution.py:363
  15.3 8.4 %collective-permute-start.2 = (bf16[96,1536]{1,0:T(8,128)(2,1)S(1)}, bf16[96,1536]{1,0:T(8,128)(2,1)S(1)}, u32[]{:S(2)}, u32[]{:S(2)}) collective-permute-start(bf16[96,1536]{1,0:T(8,128)(2,1)S(1)} %pad_maximum_fusion), channel_id=1, source_target_pairs={{0,48},{1,193},{2,50},{3,195},{4,52},{5,197},{6,54},{7,199},{8,56}... | collective-permute-start | bytes 884744 | tf_op jit(solution)/shard_map/ppermute | solution.py:363
  16.8 8.7 %collective-permute-start.3 = (bf16[96,1536]{1,0:T(8,128)(2,1)S(1)}, bf16[96,1536]{1,0:T(8,128)(2,1)S(1)}, u32[]{:S(2)}, u32[]{:S(2)}) collective-permute-start(bf16[96,1536]{1,0:T(8,128)(2,1)S(1)} %pad_maximum_fusion), channel_id=1, source_target_pairs={{0,32},{1,129},{2,34},{3,131},{4,36},{5,133},{6,38},{7,135},{8,40}... | collective-permute-start | bytes 884744 | tf_op jit(solution)/shard_map/ppermute | solution.py:363
  21.1 19.6 %copy-start.1 = (s32[1,1024]{1,0:T(1,128)S(1)}, s32[1,1024]{1,0:T(1,128)}, u32[]{:S(2)}) copy-start(s32[1,1024]{1,0:T(1,128)} %seg_ref.1) | copy-start | bytes 12292
  21.1 19.6 %copy-start.2 = (f32[24]{0:T(128)S(1)}, f32[24]{0:T(128)}, u32[]{:S(2)}) copy-start(f32[24]{0:T(128)} %rate_ref.1) | copy-start | bytes 292
  25.5 37.1 %collective-permute-start.6 = (bf16[384,1536]{1,0:T(8,128)(2,1)S(1)}, bf16[384,1536]{1,0:T(8,128)(2,1)S(1)}, u32[]{:S(2)}, u32[]{:S(2)}) collective-permute-start(bf16[384,1536]{1,0:T(8,128)(2,1)S(1)} %constant_dynamic-update-slice_fusion.rest_0_), channel_id=1, source_target_pairs={{0,128},{1,33},{2,130},{3,35},{4,132},{5,37},{6,134},{7,39},{8,136... | collective-permute-start | bytes 3538952 | tf_op jit(solution)/shard_map/ppermute | solution.py:363
  28.3 34.3 %collective-permute-start.5 = (bf16[384,1536]{1,0:T(8,128)(2,1)S(1)}, bf16[384,1536]{1,0:T(8,128)(2,1)}, u32[]{:S(2)}, u32[]{:S(2)}) collective-permute-start(bf16[384,1536]{1,0:T(8,128)(2,1)S(1)} %constant_dynamic-update-slice_fusion.rest_0_), channel_id=1, source_target_pairs={{0,192},{1,49},{2,194},{3,51},{4,196},{5,53},{6,198},{7,55},{8,200... | collective-permute-start | bytes 3538952 | tf_op jit(solution)/shard_map/ppermute | solution.py:363
  29.2 33.5 %collective-permute-start.4 = (bf16[384,1536]{1,0:T(8,128)(2,1)S(1)}, bf16[384,1536]{1,0:T(8,128)(2,1)}, u32[]{:S(2)}, u32[]{:S(2)}) collective-permute-start(bf16[384,1536]{1,0:T(8,128)(2,1)S(1)} %constant_dynamic-update-slice_fusion.rest_0_), channel_id=1, source_target_pairs={{0,64},{1,17},{2,66},{3,19},{4,68},{5,21},{6,70},{7,23},{8,72},{9,... | collective-permute-start | bytes 3538952 | tf_op jit(solution)/shard_map/ppermute | solution.py:363
  40.7 0.9 %copy-start = (bf16[2,3,64,256]{3,2,1,0:T(8,128)(2,1)S(1)}, bf16[2,3,64,256]{3,2,1,0:T(8,128)(2,1)}, u32[]{:S(2)}) copy-start(bf16[2,3,64,256]{3,2,1,0:T(8,128)(2,1)} %pad_maximum_fusion.1.weights) | copy-start | bytes 589828
  62.6 22.3 %collective-permute-start.7 = (bf16[384,1536]{1,0:T(8,128)(2,1)S(1)}, bf16[384,1536]{1,0:T(8,128)(2,1)S(1)}, u32[]{:S(2)}, u32[]{:S(2)}) collective-permute-start(bf16[384,1536]{1,0:T(8,128)(2,1)S(1)} %constant_dynamic-update-slice_fusion.rest_0_), channel_id=1, source_target_pairs={{0,1},{1,0},{2,3},{3,2},{4,5},{5,4},{6,7},{7,6},{8,9},{9,8},{10,11... | collective-permute-start | bytes 3538952 | tf_op jit(solution)/shard_map/ppermute | solution.py:363
  67.8 17.1 %collective-permute-start.8 = (bf16[384,1536]{1,0:T(8,128)(2,1)}, bf16[384,1536]{1,0:T(8,128)(2,1)S(1)}, u32[]{:S(2)}, u32[]{:S(2)}) collective-permute-start(bf16[384,1536]{1,0:T(8,128)(2,1)} %collective-permute-done.4.rest_1_), channel_id=1, source_target_pairs={{0,1},{1,0},{2,3},{3,2},{4,5},{5,4},{6,7},{7,6},{8,9},{9,8},{10,11... | collective-permute-start | bytes 3538952 | tf_op jit(solution)/shard_map/ppermute | solution.py:363
  67.9 17.0 %collective-permute-start.9 = (bf16[384,1536]{1,0:T(8,128)(2,1)}, bf16[384,1536]{1,0:T(8,128)(2,1)S(1)}, u32[]{:S(2)}, u32[]{:S(2)}) collective-permute-start(bf16[384,1536]{1,0:T(8,128)(2,1)} %collective-permute-done.5.rest_2_), channel_id=1, source_target_pairs={{0,1},{1,0},{2,3},{3,2},{4,5},{5,4},{6,7},{7,6},{8,9},{9,8},{10,11... | collective-permute-start | bytes 3538952 | tf_op jit(solution)/shard_map/ppermute | solution.py:363
  68.4 16.6 %collective-permute-start.10 = (bf16[384,1536]{1,0:T(8,128)(2,1)S(1)}, bf16[384,1536]{1,0:T(8,128)(2,1)S(1)}, u32[]{:S(2)}, u32[]{:S(2)}) collective-permute-start(bf16[384,1536]{1,0:T(8,128)(2,1)S(1)} %collective-permute-done.6.rest_3_), channel_id=1, source_target_pairs={{0,1},{1,0},{2,3},{3,2},{4,5},{5,4},{6,7},{7,6},{8,9},{9,8},{10,11... | collective-permute-start | bytes 3538952 | tf_op jit(solution)/shard_map/ppermute | solution.py:363
